TPU v7x, 32 devices: a whole 2x2x4 slice. The times are simulated.
32 devices in a mesh: pts: 4 (over x, core), coord: 8 (over z, y).
Axes of the slice: x: 2, y: 2, z: 4, core: 2. Of those that a mesh axis runs over, the one named last changes fastest.
Arguments:
- point_seed: int32 [256], P('pts'), may hold values from 0 to 16777215
- pert_seed: int32 [256, 16], P('pts'), may hold values from 0 to 16777215
- source_coef: float32 [100000], P('coord'), may hold values from -9 to 9
- w1: bfloat16 [1024, 100000], P(None, 'coord'), may hold values from -0.009765625 to 0.009765625
- b1: float32 [1024], replicated, may hold values from -3 to 3
- w2: bfloat16 [1024, 1024], replicated, may hold values from -0.1875 to 0.1875
- w3: bfloat16 [1024], replicated, may hold values from -0.1875 to 0.1875
Outputs:
- residual: float32 [256], P(('pts', 'coord'))
- grad_w1: bfloat16 [1024, 100000], P('pts', 'coord')
- grad_w2: float32 [1024, 1024], P('coord')
- grad_b1: float32 [1024], P('coord')
- grad_w3: float32 [1024], P('coord')
All inputs are finite; a program needn't handle non-finite values.
Results may differ from a plain program's by a relative error of at most 0.023.
Values may be sent and summed in bfloat16 or wider, within the bound.
No kernel may reach another device: no remote copies, remote signals or barrier semaphores. Data moves between devices by JAX's collectives and lax.ppermute only.
A program may use at most 128 MiB of HBM per device.

v0:
```python
import math

import jax
import jax.numpy as jnp
from jax import lax
from jax.sharding import PartitionSpec as P

D = 100000


hash_factor = 73244475
NOISE_SCALE = 2.0
READOUT = 0.0625


def shuffle_bits(packed_bits):
    return packed_bits ^ lax.shift_right_logical(packed_bits, jnp.full_like(packed_bits, 16))


def mix_bits(packed_bits):
    packed_bits = shuffle_bits(packed_bits)
    packed_bits = shuffle_bits(packed_bits * hash_factor)
    return shuffle_bits(packed_bits * hash_factor)


def to_unit(packed_bits):
    return ((packed_bits & 8388607).astype(jnp.float32) + 0.5) * (1.0 / 8388608.0)


def column_keys(columns):
    return (mix_bits(columns * 4), mix_bits(columns * 4 + 1), mix_bits(columns * 4 + 2))


def perturbed_rows(point_seeds, pert_seeds, column_hash, coef_part):
    key_zero, key_one, key_two = column_hash
    count_points, count_samples = pert_seeds.shape
    uniform_point = to_unit(mix_bits(key_two[None, :] ^ point_seeds[:, None]))
    coords = 2.0 * uniform_point - 1.0
    uniform_zero = to_unit(mix_bits(key_zero[None, None, :] ^ pert_seeds[:, :, None]))
    uniform_one = to_unit(mix_bits(key_one[None, None, :] ^ pert_seeds[:, :, None]))
    noise_draw = jnp.sqrt(-2.0 * jnp.log(uniform_zero)) * jnp.cos(2.0 * jnp.pi * uniform_one)
    shifted = (coords[:, None, :] + NOISE_SCALE * noise_draw).astype(jnp.bfloat16)
    shifted = shifted.reshape(count_points * count_samples, coords.shape[1])
    squares = jnp.sum(noise_draw * noise_draw, axis=2).reshape(count_points * count_samples)
    source = jnp.sum(coef_part[None, :] * jnp.sin(jnp.pi * coords), axis=1) / math.sqrt(D)
    return (shifted, squares, source)


def hidden_pass(pre_first, squares, source, w2, w3, count_samples):
    hidden_one = jnp.tanh(pre_first).astype(jnp.bfloat16)
    pre_second = lax.dot_general(
        hidden_one, w2, (((1,), (1,)), ((), ())), preferred_element_type=jnp.float32
    )
    hidden_two = jnp.tanh(pre_second).astype(jnp.bfloat16)
    values_out = READOUT * jnp.dot(hidden_two, w3, preferred_element_type=jnp.float32)
    stein_weight = (squares - D) / (NOISE_SCALE * NOISE_SCALE * count_samples)
    per_point = (stein_weight * values_out).reshape(-1, count_samples)
    residual = jnp.sum(per_point, axis=1) - source
    grad_values = (residual[:, None] * stein_weight.reshape(-1, count_samples)).reshape(-1)
    two_float = hidden_two.astype(jnp.float32)
    grad_readout = READOUT * jnp.sum(grad_values[:, None] * two_float, axis=0)
    grad_pre_two = (
        READOUT
        * grad_values[:, None]
        * w3.astype(jnp.float32)[None, :]
        * (1.0 - two_float * two_float)
    ).astype(jnp.bfloat16)
    grad_second = lax.dot_general(
        grad_pre_two, hidden_one, (((0,), (0,)), ((), ())), preferred_element_type=jnp.float32
    )
    grad_hidden = jnp.dot(grad_pre_two, w2, preferred_element_type=jnp.float32)
    one_float = hidden_one.astype(jnp.float32)
    grad_pre_one = (grad_hidden * (1.0 - one_float * one_float)).astype(jnp.bfloat16)
    grad_bias = jnp.sum(grad_pre_one.astype(jnp.float32), axis=0)
    return (residual, grad_pre_one, grad_second, grad_bias, grad_readout, hidden_one, grad_pre_two)


def shards(point_seed, pert_seed, source_coef, w1, b1, w2, w3):
    coord_count = lax.axis_size("coord")
    coord_width = w1.shape[1]
    points_here, samples = pert_seed.shape
    rows_here = points_here * samples
    rows_local = rows_here // coord_count
    points_local = points_here // coord_count
    coord_index = lax.axis_index("coord")
    columns = coord_index * coord_width + jnp.arange(coord_width, dtype=jnp.int32)
    column_hash = column_keys(columns)
    shifted, squares, source = perturbed_rows(point_seed, pert_seed, column_hash, source_coef)
    picked = shifted
    pre_local = lax.psum_scatter(
        lax.dot_general(picked, w1, (((1,), (1,)), ((), ())), preferred_element_type=jnp.float32),
        "coord",
        scatter_dimension=0,
        tiled=True,
    )
    squares_all, source_all = lax.psum((squares, source), "coord")
    squares_local = lax.dynamic_slice_in_dim(squares_all, coord_index * rows_local, rows_local, 0)
    source_local = lax.dynamic_slice_in_dim(source_all, coord_index * points_local, points_local, 0)
    residual, grad_pre_one, grad_second, grad_bias, grad_readout, hidden_one, grad_pre_two = (
        hidden_pass(pre_local + b1[None, :], squares_local, source_local, w2, w3, samples)
    )
    grad_rows = lax.all_gather(grad_pre_one, "coord", axis=0, tiled=True)
    picked = grad_rows
    grad_first = lax.psum_scatter(
        lax.dot_general(
            picked, shifted, (((0,), (0,)), ((), ())), preferred_element_type=jnp.float32
        ).astype(jnp.bfloat16),
        "pts",
        scatter_dimension=0,
        tiled=True,
    )
    share_second, share_bias, share_readout = (
        lax.psum_scatter(
            grad_second.astype(jnp.bfloat16), "coord", scatter_dimension=0, tiled=True
        ).astype(jnp.float32),
        lax.psum_scatter(
            grad_bias.astype(jnp.bfloat16), "coord", scatter_dimension=0, tiled=True
        ).astype(jnp.float32),
        lax.psum_scatter(
            grad_readout.astype(jnp.bfloat16), "coord", scatter_dimension=0, tiled=True
        ).astype(jnp.float32),
    )
    out_second, out_bias, out_readout = (
        lax.psum(share_second.astype(jnp.bfloat16), "pts").astype(jnp.float32),
        lax.psum(share_bias.astype(jnp.bfloat16), "pts").astype(jnp.float32),
        lax.psum(share_readout.astype(jnp.bfloat16), "pts").astype(jnp.float32),
    )
    return (residual, grad_first, out_second, out_bias, out_readout)


def solution(mesh):
    return jax.shard_map(
        shards,
        mesh=mesh,
        in_specs=(P("pts"), P("pts", None), P("coord"), P(None, "coord"), P(), P(), P()),
        out_specs=(
            P(("pts", "coord")),
            P("pts", "coord"),
            P("coord", None),
            P("coord"),
            P("coord"),
        ),
        check_vma=False,
    )
```

profile of v0, /device:TPU:0, one launch (start us, length us, event | category | flops | bytes accessed | tf_op | source)
XLA Modules:
  0.0 897.4 jit_solution(8827649979673939731)
XLA Ops:
  7.2 0.0 copy-start
  7.2 0.0 reduce-scatter.4.cloned.1.call-start
  7.3 0.9 copy.17
  8.2 0.1 xor.202
  8.3 13.2 %multiply_reduce_fusion = (f32[64]{0:T(128)S(1)}, f32[64,12500]{1,0:T(8,128)S(1)}) fusion(f32[12500]{0:T(1024)} %param.9, s32[64]{0:T(128)} %param.7, s32[12500]{0:T(1024)S(1)} %get-tuple-element.17), kind=kLoop, calls=%fused_computation.62 | loop fusion | flops 13599936 | bytes 3300512 | tf_op jit(solution)/shard_map/reduce_sum | solution.py:45
  21.5 241.7 %fusion.37 = bf16[1024,12500]{1,0:T(8,128)(2,1)} fusion(s32[12500]{0:T(1024)S(1)} %get-tuple-element.18, s32[1024]{0:T(1024)S(1)} %xor.202, s32[12500]{0:T(1024)S(1)} %shift-right-logical_xor_fusion.21, f32[64,12500]{1,0:T(8,128)S(1)} %get-tuple-element.14), kind=kLoop, calls=%fused_computation.49 | loop fusion | flops 396800000 | bytes 28904096 | tf_op jit(solution)/shard_map/convert_element_type | solution.py:42
  263.2 0.0 copy-start.1
  263.2 34.1 %fusion.67 = f32[1024,1024]{1,0:T(8,128)} fusion(bf16[1024,12500]{1,0:T(8,128)(2,1)} %fusion.37, bf16[1024,12500]{0,1:T(8,128)(2,1)} %param.10), kind=kOutput, calls=%fused_computation.103 | convolution fusion | flops 26214400000 | bytes 55394304 | tf_op jit(solution)/shard_map/dot_general | solution.py:91
  297.4 0.0 reduce-scatter.4.cloned.1.call-update
  297.4 0.0 reduce-scatter.8.cloned.1.call-start
  297.4 0.0 copy-done.1
  297.5 0.0 copy-start.2
  297.5 228.7 %fusion.38 = f32[64,16]{1,0:T(8,128)S(1)} fusion(s32[12500]{0:T(1024)S(1)} %get-tuple-element.18, s32[64,16]{1,0:T(8,128)S(1)} %copy.17, s32[12500]{0:T(1024)S(1)} %shift-right-logical_xor_fusion.21), kind=kLoop, calls=%fused_computation.50 | loop fusion | flops 383998976 | bytes 108192 | tf_op jit(solution)/shard_map/reduce_sum | solution.py:44
  526.2 0.1 reshape.111
  526.3 23.4 %all-reduce.2 = (f32[1024]{0:T(1024)S(1)}, f32[64]{0:T(128)S(1)}) all-reduce(f32[1024]{0:T(1024)S(1)} %reshape.111, f32[64]{0:T(128)S(1)} %broadcast_multiply_fusion), channel_id=1, replica_groups=mesh['pts'=4,'coord'=8] {'coord'}, use_global_device_ids=true, to_apply=%region_1.0 | all-reduce | flops 1088 | bytes 8704 | tf_op jit(solution)/shard_map/psum | solution.py:96
  549.6 0.0 reduce-scatter.4.cloned.1.call-done
  549.7 0.0 copy-done.2
  549.7 1.1 tanh_convert_fusion
  550.8 0.0 copy-done
  550.8 0.8 fusion.46
  551.6 0.2 fusion.49
  551.8 0.1 reshape.112
  551.9 0.1 reduce_sum.49
  552.0 0.1 dynamic-slice_subtract_fusion
  552.1 0.0 copy-start.3
  552.1 0.1 mul.286
  552.2 0.1 mul.287
  552.3 0.1 broadcast_multiply_fusion.1
  552.4 2.1 convolution_convert_fusion.1
  554.5 0.0 reduce-scatter.8.cloned.1.call-update
  554.5 0.0 all-gather.2.cloned.1.call-start
  554.6 1.2 fusion.66
  555.8 0.0 all-gather.2.cloned.1.call-update
  555.8 0.0 all-reduce.7.cloned.1.call-start
  555.9 63.7 %reduce-scatter.8.cloned.1.call-done = bf16[128,1024]{1,0:T(8,128)(2,1)} async-done(((bf16[1024,1024]{1,0:T(8,128)(2,1)}), bf16[128,1024]{1,0:T(8,128)(2,1)}) %reduce-scatter.8.cloned.1.call-update) | async-done | bytes 262160 | tf_op jit(solution)/shard_map/reduce_scatter | solution.py:113
  619.6 0.0 all-reduce.7.cloned.1.call-update
  619.6 0.0 copy-start.4
  619.6 0.0 reduce-scatter.6.cloned.1.call-start
  619.7 51.2 %all-gather.2.cloned.1.call-done = bf16[1024,1024]{1,0:T(8,128)(2,1)} async-done(((bf16[128,1024]{1,0:T(8,128)(2,1)}), bf16[1024,1024]{1,0:T(8,128)(2,1)}) %all-gather.2.cloned.1.call-update) | async-done | bytes 2097168 | tf_op jit(solution)/shard_map/all_gather | solution.py:102
  670.9 34.0 %convolution_convert_fusion = bf16[1024,12500]{0,1:T(8,128)(2,1)} fusion(bf16[1024,1024]{1,0:T(8,128)(2,1)} %all-gather.2.cloned.1.call-done, bf16[1024,12500]{1,0:T(8,128)(2,1)} %fusion.37), kind=kOutput, calls=%fused_computation.51 | convolution fusion | flops 26227200000 | bytes 53297152 | tf_op jit(solution)/shard_map/dot_general | solution.py:105
  704.9 0.0 copy-done.3
  704.9 0.0 reduce-scatter.6.cloned.1.call-update
  704.9 0.0 copy-done.4
  704.9 0.6 dynamic-slice
  706.2 0.1 fusion.53
  706.3 18.9 %all-reduce.3 = (bf16[1024]{0:T(1024)(128)(2,1)S(1)}, bf16[1024]{0:T(1024)(128)(2,1)S(1)}) all-reduce(bf16[1024]{0:T(1024)(128)(2,1)S(1)} %get-tuple-element.15, bf16[1024]{0:T(1024)(128)(2,1)S(1)} %multiply_convert_fusion), channel_id=5, replica_groups=mesh['pts'=4,'coord'=8] {'coord'}, use_global_device_ids=true, to_apply=%region_10.0.clone | all-reduce | flops 2048 | bytes 8192
  725.2 0.1 dynamic-slice.1
  725.3 0.1 dynamic-slice.3
  725.4 5.6 all-reduce.4
  731.0 0.5 convert_element_type.86
  731.6 0.5 convert_element_type.88
  732.1 0.0 all-reduce.7.cloned.1.call-done
  732.1 1.8 convert_element_type.85
  733.9 156.6 %reduce-scatter.6.cloned.1.call-done = bf16[256,12500]{0,1:T(8,128)(2,1)} async-done(((bf16[1024,12500]{0,1:T(8,128)(2,1)}), bf16[256,12500]{0,1:T(8,128)(2,1)}) %reduce-scatter.6.cloned.1.call-update) | async-done | bytes 6400016 | tf_op jit(solution)/shard_map/reduce_scatter | solution.py:104
  (6 shorter events, 0.1 us)
Async XLA Ops:
  7.2 543.6 %copy-start = (bf16[1024,1024]{1,0:T(8,128)(2,1)S(1)}, bf16[1024,1024]{1,0:T(8,128)(2,1)}, u32[]{:S(2)}) copy-start(bf16[1024,1024]{1,0:T(8,128)(2,1)} %param.12) | copy-start | bytes 6291460
  7.2 542.5 %reduce-scatter.4.cloned.1.call-start = ((), (), s32[]{:S(2)}) async-start(), calls=%async_computation.3 | async-start | bytes 4718592 | tf_op jit(solution)/shard_map/reduce_scatter | solution.py:90
  263.2 34.2 %copy-start.1 = (bf16[1024]{0:T(1024)(128)(2,1)S(1)}, bf16[1024]{0:T(1024)(128)(2,1)}, u32[]{:S(2)}) copy-start(bf16[1024]{0:T(1024)(128)(2,1)} %param.13) | copy-start | bytes 6148
  297.4 322.2 %reduce-scatter.8.cloned.1.call-start = ((), (), s32[]{:S(2)}) async-start(), calls=%async_computation.6 | async-start | bytes 2359296 | tf_op jit(solution)/shard_map/reduce_scatter | solution.py:113
  297.5 252.2 %copy-start.2 = (f32[1024]{0:T(1024)S(1)}, f32[1024]{0:T(1024)}, u32[]{:S(2)}) copy-start(f32[1024]{0:T(1024)} %param.11) | copy-start | bytes 12292
  552.1 152.8 %copy-start.3 = (f32[8]{0:T(128)}, f32[8]{0:T(128)S(1)}, u32[]{:S(2)}) copy-start(f32[8]{0:T(128)S(1)} %dynamic-slice_subtract_fusion) | copy-start | bytes 100
  554.5 116.3 %all-gather.2.cloned.1.call-start = ((), (), s32[]{:S(2)}) async-start(), calls=%async_computation.4 | async-start | bytes 2359296 | tf_op jit(solution)/shard_map/all_gather | solution.py:102
  555.8 176.2 %all-reduce.7.cloned.1.call-start = ((), (), s32[]{:S(2)}) async-start(), calls=%async_computation.7 | async-start | bytes 524288 | tf_op jit(solution)/shard_map/psum | solution.py:124
  619.6 85.3 %copy-start.4 = (u32[32]{0:T(128)S(1)}, u32[32]{0:T(128)}, u32[]{:S(2)}) copy-start(u32[32]{0:T(128)} %constant.77) | copy-start | bytes 388
  619.6 270.9 %reduce-scatter.6.cloned.1.call-start = ((), (), s32[]{:S(2)}) async-start(), calls=%async_computation.5 | async-start | bytes 32010240 | tf_op jit(solution)/shard_map/reduce_scatter | solution.py:104
Sparse Core Ops, SparseCore 0:
  297.5 90.7 reduce-scatter.3
  554.6 64.8 reduce-scatter.7
  622.5 48.2 all-gather.1
  673.1 30.4 all-reduce.6
  706.7 183.7 reduce-scatter.5
where the time goes:
time: 907 us; the launch traced here: 897 us
  other arithmetic  488 us (54%)
  waiting for transfers between devices  272 us (30%)
  matrix products  72.6 us (8%)
  blocking collectives  47.9 us (5%)
  between operations  15 us (2%)
    convert_element_type x1, other arithmetic, perturbed_rows(): (coords[:, None, :] + NOISE_SCALE * noise_draw).astype(jnp.bfloat16)  242 us
    reduce_sum x1, other arithmetic, perturbed_rows(): jnp.sum(noise_draw * noise_draw, axis=2)  229 us
    reduce_scatter x1, waiting for transfers between devices, shards(): lax.psum_scatter(lax.dot_general(picked, shifted, (((0,), (0,)), ((), ())...  157 us
    reduce_scatter x1, waiting for transfers between devices, shards(): lax.psum_scatter(grad_second.astype(jnp.bfloat16), 'coord', scatter_dimen...  63.7 us
    all_gather x1, waiting for transfers between devices, shards(): grad_rows = lax.all_gather(grad_pre_one, 'coord', axis=0, tiled=True)  51.2 us
    dot_general x1, matrix products, shards(): lax.dot_general(picked, w1, (((1,), (1,)), ((), ())), preferred_element_t...  34.1 us
    dot_general x1, matrix products, shards(): lax.dot_general(picked, shifted, (((0,), (0,)), ((), ())), preferred_elem...  34 us
    psum x1, blocking collectives, shards(): squares_all, source_all = lax.psum((squares, source), 'coord')  23.4 us
  transfers between devices with their start and end apart: 5, of which 3 were waited for; matrix products, arithmetic and copies ran while one was open for 30% of the time, Pallas kernels for 0%

commit v1 on v0

v1 whole, which is shorter than its diff:
```python
import functools
import math

import jax
import jax.numpy as jnp
import numpy as np
from jax import lax
from jax.experimental import pallas as pl
from jax.experimental.pallas import tpu as pltpu
from jax.sharding import PartitionSpec as P

D = 100000

HASH_FACTOR = 73244475
NOISE_SCALE = 2.0
READOUT = 0.0625
LANES = 128
GROUP = 256
MASK = 8388607
VMEM_BYTES = 56 * 1024 * 1024

C0, C1, C2, C3 = 6.283164044286755, -2.583571398038591, 0.3177373780982648, -0.017332380925367475
B0, B1, B2 = C0 / C3, C1 / C3, C2 / C3
SINE_SCALE = -C3 * 2.0**-23
LOG_SCALE = -2.0 * math.log(2.0) * (NOISE_SCALE * SINE_SCALE) ** 2


def shuffle_bits(bits):
    return bits ^ lax.shift_right_logical(bits, jnp.full_like(bits, 16))


def mix_tail(bits):
    bits = shuffle_bits(bits * HASH_FACTOR)
    return shuffle_bits(bits * HASH_FACTOR)


def mix_bits(bits):
    return mix_tail(shuffle_bits(bits))


def turn_wave(index):
    y = jnp.abs(index.astype(jnp.float32) + (0.5 - 4194304.0)) - 2097152.0
    s = (y * y) * 2.0**-42
    m = ((s + B2) * s + B1) * s + B0
    return y, -m


def tile_lanes(a, width):
    return jnp.concatenate([a] * (width // a.shape[1]), axis=1)


def column_keys(base, step, width):
    columns = lax.broadcasted_iota(jnp.int32, (8, width), 1) + step * width
    four = (columns + base) * 4
    return columns, [shuffle_bits(mix_bits(four + t)) for t in range(3)]


def draw(seeds, key_zero, key_one):
    width = key_zero.shape[1]
    seeds = tile_lanes(seeds, width)
    first = mix_tail(seeds ^ jnp.concatenate([key_zero] * 2, axis=0))
    second = mix_tail(seeds ^ jnp.concatenate([key_one] * 2, axis=0))
    u0 = ((first & MASK).astype(jnp.float32) + 0.5) * 2.0**-23
    n = jnp.log2(u0) * LOG_SCALE
    y, m = turn_wave(second & MASK)
    return ((n * lax.rsqrt(n)) * y) * m


def pieces(width):
    tiles = width // LANES
    parts = -(-tiles // 4)
    edges = [tiles * i // parts for i in range(parts + 1)]
    return [(a * LANES, b * LANES) for a, b in zip(edges, edges[1:])]


def point_rows(seeds, key, width):
    return mix_tail(tile_lanes(seeds, width) ^ key) & MASK


def coordinate(index):
    return (index.astype(jnp.float32) + (0.5 - 4194304.0)) * 2.0**-22


def forward_kernel(
    valid, base_ref, pert_ref, point_ref, coef_ref, w_prev, w_now,
    z_ref, pre_ref, sq_ref, src_ref, held_a, held_b, acc, keys, xs,
):
    step, last = pl.program_id(0), pl.num_programs(0) - 1
    rows, width = z_ref.shape
    points = point_ref.shape[0]
    samples = rows // points
    groups = rows // GROUP
    steps = -(-valid // width)
    pad = steps * width - valid

    @pl.when(step == 0)
    def _():
        acc[...] = jnp.zeros_like(acc)
        held_b[...] = jnp.zeros_like(held_b)
        sq_ref[...] = jnp.zeros_like(sq_ref)
        src_ref[...] = jnp.zeros_like(src_ref)

    columns, (key_zero, key_one, key_two) = column_keys(base_ref[0], step, width)
    keys[0:8] = key_zero
    keys[8:16] = key_one
    inside = columns < valid
    coef = jnp.where(inside, jnp.broadcast_to(coef_ref[...], (8, width)), 0.0)
    for at in range(0, points, 8):
        index = point_rows(point_ref[at:at + 8], key_two, width)
        xs[at:at + 8] = coordinate(index)
        y, m = turn_wave((index + 2097152) & MASK)
        term = ((y * SINE_SCALE) * m) * coef
        src_ref[at:at + 8] += sum(
            term[:, a:a + LANES] for a in range(0, width, LANES)
        )

    def weights(ref, of):
        cut = width - -(-pad // 16) * 16
        if cut == width:
            return ref[...]
        place = lax.broadcasted_iota(jnp.int32, (width - cut, ref.shape[1]), 0) + (of * width + cut)
        tail = jnp.where(place < valid, ref[cut:, :], jnp.zeros((), ref.dtype))
        return jnp.concatenate([ref[:cut, :], tail], axis=0)

    def multiply(group, held, ref, of):
        at = group * GROUP
        acc[at:at + GROUP, :] += jnp.dot(
            held[...], weights(ref, of), preferred_element_type=jnp.float32
        )

    for group in range(groups):
        held = (held_a, held_b)[group % 2]
        for at in range(0, GROUP, samples):
            row = group * GROUP + at
            point = row // samples
            seeds = pert_ref[row:row + samples]
            total = None
            for a, b in pieces(width):
                noise = draw(seeds, keys[0:8, a:b], keys[8:16, a:b])
                x = jnp.broadcast_to(xs[point:point + 1, a:b], (samples, b - a))
                z = (x + noise).astype(jnp.bfloat16)
                held[at:at + samples, a:b] = z
                z_ref[row:row + samples, a:b] = z
                square = noise * noise
                for c in range(a, b, LANES):
                    part = square[:, c - a:c - a + LANES]
                    if (steps - 1) * width + c + LANES > valid:
                        part = jnp.where(jnp.concatenate([inside[:, c:c + LANES]] * 2, axis=0), part, 0.0)
                    total = part if total is None else total + part
            sq_ref[row:row + samples] += total
        if group == 0:
            multiply(groups - 1, held_b, w_prev, jnp.maximum(step - 1, 0))
        else:
            multiply(group - 1, (held_b, held_a)[group % 2], w_now, step)

    @pl.when(step == last)
    def _():
        multiply(groups - 1, held_b, w_now, step)
        pre_ref[...] = acc[...].astype(pre_ref.dtype)


def redraw_kernel(first, base_ref, pert_ref, point_ref, z_ref, keys, xs):
    step = pl.program_id(0) + first
    rows, width = z_ref.shape
    points = point_ref.shape[0]
    samples = rows // points
    _, (key_zero, key_one, key_two) = column_keys(base_ref[0], step, width)
    keys[0:8] = key_zero
    keys[8:16] = key_one
    for at in range(0, points, 8):
        xs[at:at + 8] = coordinate(point_rows(point_ref[at:at + 8], key_two, width))

    @pl.loop(0, points // 8)
    def _(block):
        eight = xs[pl.ds(pl.multiple_of(block * 8, 8), 8)]
        for inner in range(8):
            row = pl.multiple_of((block * 8 + inner) * samples, samples)
            seeds = pert_ref[pl.ds(row, samples)]
            for a, b in pieces(width):
                noise = draw(seeds, keys[0:8, a:b], keys[8:16, a:b])
                x = jnp.broadcast_to(eight[inner:inner + 1, a:b], (samples, b - a))
                z_ref[pl.ds(row, samples), a:b] = (x + noise).astype(jnp.bfloat16)


def gradient_kernel(count, d_ref, *refs):
    z_refs, (keep_ref, send_ref) = refs[:count], refs[count:]
    blocks, _, hidden, _ = d_ref.shape
    half = hidden // 2
    left = jnp.concatenate(
        [d_ref[block, source] for source in range(count) for block in range(blocks)], axis=1
    )
    width = keep_ref.shape[0]
    stride = 256 if width % 256 == 0 else LANES
    for a in range(0, width, stride):
        z = jnp.concatenate([ref[:, a:a + stride] for ref in z_refs], axis=0)
        part = jnp.dot(left, z, preferred_element_type=jnp.float32).astype(jnp.bfloat16).T
        keep_ref[a:a + stride, :] = part[:, :half]
        send_ref[a:a + stride, :] = part[:, half:]


def join_kernel(*refs):
    keep_ref, got_ref, out_ref = refs[0], refs[1], refs[-1]
    out_ref[...] = (keep_ref[...].astype(jnp.float32) + got_ref[...].astype(jnp.float32)).astype(jnp.bfloat16)


def params():
    return pltpu.CompilerParams(dimension_semantics=("arbitrary",), vmem_limit_bytes=VMEM_BYTES)


def whole(shape):
    return pl.BlockSpec(shape, lambda s: (0,) * len(shape))


def lanes_of(seeds):
    return jnp.broadcast_to(shuffle_bits(seeds.reshape(-1))[:, None], (seeds.size, LANES))


def forward(base, pert, point, coef, w, width):
    valid, hidden = w.shape
    rows, points = pert.shape[0], point.shape[0]
    steps = -(-valid // width)
    smem = pl.BlockSpec(memory_space=pltpu.SMEM)
    return pl.pallas_call(
        functools.partial(forward_kernel, valid),
        grid=(steps,),
        in_specs=[
            smem, whole(pert.shape), whole(point.shape),
            pl.BlockSpec((1, width), lambda s: (0, s)),
            pl.BlockSpec((width, hidden), lambda s: (jnp.maximum(s - 1, 0), 0)),
            pl.BlockSpec((width, hidden), lambda s: (s, 0)),
        ],
        out_specs=[
            pl.BlockSpec((rows, width), lambda s: (0, s)),
            whole((rows, hidden)), whole((rows, LANES)), whole((points, LANES)),
        ],
        out_shape=[
            jax.ShapeDtypeStruct((rows, steps * width), jnp.bfloat16),
            jax.ShapeDtypeStruct((rows, hidden), jnp.bfloat16),
            jax.ShapeDtypeStruct((rows, LANES), jnp.float32),
            jax.ShapeDtypeStruct((points, LANES), jnp.float32),
        ],
        scratch_shapes=[
            pltpu.VMEM((GROUP, width), jnp.bfloat16),
            pltpu.VMEM((GROUP, width), jnp.bfloat16),
            pltpu.VMEM((rows, hidden), jnp.float32),
            pltpu.VMEM((16, width), jnp.int32),
            pltpu.VMEM((points, width), jnp.float32),
        ],
        compiler_params=params(),
        cost_estimate=pl.CostEstimate(
            flops=100 * rows * valid * 40, bytes_accessed=4 * rows * valid, transcendentals=2 * rows * valid
        ),
        name="forward",
    )(base, pert, point, coef, w, w)


def redraw(base, pert, point, width, first, count):
    rows, points = pert.shape[0], point.shape[0]
    return pl.pallas_call(
        functools.partial(redraw_kernel, first),
        grid=(count,),
        in_specs=[pl.BlockSpec(memory_space=pltpu.SMEM), whole(pert.shape), whole(point.shape)],
        out_specs=pl.BlockSpec((rows, width), lambda s: (0, s)),
        out_shape=jax.ShapeDtypeStruct((rows, count * width), jnp.bfloat16),
        scratch_shapes=[pltpu.VMEM((16, width), jnp.int32), pltpu.VMEM((points, width), jnp.float32)],
        compiler_params=params(),
        cost_estimate=pl.CostEstimate(
            flops=100 * rows * width * count * 40, bytes_accessed=2 * rows * width * count,
            transcendentals=2 * rows * width * count,
        ),
        name="redraw",
    )(base, pert, point)


def gradient(cotangent, own, others, width, first, count, valid):
    if count % 2 == 0 and first % 2 == 0:
        width, first, count = 2 * width, first // 2, count // 2
    rows = own.shape[0]
    half = cotangent.shape[2] // 2
    height = min(valid, (first + count) * width) - first * width
    return pl.pallas_call(
        functools.partial(gradient_kernel, 1 + len(others)),
        grid=(count,),
        in_specs=[whole(cotangent.shape), pl.BlockSpec((rows, width), lambda s: (0, s + first))]
        + [pl.BlockSpec((rows, width), lambda s: (0, s)) for _ in others],
        out_specs=[pl.BlockSpec((width, half), lambda s: (s, 0))] * 2,
        out_shape=[jax.ShapeDtypeStruct((height, half), jnp.bfloat16)] * 2,
        compiler_params=params(),
        cost_estimate=pl.CostEstimate(
            flops=4 * half * rows * (1 + len(others)) * width * count,
            bytes_accessed=2 * rows * (1 + len(others)) * width * count, transcendentals=0,
        ),
        name="gradient",
    )(cotangent, own, *others)


def join(keep, got, before, width, first, valid):
    height, half = keep.shape
    count = -(-height // width)
    specs = [pl.BlockSpec((width, half), lambda s: (s, 0))] * 2
    operands, aliases = [keep, got], {}
    if before is not None:
        specs, operands, aliases = specs + [pl.BlockSpec(memory_space=pl.ANY)], operands + [before], {2: 0}
    return pl.pallas_call(
        join_kernel,
        grid=(count,),
        in_specs=specs,
        out_specs=pl.BlockSpec((width, half), lambda s: (s + first, 0)),
        out_shape=jax.ShapeDtypeStruct((valid, half), jnp.bfloat16),
        input_output_aliases=aliases,
        compiler_params=params(),
        cost_estimate=pl.CostEstimate(flops=height * half, bytes_accessed=6 * height * half, transcendentals=0),
        name="join",
    )(*operands)


def hidden_pass(pre_first, squares, source, w2, w3, count_samples):
    hidden_one = jnp.tanh(pre_first).astype(jnp.bfloat16)
    pre_second = lax.dot_general(
        hidden_one, w2, (((1,), (1,)), ((), ())), preferred_element_type=jnp.float32
    )
    hidden_two = jnp.tanh(pre_second).astype(jnp.bfloat16)
    values_out = READOUT * jnp.dot(hidden_two, w3, preferred_element_type=jnp.float32)
    stein_weight = (squares - D) / (NOISE_SCALE * NOISE_SCALE * count_samples)
    per_point = (stein_weight * values_out).reshape(-1, count_samples)
    residual = jnp.sum(per_point, axis=1) - source
    grad_values = (residual[:, None] * stein_weight.reshape(-1, count_samples)).reshape(-1)
    two_float = hidden_two.astype(jnp.float32)
    grad_readout = READOUT * jnp.sum(grad_values[:, None] * two_float, axis=0)
    grad_pre_two = (
        READOUT
        * grad_values[:, None]
        * w3.astype(jnp.float32)[None, :]
        * (1.0 - two_float * two_float)
    ).astype(jnp.bfloat16)
    grad_hidden = jnp.dot(grad_pre_two, w2, preferred_element_type=jnp.float32)
    one_float = hidden_one.astype(jnp.float32)
    grad_pre_one = (grad_hidden * (1.0 - one_float * one_float)).astype(jnp.bfloat16)
    return (residual, grad_pre_one, grad_readout, hidden_one, grad_pre_two)


def block_width(valid):
    tiles = -(-valid // LANES)
    best = min((8, 7, 6, 5), key=lambda t: -(-tiles // t) * t)
    return best * LANES


def tie(first, second):
    return lax.optimization_barrier((first, second))


def shards(point_seed, pert_seed, source_coef, w1, b1, w2, w3):
    coord_count = lax.axis_size("coord")
    pts_count = lax.axis_size("pts")
    chips = pts_count // 2
    hidden, valid = w1.shape
    points_here, samples = pert_seed.shape
    rows_here = points_here * samples
    rows_local = rows_here // coord_count
    points_local = points_here // coord_count
    coord_index = lax.axis_index("coord")
    pts_index = lax.axis_index("pts")
    share = hidden // pts_count
    width = block_width(valid)
    steps = -(-valid // width)
    base = (coord_index * valid).astype(jnp.int32).reshape(1)

    def shift(a, by):
        return jax.tree.map(
            lambda leaf: lax.ppermute(
                leaf, "pts", [(i, (i + 2 * by) % pts_count) for i in range(pts_count)]
            ), a,
        )

    other_seeds = [shift((pert_seed, point_seed), by) for by in range(1, chips)]

    pert, point = lanes_of(pert_seed), lanes_of(point_seed)
    own, pre, squares, source = forward(base, pert, point, source_coef[None, :], w1.T, width)
    other_seeds, pre = tie(other_seeds, pre)
    others_in = [(lanes_of(a), lanes_of(b)) for a, b in other_seeds]

    pre_local = lax.psum_scatter(pre, "coord", scatter_dimension=0, tiled=True)
    sums = jnp.concatenate(
        [jnp.sum(squares, axis=1) / NOISE_SCALE**2, jnp.sum(source, axis=1) / math.sqrt(D)]
    )
    sums = jnp.sum(lax.all_gather(sums, "coord", axis=0), axis=0)
    squares_local = lax.dynamic_slice_in_dim(sums, coord_index * rows_local, rows_local, 0)
    source_local = lax.dynamic_slice_in_dim(sums, rows_here + coord_index * points_local, points_local, 0)

    early = steps // 2 + (steps // 2) % 2
    cuts = [(0, early), (early, steps - early)]
    drawn = [[redraw(base, a, b, width, *cuts[0]) for a, b in others_in]]

    residual, grad_pre_one, grad_readout, hidden_one, grad_pre_two = hidden_pass(
        pre_local.astype(jnp.float32) + b1[None, :], squares_local, source_local, w2, w3, samples
    )
    turned = grad_pre_one.T

    def share_of(index):
        return [lax.dynamic_slice_in_dim(turned, i * share, share, 0) for i in (index, index ^ 1)]

    sent = [jnp.concatenate(share_of((pts_index + 2 * by) % pts_count), axis=0) for by in range(chips)]
    mine = jnp.stack([sent[0]] + [shift(sent[by], by) for by in range(1, chips)])
    others_in, mine = tie(others_in, mine)
    cotangent = lax.all_gather(mine, "coord", axis=0)
    blocks = rows_here // LANES
    if rows_local != LANES:
        cotangent = cotangent.transpose(1, 2, 0, 3).reshape(chips, 2 * share, blocks, LANES)
        cotangent = cotangent.transpose(2, 0, 1, 3)
    drawn.append([redraw(base, a, b, width, *cuts[1]) for a, b in others_in])

    (hidden_one, grad_pre_two), cotangent = tie((hidden_one, grad_pre_two), cotangent)
    grad_second = lax.dot_general(
        grad_pre_two, hidden_one, (((0,), (0,)), ((), ())), preferred_element_type=jnp.float32
    )
    grad_bias = jnp.sum(grad_pre_one.astype(jnp.float32), axis=0)
    small = jnp.concatenate(
        [grad_second, grad_bias[:, None], grad_readout[:, None], jnp.zeros((hidden, LANES - 2), jnp.float32)], axis=1
    ).astype(jnp.bfloat16)
    small = lax.psum_scatter(small, "coord", scatter_dimension=0, tiled=True)
    small = lax.psum(small, "pts").astype(jnp.float32)

    out = None
    swap = [(i, i ^ 1) for i in range(pts_count)]
    for (first, count), z in zip(cuts, drawn):
        keep, send = gradient(cotangent, own, z, width, first, count, valid)
        got = lax.ppermute(send, "pts", swap)
        wide = 2 * width if count % 2 == 0 and first % 2 == 0 else width
        out = join(keep, got, out, wide, first * width // wide, valid)
    return (residual, out.T, small[:, :hidden], small[:, hidden], small[:, hidden + 1])


def solution(mesh):
    return jax.shard_map(
        shards,
        mesh=mesh,
        in_specs=(P("pts"), P("pts", None), P("coord"), P(None, "coord"), P(), P(), P()),
        out_specs=(
            P(("pts", "coord")),
            P("pts", "coord"),
            P("coord", None),
            P("coord"),
            P("coord"),
        ),
        check_vma=False,
    )
```

time: 907 us -> 405 us (0.45)
  other arithmetic: 488 us -> 4.76 us
  Pallas kernels: 0 us -> 232 us
  waiting for transfers between devices: 272 us -> 82.6 us
  matrix products: 72.6 us -> 3.57 us
  local copies, waits for them, and re-layouts: 2.06 us -> 22.5 us
  blocking collectives: 47.9 us -> 38.5 us
    convert_element_type x5 -> x1, other arithmetic: 245 us -> 1 us  [shards(): small = lax.psum(small, 'pts').astype(jnp.float32)]
    reduce_sum x2 -> x3, other arithmetic: 242 us -> 1.38 us  [the longest x1 1.25 us: shards(): jnp.sum(squares, axis=1) / NOISE_SCALE ** 2]
    pallas_call x0 -> x7, Pallas kernels: none -> 232 us  [the longest x1 106 us: forward(): pl.pallas_call(functools.partial(forward_kernel, valid), grid=(steps,), i...]
    reduce_scatter x3 -> x1, waiting for transfers between devices: 220 us -> 28.4 us  [shards(): pre_local = lax.psum_scatter(pre, 'coord', scatter_dimension=0, tiled=True)]
    dot_general x3 -> x1, matrix products: 70.3 us -> 2.07 us  [shards(): lax.dot_general(grad_pre_two, hidden_one, (((0,), (0,)), ((), ())), prefe...]
    all_gather x1, waiting for transfers between devices: 51.2 us -> 0.01 us  [shards(): cotangent = lax.all_gather(mine, 'coord', axis=0)]
    unnamed x5, waiting for transfers between devices: 0.08 us -> 29.1 us
    psum x2 -> x0, blocking collectives: 29 us -> none  [the longest x1 23.4 us: shards(): squares_all, source_all = lax.psum((squares, source), 'coord')]
  transfers between devices with their start and end apart: 5 -> 9, of which waited for: 3 -> 4; matrix products, arithmetic and copies ran while one was open for 30% -> 2% of each run, Pallas kernels for 0% -> 57%
where the time goes in v1:
time: 405 us; the launch traced here: 404 us
  Pallas kernels  232 us (57%)
  waiting for transfers between devices  82.6 us (20%)
  blocking collectives  38.5 us (10%)
  local copies, waits for them, and re-layouts  22.5 us (6%)
  between operations  14.7 us (4%)
  starting transfers between devices  5.29 us (1%)
  other arithmetic  4.76 us (1%)
    pallas_call x1, Pallas kernels, forward(): pl.pallas_call(functools.partial(forward_kernel, valid), grid=(steps,), i...  106 us
    pallas_call x2, Pallas kernels, redraw(): pl.pallas_call(functools.partial(redraw_kernel, first), grid=(count,), in...  77.1 us
    unnamed x1, blocking collectives  38.5 us
    pallas_call x2, Pallas kernels, gradient(): pl.pallas_call(functools.partial(gradient_kernel, 1 + len(others)), grid=...  38.4 us
    unnamed x5, waiting for transfers between devices  29.1 us
    reduce_scatter x1, waiting for transfers between devices, shards(): pre_local = lax.psum_scatter(pre, 'coord', scatter_dimension=0, tiled=True)  28.4 us
    psum x1, waiting for transfers between devices, shards(): small = lax.psum(small, 'pts').astype(jnp.float32)  21.4 us
    pallas_call x2, Pallas kernels, join(): pl.pallas_call(join_kernel, grid=(count,), in_specs=specs, out_specs=pl.B...  10.7 us
  transfers between devices with their start and end apart: 9, of which 4 were waited for; matrix products, arithmetic and copies ran while one was open for 2% of the time, Pallas kernels for 57%

profile of v1, /device:TPU:0, one launch (start us, length us, event | category | flops | bytes accessed | tf_op | source)
XLA Modules:
  0.0 404.4 jit_solution(13679432909788409214)
XLA Ops:
  7.2 0.0 copy-start
  7.2 0.0 reduce-scatter.5.cloned.1.call-start
  7.2 3.0 collective-permute-start
  10.2 0.1 collective-permute-start.1
  10.3 0.8 copy.23
  11.1 0.7 shift-right-logical_xor_fusion.3
  11.7 0.1 reshape.68
  11.8 1.5 broadcast_in_dim.17.coef_ref
  13.3 1.0 broadcast_in_dim.15.pert_ref
  14.3 0.7 broadcast_in_dim.16.point_ref
  15.0 106.2 %forward.1 = (bf16[1024,12544]{1,0:T(8,128)(2,1)}, bf16[1024,1024]{1,0:T(8,128)(2,1)}, f32[1024,128]{1,0:T(8,128)}, f32[64,128]{1,0:T(8,128)}) custom-call(s32[1]{0:T(128)} %bitcast.base_ref, s32[1024,128]{1,0:T(8,128)} %broadcast_in_dim.15.pert_ref, s32[64,128]{1,0:T(8,128)} %broadcast_in_dim.16.point_ref, f32[1,12500]{1,0:T(1,128)} %broadcast_in_dim.17.coef_ref, ...), custom_call_target="tpu_custom_call" | custom-call | flops 51200000000 | bytes 51200000 | tf_op jit(solution)/shard_map/forward/pallas_call | solution.py:223
  121.2 0.0 copy-start.6
  121.2 0.0 copy-start.4
  121.2 0.0 collective-permute-done.1
  121.3 0.0 collective-permute-done
  121.3 0.0 reduce-scatter.5.cloned.1.call-update
  121.3 0.0 all-gather.4.cloned.1.call-start
  121.4 1.2 reduce_sum.54
  122.7 0.1 reduce_sum.55
  122.8 0.6 dynamic-slice.16
  124.1 0.1 maximum_dynamic-update-slice_fusion
  124.2 38.5 %all-reduce = f32[8704]{0:T(1024)S(1)} all-reduce(f32[8704]{0:T(1024)S(1)} %maximum_dynamic-update-slice_fusion), channel_id=2, replica_groups=mesh['pts'=4,'coord'=8] {'coord'}, use_global_device_ids=true, to_apply=%add | all-reduce | flops 8704 | bytes 69632
  162.7 0.1 reshape.71
  162.8 0.1 copy.24
  162.9 0.1 reshape.70
  163.0 28.4 %reduce-scatter.5.cloned.1.call-done = bf16[128,1024]{1,0:T(8,128)(2,1)} async-done(((bf16[1024,1024]{1,0:T(8,128)(2,1)}), bf16[128,1024]{1,0:T(8,128)(2,1)}) %reduce-scatter.5.cloned.1.call-update) | async-done | bytes 262160 | tf_op jit(solution)/shard_map/reduce_scatter | solution.py:382
  191.4 1.0 tanh_convert_fusion
  192.4 0.8 fusion
  193.2 0.2 fusion.3
  193.4 0.1 reshape.69
  193.5 0.1 reduce_sum.57
  193.6 0.1 dynamic-slice_subtract_fusion
  193.7 0.1 mul.103
  193.8 0.1 mul.104
  193.9 0.1 broadcast_multiply_fusion.1
  193.9 0.2 fusion.7
  194.1 0.5 fusion.10
  194.7 1.4 collective-permute-start.2
  196.1 3.6 collective-permute-done.2
  199.8 1.0 broadcast_in_dim.18.pert_ref
  200.8 0.7 broadcast_in_dim.19.point_ref
  201.5 0.8 copy.25
  202.3 0.0 all-gather.4.cloned.1.call-update
  202.3 0.2 reduce-scatter.7.cloned.1.call-start
  202.5 43.7 %redraw.3.refs_1_ = bf16[1024,7168]{1,0:T(8,128)(2,1)} custom-call(s32[1]{0:T(128)} %bitcast.base_ref, s32[1024,128]{1,0:T(8,128)} %broadcast_in_dim.18.pert_ref, s32[64,128]{1,0:T(8,128)} %broadcast_in_dim.19.point_ref), custom_call_target="tpu_custom_call" | custom-call | flops 29360128000 | bytes 14680064 | tf_op jit(solution)/shard_map/redraw/pallas_call | solution.py:259
  246.3 33.4 %redraw.2.refs_1_ = bf16[1024,5376]{1,0:T(8,128)(2,1)} custom-call(s32[1]{0:T(128)} %bitcast.base_ref, s32[1024,128]{1,0:T(8,128)} %broadcast_in_dim.18.pert_ref, s32[64,128]{1,0:T(8,128)} %broadcast_in_dim.19.point_ref), custom_call_target="tpu_custom_call" | custom-call | flops 22020096000 | bytes 11010048 | tf_op jit(solution)/shard_map/redraw/pallas_call | solution.py:259
  279.7 2.1 convolution_convert_fusion
  281.8 8.0 %concatenate.16 = bf16[1024,1152]{0,1:T(8,128)(2,1)S(1)} concatenate(bf16[1024,1024]{0,1:T(8,128)(2,1)} %convolution_convert_fusion, bf16[1024,1]{0,1:T(2,128)(2,1)S(1)} %broadcast_in_dim.20, bf16[1024,1]{0,1:T(2,128)(2,1)S(1)} %mul.122, bf16[1024,126]{0,1:T(8,128)(2,1)S(1)} %broadcast_in_dim.21), dimensions={1} | concatenate | bytes 4718592 | tf_op jit(solution)/shard_map/concatenate | solution.py:417
  289.8 2.5 copy.27
  292.3 0.0 reduce-scatter.7.cloned.1.call-update
  292.3 0.0 all-reduce.3.cloned.1.call-start
  292.4 21.1 %gradient.3 = (bf16[7168,256]{1,0:T(8,128)(2,1)}, bf16[7168,256]{1,0:T(8,128)(2,1)}) custom-call(bf16[8,2,512,128]{3,2,1,0:T(8,128)(2,1)} %bitcast.39, bf16[1024,12544]{1,0:T(8,128)(2,1)} %get-tuple-element.30.refs_0_, bf16[1024,7168]{1,0:T(8,128)(2,1)} %redraw.3.refs_1_), custom_call_target="tpu_custom_call" | custom-call | flops 15032385536 | bytes 29360128 | tf_op jit(solution)/shard_map/gradient/pallas_call | solution.py:281
  313.5 17.3 %gradient.2 = (bf16[5332,256]{1,0:T(8,128)(2,1)}, bf16[5332,256]{1,0:T(8,128)(2,1)}) custom-call(bf16[8,2,512,128]{3,2,1,0:T(8,128)(2,1)} %bitcast.40, bf16[1024,12544]{1,0:T(8,128)(2,1)} %get-tuple-element.30.refs_0_, bf16[1024,5376]{1,0:T(8,128)(2,1)} %redraw.2.refs_1_), custom_call_target="tpu_custom_call" | custom-call | flops 11274289152 | bytes 22020096 | tf_op jit(solution)/shard_map/gradient/pallas_call | solution.py:281
  330.8 0.5 collective-permute-start.3
  331.3 29.1 %reduce-scatter.7.cloned.1.call-done = bf16[128,1152]{1,0:T(8,128)(2,1)} async-done(((bf16[1024,1152]{1,0:T(8,128)(2,1)}), bf16[128,1152]{1,0:T(8,128)(2,1)}) %reduce-scatter.7.cloned.1.call-update) | async-done | bytes 294928
  360.3 1.8 copy.28
  362.2 0.0 all-reduce.3.cloned.1.call-update
  362.2 5.6 %join.2.refs_2_ = bf16[12500,256]{1,0:T(8,128)(2,1)} custom-call(bf16[7168,256]{1,0:T(8,128)(2,1)} %get-tuple-element.35.refs_0_, bf16[7168,256]{1,0:T(8,128)(2,1)} %collective-permute-done.4.refs_1_), custom_call_target="tpu_custom_call" | custom-call | flops 1835008 | bytes 11010048 | tf_op jit(solution)/shard_map/join/pallas_call | solution.py:304
  367.8 5.2 %join.3 = bf16[12500,256]{1,0:T(8,128)(2,1)} custom-call(bf16[5332,256]{1,0:T(8,128)(2,1)} %get-tuple-element.33.refs_0_, bf16[5332,256]{1,0:T(8,128)(2,1)} %collective-permute-done.3.refs_1_, bf16[12500,256]{1,0:T(8,128)(2,1)} %join.2.refs_2_), custom_call_target="tpu_custom_call", output_to_operand_aliasing={{}: (2, {})} | custom-call | flops 1364992 | bytes 8189952 | tf_op jit(solution)/shard_map/join/pallas_call | solution.py:304
  373.0 21.4 %all-reduce.3.cloned.1.call-done = bf16[128,1152]{0,1:T(8,128)(2,1)} async-done(((bf16[128,1152]{0,1:T(8,128)(2,1)}), bf16[128,1152]{0,1:T(8,128)(2,1)}) %all-reduce.3.cloned.1.call-update) | async-done | bytes 294928 | tf_op jit(solution)/shard_map/psum | solution.py:421
  394.4 1.0 slice.12
  395.3 1.0 copy.26
  396.3 1.0 convert_element_type.40
  397.3 0.5 slice_bitcast_fusion
  (32 shorter events, 0.2 us)
Async XLA Ops:
  7.2 185.2 %copy-start = (bf16[1024,1024]{1,0:T(8,128)(2,1)S(1)}, bf16[1024,1024]{1,0:T(8,128)(2,1)}, u32[]{:S(2)}) copy-start(bf16[1024,1024]{1,0:T(8,128)(2,1)} %param.12) | copy-start | bytes 6291460
  7.2 184.2 %reduce-scatter.5.cloned.1.call-start = ((), (), s32[]{:S(2)}) async-start(), calls=%async_computation.2 | async-start | bytes 2359296 | tf_op jit(solution)/shard_map/reduce_scatter | solution.py:382
  7.2 114.0 %collective-permute-start = (s32[64,16]{0,1:T(8,128)}, s32[64,16]{0,1:T(8,128)S(1)}, u32[]{:S(2)}, u32[]{:S(2)}) collective-permute-start(s32[64,16]{0,1:T(8,128)} %param.8), channel_id=1, source_target_pairs={{0,16},{8,24},{16,0},{24,8},{1,17},{9,25},{17,1},{25,9},{2,18},{10... | collective-permute-start | bytes 12296 | tf_op jit(solution)/shard_map/ppermute | solution.py:370
  10.2 111.0 %collective-permute-start.1 = (s32[64]{0:T(128)}, s32[64]{0:T(128)S(1)}, u32[]{:S(2)}, u32[]{:S(2)}) collective-permute-start(s32[64]{0:T(128)} %param.7), channel_id=1, source_target_pairs={{0,16},{8,24},{16,0},{24,8},{1,17},{9,25},{17,1},{25,9},{2,18},{10... | collective-permute-start | bytes 776 | tf_op jit(solution)/shard_map/ppermute | solution.py:370
  15.0 106.4 %copy-start.3 = (bf16[1024]{0:T(1024)(128)(2,1)S(1)}, bf16[1024]{0:T(1024)(128)(2,1)}, u32[]{:S(2)}) copy-start(bf16[1024]{0:T(1024)(128)(2,1)} %param.13) | copy-start | bytes 6148
  121.2 1.5 copy-start.2
  121.2 1.6 copy-start.6
  121.2 70.1 %copy-start.4 = (f32[1024]{0:T(1024)S(1)}, f32[1024]{0:T(1024)}, u32[]{:S(2)}) copy-start(f32[1024]{0:T(1024)} %param.11) | copy-start | bytes 12292
  121.3 158.4 %all-gather.4.cloned.1.call-start = ((), (), s32[]{:S(2)}) async-start(), calls=%async_computation.4 | async-start | bytes 2359296 | tf_op jit(solution)/shard_map/all_gather | solution.py:405
  193.7 7.1 %copy-start.5 = (f32[8]{0:T(128)}, f32[8]{0:T(128)S(1)}, u32[]{:S(2)}) copy-start(f32[8]{0:T(128)S(1)} %dynamic-slice_subtract_fusion) | copy-start | bytes 100
  194.7 5.0 %collective-permute-start.2 = (bf16[512,128]{0,1:T(8,128)(2,1)S(1)}, bf16[512,128]{0,1:T(8,128)(2,1)S(1)}, u32[]{:S(2)}, u32[]{:S(2)}) collective-permute-start(bf16[512,128]{0,1:T(8,128)(2,1)S(1)} %pad_maximum_fusion.1), channel_id=1, source_target_pairs={{0,16},{8,24},{16,0},{24,8},{1,17},{9,25},{17,1},{25,9},{2,18},{10... | collective-permute-start | bytes 393224 | tf_op jit(solution)/shard_map/ppermute | solution.py:370
  202.3 158.0 %reduce-scatter.7.cloned.1.call-start = ((), (), s32[]{:S(2)}) async-start(), calls=%async_computation.5 | async-start | bytes 2654208
  292.3 102.0 %all-reduce.3.cloned.1.call-start = ((), (), s32[]{:S(2)}) async-start(), calls=%async_computation.3 | async-start | bytes 589824 | tf_op jit(solution)/shard_map/psum | solution.py:421
  313.5 48.7 %collective-permute-start.4 = (bf16[7168,256]{1,0:T(8,128)(2,1)}, bf16[7168,256]{1,0:T(8,128)(2,1)}, u32[]{:S(2)}, u32[]{:S(2)}) collective-permute-start(bf16[7168,256]{1,0:T(8,128)(2,1)} %get-tuple-element.36), channel_id=1, source_target_pairs={{0,8},{8,0},{16,24},{24,16},{1,9},{9,1},{17,25},{25,17},{2,10},{10... | collective-permute-start | bytes 11010056 | tf_op jit(solution)/shard_map/ppermute | solution.py:427
  330.8 37.0 %collective-permute-start.3 = (bf16[5332,256]{1,0:T(8,128)(2,1)}, bf16[5332,256]{1,0:T(8,128)(2,1)}, u32[]{:S(2)}, u32[]{:S(2)}) collective-permute-start(bf16[5332,256]{1,0:T(8,128)(2,1)} %get-tuple-element.34), channel_id=1, source_target_pairs={{0,8},{8,0},{16,24},{24,16},{1,9},{9,1},{17,25},{25,17},{2,10},{10... | collective-permute-start | bytes 8189960 | tf_op jit(solution)/shard_map/ppermute | solution.py:427
  367.8 30.1 %copy-start.1 = (bf16[1024,1024]{1,0:T(8,128)(2,1)S(1)}, bf16[1024,1024]{1,0:T(8,128)(2,1)}, u32[]{:S(2)}) copy-start(bf16[1024,1024]{1,0:T(8,128)(2,1)} %param.12) | copy-start | bytes 6291460
Sparse Core Ops, SparseCore 0:
  121.4 69.8 reduce-scatter.4
  202.4 48.2 all-gather.3
  292.4 67.8 reduce-scatter.6
  363.1 31.2 all-reduce.2

commit v2 on v1

--- a/solution.py
+++ b/solution.py
@@ -68,7 +68,7 @@
 
 def pieces(width):
     tiles = width // LANES
-    parts = -(-tiles // 4)
+    parts = -(-tiles // 2)
     edges = [tiles * i // parts for i in range(parts + 1)]
     return [(a * LANES, b * LANES) for a, b in zip(edges, edges[1:])]
 
@@ -83,7 +83,7 @@
 
 def forward_kernel(
     valid, base_ref, pert_ref, point_ref, coef_ref, w_prev, w_now,
-    z_ref, pre_ref, sq_ref, src_ref, held_a, held_b, acc, keys, xs,
+    z_ref, pre_ref, sums_ref, held_a, held_b, acc, keys, xs, sq_ref, src_ref,
 ):
     step, last = pl.program_id(0), pl.num_programs(0) - 1
     rows, width = z_ref.shape
@@ -114,23 +114,33 @@
             term[:, a:a + LANES] for a in range(0, width, LANES)
         )
 
-    def weights(ref, of):
-        cut = width - -(-pad // 16) * 16
-        if cut == width:
-            return ref[...]
-        place = lax.broadcasted_iota(jnp.int32, (width - cut, ref.shape[1]), 0) + (of * width + cut)
-        tail = jnp.where(place < valid, ref[cut:, :], jnp.zeros((), ref.dtype))
-        return jnp.concatenate([ref[:cut, :], tail], axis=0)
-
-    def multiply(group, held, ref, of):
-        at = group * GROUP
-        acc[at:at + GROUP, :] += jnp.dot(
-            held[...], weights(ref, of), preferred_element_type=jnp.float32
+    cut = width - -(-pad // 16) * 16
+
+    def multiply(group, part, held, ref, of):
+        at, left = group * GROUP, part * GROUP
+        w = ref[:, left:left + GROUP]
+        if pad:
+            place = lax.broadcasted_iota(jnp.int32, (width - cut, GROUP), 0) + (of * width + cut)
+            tail = jnp.where(place < valid, w[cut:], jnp.zeros((), w.dtype))
+            w = jnp.concatenate([w[:cut], tail], axis=0)
+        acc[at:at + GROUP, left:left + GROUP] += jnp.dot(
+            held[...], w, preferred_element_type=jnp.float32
         )
+
+    parts = acc.shape[1] // GROUP
+    group_points = GROUP // samples
 
     for group in range(groups):
         held = (held_a, held_b)[group % 2]
-        for at in range(0, GROUP, samples):
+        other = (held_b, held_a)[group % 2]
+        for number in range(group_points):
+            if number % (group_points // parts) == 0:
+                part = number // (group_points // parts)
+                if group == 0:
+                    multiply(groups - 1, part, other, w_prev, jnp.maximum(step - 1, 0))
+                else:
+                    multiply(group - 1, part, other, w_now, step)
+            at = number * samples
             row = group * GROUP + at
             point = row // samples
             seeds = pert_ref[row:row + samples]
@@ -143,23 +153,25 @@
                 z_ref[row:row + samples, a:b] = z
                 square = noise * noise
                 for c in range(a, b, LANES):
-                    part = square[:, c - a:c - a + LANES]
+                    cell = square[:, c - a:c - a + LANES]
                     if (steps - 1) * width + c + LANES > valid:
-                        part = jnp.where(jnp.concatenate([inside[:, c:c + LANES]] * 2, axis=0), part, 0.0)
-                    total = part if total is None else total + part
+                        cell = jnp.where(jnp.concatenate([inside[:, c:c + LANES]] * 2, axis=0), cell, 0.0)
+                    total = cell if total is None else total + cell
             sq_ref[row:row + samples] += total
-        if group == 0:
-            multiply(groups - 1, held_b, w_prev, jnp.maximum(step - 1, 0))
-        else:
-            multiply(group - 1, (held_b, held_a)[group % 2], w_now, step)
 
     @pl.when(step == last)
     def _():
-        multiply(groups - 1, held_b, w_now, step)
+        for part in range(parts):
+            multiply(groups - 1, part, held_b, w_now, step)
         pre_ref[...] = acc[...].astype(pre_ref.dtype)
-
-
-def redraw_kernel(first, base_ref, pert_ref, point_ref, z_ref, keys, xs):
+        sums_ref[...] = jnp.zeros_like(sums_ref)
+        for block in range(rows // LANES):
+            square = jnp.sum(sq_ref[block * LANES:(block + 1) * LANES].T, axis=0, keepdims=True)
+            sums_ref[block:block + 1] = square / NOISE_SCALE**2
+        sums_ref[8:9, :points] = jnp.sum(src_ref[...].T, axis=0, keepdims=True) / math.sqrt(D)
+
+
+def redraw_kernel(first, base_ref, pert_ref, point_ref, _, z_ref, mark_ref, keys, xs):
     step = pl.program_id(0) + first
     rows, width = z_ref.shape
     points = point_ref.shape[0]
@@ -167,6 +179,7 @@
     _, (key_zero, key_one, key_two) = column_keys(base_ref[0], step, width)
     keys[0:8] = key_zero
     keys[8:16] = key_one
+    mark_ref[...] = jnp.zeros_like(mark_ref)
     for at in range(0, points, 8):
         xs[at:at + 8] = coordinate(point_rows(point_ref[at:at + 8], key_two, width))
 
@@ -182,18 +195,27 @@
                 z_ref[pl.ds(row, samples), a:b] = (x + noise).astype(jnp.bfloat16)
 
 
-def gradient_kernel(count, d_ref, *refs):
-    z_refs, (keep_ref, send_ref) = refs[:count], refs[count:]
-    blocks, _, hidden, _ = d_ref.shape
+def gradient_kernel(count, per, _, d_ref, *refs):
+    z_refs, (keep_ref, send_ref, left) = refs[:count], refs[count:]
+    blocks, _, hidden = d_ref.shape
     half = hidden // 2
-    left = jnp.concatenate(
-        [d_ref[block, source] for source in range(count) for block in range(blocks)], axis=1
-    )
+    together = LANES // per
+
+    @pl.when(pl.program_id(0) == 0)
+    def _():
+        for source in range(count):
+            for block in range(0, blocks, together):
+                at = source * blocks * per + block * per
+                rows = jnp.concatenate(
+                    [d_ref[block + i, source * per:(source + 1) * per] for i in range(together)], axis=0
+                )
+                left[:, at:at + LANES] = rows.T
+
     width = keep_ref.shape[0]
     stride = 256 if width % 256 == 0 else LANES
     for a in range(0, width, stride):
         z = jnp.concatenate([ref[:, a:a + stride] for ref in z_refs], axis=0)
-        part = jnp.dot(left, z, preferred_element_type=jnp.float32).astype(jnp.bfloat16).T
+        part = jnp.dot(left[...], z, preferred_element_type=jnp.float32).astype(jnp.bfloat16).T
         keep_ref[a:a + stride, :] = part[:, :half]
         send_ref[a:a + stride, :] = part[:, half:]
 
@@ -231,13 +253,12 @@
         ],
         out_specs=[
             pl.BlockSpec((rows, width), lambda s: (0, s)),
-            whole((rows, hidden)), whole((rows, LANES)), whole((points, LANES)),
+            whole((rows, hidden)), whole((16, LANES)),
         ],
         out_shape=[
             jax.ShapeDtypeStruct((rows, steps * width), jnp.bfloat16),
             jax.ShapeDtypeStruct((rows, hidden), jnp.bfloat16),
-            jax.ShapeDtypeStruct((rows, LANES), jnp.float32),
-            jax.ShapeDtypeStruct((points, LANES), jnp.float32),
+            jax.ShapeDtypeStruct((16, LANES), jnp.float32),
         ],
         scratch_shapes=[
             pltpu.VMEM((GROUP, width), jnp.bfloat16),
@@ -245,6 +266,8 @@
             pltpu.VMEM((rows, hidden), jnp.float32),
             pltpu.VMEM((16, width), jnp.int32),
             pltpu.VMEM((points, width), jnp.float32),
+            pltpu.VMEM((rows, LANES), jnp.float32),
+            pltpu.VMEM((points, LANES), jnp.float32),
         ],
         compiler_params=params(),
         cost_estimate=pl.CostEstimate(
@@ -254,14 +277,20 @@
     )(base, pert, point, coef, w, w)
 
 
-def redraw(base, pert, point, width, first, count):
+def redraw(base, pert, point, after, width, first, count):
     rows, points = pert.shape[0], point.shape[0]
     return pl.pallas_call(
         functools.partial(redraw_kernel, first),
         grid=(count,),
-        in_specs=[pl.BlockSpec(memory_space=pltpu.SMEM), whole(pert.shape), whole(point.shape)],
-        out_specs=pl.BlockSpec((rows, width), lambda s: (0, s)),
-        out_shape=jax.ShapeDtypeStruct((rows, count * width), jnp.bfloat16),
+        in_specs=[
+            pl.BlockSpec(memory_space=pltpu.SMEM), whole(pert.shape), whole(point.shape),
+            pl.BlockSpec(memory_space=pl.ANY),
+        ],
+        out_specs=[pl.BlockSpec((rows, width), lambda s: (0, s)), whole((8, LANES))],
+        out_shape=[
+            jax.ShapeDtypeStruct((rows, count * width), jnp.bfloat16),
+            jax.ShapeDtypeStruct((8, LANES), jnp.float32),
+        ],
         scratch_shapes=[pltpu.VMEM((16, width), jnp.int32), pltpu.VMEM((points, width), jnp.float32)],
         compiler_params=params(),
         cost_estimate=pl.CostEstimate(
@@ -269,29 +298,30 @@
             transcendentals=2 * rows * width * count,
         ),
         name="redraw",
-    )(base, pert, point)
-
-
-def gradient(cotangent, own, others, width, first, count, valid):
+    )(base, pert, point, after)
+
+
+def gradient(after, cotangent, per, own, others, width, first, count, valid):
     if count % 2 == 0 and first % 2 == 0:
         width, first, count = 2 * width, first // 2, count // 2
     rows = own.shape[0]
     half = cotangent.shape[2] // 2
     height = min(valid, (first + count) * width) - first * width
     return pl.pallas_call(
-        functools.partial(gradient_kernel, 1 + len(others)),
+        functools.partial(gradient_kernel, 1 + len(others), per),
         grid=(count,),
-        in_specs=[whole(cotangent.shape), pl.BlockSpec((rows, width), lambda s: (0, s + first))]
+        in_specs=[pl.BlockSpec(memory_space=pl.ANY), whole(cotangent.shape), pl.BlockSpec((rows, width), lambda s: (0, s + first))]
         + [pl.BlockSpec((rows, width), lambda s: (0, s)) for _ in others],
         out_specs=[pl.BlockSpec((width, half), lambda s: (s, 0))] * 2,
         out_shape=[jax.ShapeDtypeStruct((height, half), jnp.bfloat16)] * 2,
+        scratch_shapes=[pltpu.VMEM((2 * half, (1 + len(others)) * rows), jnp.bfloat16)],
         compiler_params=params(),
         cost_estimate=pl.CostEstimate(
             flops=4 * half * rows * (1 + len(others)) * width * count,
             bytes_accessed=2 * rows * (1 + len(others)) * width * count, transcendentals=0,
         ),
         name="gradient",
-    )(cotangent, own, *others)
+    )(after, cotangent, own, *others)
 
 
 def join(keep, got, before, width, first, valid):
@@ -375,59 +405,76 @@
     other_seeds = [shift((pert_seed, point_seed), by) for by in range(1, chips)]
 
     pert, point = lanes_of(pert_seed), lanes_of(point_seed)
-    own, pre, squares, source = forward(base, pert, point, source_coef[None, :], w1.T, width)
-    other_seeds, pre = tie(other_seeds, pre)
+    own, pre, sums = forward(base, pert, point, source_coef[None, :], w1.T, width)
     others_in = [(lanes_of(a), lanes_of(b)) for a, b in other_seeds]
 
+    sums = lax.all_gather(sums, "coord", axis=0)
     pre_local = lax.psum_scatter(pre, "coord", scatter_dimension=0, tiled=True)
-    sums = jnp.concatenate(
-        [jnp.sum(squares, axis=1) / NOISE_SCALE**2, jnp.sum(source, axis=1) / math.sqrt(D)]
-    )
-    sums = jnp.sum(lax.all_gather(sums, "coord", axis=0), axis=0)
-    squares_local = lax.dynamic_slice_in_dim(sums, coord_index * rows_local, rows_local, 0)
-    source_local = lax.dynamic_slice_in_dim(sums, rows_here + coord_index * points_local, points_local, 0)
 
     early = steps // 2 + (steps // 2) % 2
     cuts = [(0, early), (early, steps - early)]
-    drawn = [[redraw(base, a, b, width, *cuts[0]) for a, b in others_in]]
-
+    drawn = [[redraw(base, a, b, pre, width, *cuts[0]) for a, b in others_in]]
+    (pre_local, sums), _ = tie((pre_local, sums), [mark for _, mark in drawn[0]])
+
+    sums = jnp.sum(sums, axis=0)
+    squares_local = lax.dynamic_slice_in_dim(sums[:8].reshape(-1), coord_index * rows_local, rows_local, 0)
+    source_local = lax.dynamic_slice_in_dim(sums[8], coord_index * points_local, points_local, 0)
     residual, grad_pre_one, grad_readout, hidden_one, grad_pre_two = hidden_pass(
         pre_local.astype(jnp.float32) + b1[None, :], squares_local, source_local, w2, w3, samples
     )
-    turned = grad_pre_one.T
 
     def share_of(index):
-        return [lax.dynamic_slice_in_dim(turned, i * share, share, 0) for i in (index, index ^ 1)]
-
-    sent = [jnp.concatenate(share_of((pts_index + 2 * by) % pts_count), axis=0) for by in range(chips)]
-    mine = jnp.stack([sent[0]] + [shift(sent[by], by) for by in range(1, chips)])
-    others_in, mine = tie(others_in, mine)
+        return jnp.concatenate(
+            [lax.dynamic_slice_in_dim(grad_pre_one, i * share, share, 1) for i in (index, index ^ 1)], axis=1
+        )
+
+    sent = [share_of((pts_index + 2 * by) % pts_count) for by in range(chips)]
+    readout_rows = grad_readout.astype(jnp.bfloat16).reshape(-1, 2 * share)
+    readout_rows = jnp.pad(readout_rows, ((0, 16 - readout_rows.shape[0]), (0, 0)))
+    mine = jnp.concatenate([sent[0]] + [shift(sent[by], by) for by in range(1, chips)] + [readout_rows], axis=0)
     cotangent = lax.all_gather(mine, "coord", axis=0)
-    blocks = rows_here // LANES
-    if rows_local != LANES:
-        cotangent = cotangent.transpose(1, 2, 0, 3).reshape(chips, 2 * share, blocks, LANES)
-        cotangent = cotangent.transpose(2, 0, 1, 3)
-    drawn.append([redraw(base, a, b, width, *cuts[1]) for a, b in others_in])
-
-    (hidden_one, grad_pre_two), cotangent = tie((hidden_one, grad_pre_two), cotangent)
+    drawn.append([redraw(base, a, b, mine, width, *cuts[1]) for a, b in others_in])
+
+    def rotate(a, by):
+        return lax.ppermute(a, "pts", [(i, (i + by) % pts_count) for i in range(pts_count)])
+
     grad_second = lax.dot_general(
         grad_pre_two, hidden_one, (((0,), (0,)), ((), ())), preferred_element_type=jnp.float32
+    ).astype(jnp.bfloat16)
+    quarter = hidden // coord_count // pts_count
+    grad_second = grad_second.reshape(coord_count, pts_count, quarter, hidden)
+
+    def second_part(index):
+        return lax.dynamic_slice_in_dim(grad_second, index, 1, 1).reshape(coord_count * quarter, hidden)
+
+    second = second_part(pts_index).astype(jnp.float32)
+    for by in range(1, pts_count):
+        second += rotate(second_part((pts_index + by) % pts_count), by).astype(jnp.float32)
+    second, _ = tie(second.astype(jnp.bfloat16), cotangent[0, :16])
+    scattered = lax.psum_scatter(second, "coord", scatter_dimension=0, tiled=True)
+    second = lax.all_gather(scattered, "pts", axis=0, tiled=True).astype(jnp.float32)
+
+    wide = cotangent.astype(jnp.float32)
+    bias_half = jnp.sum(wide[:, :chips * rows_local], axis=(0, 1))
+    readout = jnp.sum(wide[:, chips * rows_local:chips * rows_local + pts_count // 2], axis=0).reshape(-1)
+    bias = jnp.zeros((hidden,), jnp.float32)
+    for number, index in enumerate((pts_index, pts_index ^ 1)):
+        bias = lax.dynamic_update_slice_in_dim(bias, bias_half[number * share:(number + 1) * share], index * share, 0)
+    vectors = jnp.stack([bias, readout]).reshape(-1, LANES)
+    vectors = vectors + sum(rotate(vectors, by) for by in range(1, pts_count))
+    bias, readout = (
+        lax.dynamic_slice_in_dim(v, coord_index * (hidden // coord_count), hidden // coord_count, 0)
+        for v in vectors.reshape(2, hidden)
     )
-    grad_bias = jnp.sum(grad_pre_one.astype(jnp.float32), axis=0)
-    small = jnp.concatenate(
-        [grad_second, grad_bias[:, None], grad_readout[:, None], jnp.zeros((hidden, LANES - 2), jnp.float32)], axis=1
-    ).astype(jnp.bfloat16)
-    small = lax.psum_scatter(small, "coord", scatter_dimension=0, tiled=True)
-    small = lax.psum(small, "pts").astype(jnp.float32)
 
     out = None
     swap = [(i, i ^ 1) for i in range(pts_count)]
-    for (first, count), z in zip(cuts, drawn):
-        keep, send = gradient(cotangent, own, z, width, first, count, valid)
+    for (first, count), z, after in zip(cuts, drawn, (mine, scattered)):
+        keep, send = gradient(after, cotangent, rows_local, own, [a for a, _ in z], width, first, count, valid)
         got = lax.ppermute(send, "pts", swap)
         wide = 2 * width if count % 2 == 0 and first % 2 == 0 else width
         out = join(keep, got, out, wide, first * width // wide, valid)
-    return (residual, out.T, small[:, :hidden], small[:, hidden], small[:, hidden + 1])
+    return (residual, out.T, second, bias, readout)
 
 
 def solution(mesh):

time: 405 us -> 390 us (0.963)
  local copies, waits for them, and re-layouts: 22.5 us -> 7.74 us
  waiting for transfers between devices: 82.6 us -> 76 us
  starting transfers between devices: 5.29 us -> 10.2 us
    unnamed x1 -> x0, blocking collectives: 38.5 us -> none
    all_gather x0 -> x2, blocking collectives: none -> 37.9 us  [the longest x1 31.7 us: shards(): sums = lax.all_gather(sums, 'coord', axis=0)]
    reduce_scatter x0 -> x1, waiting for transfers between devices: none -> 37.1 us  [shards(): lax.psum_scatter(second, 'coord', scatter_dimension=0, tiled=True)]
    unnamed x5 -> x3, waiting for transfers between devices: 29.1 us -> 0.05 us
    psum x1 -> x0, waiting for transfers between devices: 21.4 us -> none  [shards(): small = lax.psum(small, 'pts').astype(jnp.float32)]
    concatenate x1 -> x0, local copies, waits for them, and re-layouts: 7.97 us -> none  [shards(): jnp.concatenate([grad_second, grad_bias[:, None], grad_readout[:, None],...]
    reduce_scatter x1, waiting for transfers between devices: 28.4 us -> 35.4 us  [shards(): pre_local = lax.psum_scatter(pre, 'coord', scatter_dimension=0, tiled=True)]
    unnamed x21 -> x23, local copies, waits for them, and re-layouts: 6.77 us -> 0.97 us
  transfers between devices with their start and end apart: 9 -> 14, of which waited for: 4 -> 3; matrix products, arithmetic and copies ran while one was open for 2% -> 2% of each run, Pallas kernels for 57% -> 32%
where the time goes in v2:
time: 390 us
  Pallas kernels  236 us (61%)
  waiting for transfers between devices  76 us (19%)
  blocking collectives  37.9 us (10%)
  between operations  14.1 us (4%)
  starting transfers between devices  10.2 us (3%)
  local copies, waits for them, and re-layouts  7.74 us (2%)
  other arithmetic  4.84 us (1%)
    pallas_call x1, Pallas kernels, forward(): pl.pallas_call(functools.partial(forward_kernel, valid), grid=(steps,), i...  106 us
    pallas_call x2, Pallas kernels, redraw(): pl.pallas_call(functools.partial(redraw_kernel, first), grid=(count,), in...  76.7 us
    pallas_call x2, Pallas kernels, gradient(): pl.pallas_call(functools.partial(gradient_kernel, 1 + len(others), per),...  42.9 us
    reduce_scatter x1, waiting for transfers between devices, shards(): lax.psum_scatter(second, 'coord', scatter_dimension=0, tiled=True)  37.1 us
    reduce_scatter x1, waiting for transfers between devices, shards(): pre_local = lax.psum_scatter(pre, 'coord', scatter_dimension=0, tiled=True)  35.4 us
    all_gather x1, blocking collectives, shards(): sums = lax.all_gather(sums, 'coord', axis=0)  31.7 us
    pallas_call x2, Pallas kernels, join(): pl.pallas_call(join_kernel, grid=(count,), in_specs=specs, out_specs=pl.B...  10.7 us
  transfers between devices with their start and end apart: 14, of which 3 were waited for; matrix products, arithmetic and copies ran while one was open for 2% of the time, Pallas kernels for 32%

profile of v2, /device:TPU:0, one launch (start us, length us, event | category | flops | bytes accessed | tf_op | source)
XLA Modules:
  0.0 390.1 jit_solution(4891693324705981197)
XLA Ops:
  7.2 0.0 copy-start
  7.2 0.0 reduce-scatter.3.cloned.1.call-start
  7.2 0.9 copy.17
  8.2 0.1 reshape.100
  8.2 1.5 broadcast_in_dim.12.coef_ref
  9.7 0.7 shift-right-logical_xor_fusion.3
  10.4 1.0 broadcast_in_dim.10.pert_ref
  11.4 0.7 broadcast_in_dim.11.point_ref
  12.0 105.8 %forward.1 = (bf16[1024,12544]{1,0:T(8,128)(2,1)}, bf16[1024,1024]{1,0:T(8,128)(2,1)}, f32[16,128]{1,0:T(8,128)}) custom-call(s32[1]{0:T(128)} %bitcast.base_ref, s32[1024,128]{1,0:T(8,128)} %broadcast_in_dim.10.pert_ref, s32[64,128]{1,0:T(8,128)} %broadcast_in_dim.11.point_ref, f32[1,12500]{1,0:T(1,128)} %broadcast_in_dim.12.coef_ref, ...), custom_call_target="tpu_custom_call" | custom-call | flops 51200000000 | bytes 51200000 | tf_op jit(solution)/shard_map/forward/pallas_call | solution.py:245
  117.8 0.0 reduce-scatter.3.cloned.1.call-update
  117.8 0.0 all-gather.4.cloned.1.call-start
  117.9 3.0 collective-permute-start.4
  120.9 0.1 collective-permute-start.5
  121.0 31.7 %all-gather = f32[128,128]{1,0:T(8,128)S(1)} all-gather(f32[16,128]{1,0:T(8,128)} %get-tuple-element.17), channel_id=2, replica_groups=mesh['pts'=4,'coord'=8] {'coord'}, dimensions={0}, use_global_device_ids=true | all-gather | bytes 73728 | tf_op jit(solution)/shard_map/all_gather | solution.py:411
  152.8 0.0 collective-permute-done.5
  152.8 0.1 copy.22
  152.9 0.1 reshape.107
  153.0 35.4 %reduce-scatter.3.cloned.1.call-done = bf16[128,1024]{1,0:T(8,128)(2,1)} async-done(((bf16[1024,1024]{1,0:T(8,128)(2,1)}), bf16[128,1024]{1,0:T(8,128)(2,1)}) %reduce-scatter.3.cloned.1.call-update) | async-done | bytes 262160 | tf_op jit(solution)/shard_map/reduce_scatter | solution.py:412
  188.5 1.8 fusion
  190.3 0.2 fusion.3
  190.5 0.1 reshape.102
  190.5 0.1 reduce_sum.46
  190.7 0.1 fusion.16
  190.8 0.1 mul.103
  190.8 0.1 mul.104
  190.9 0.1 broadcast_multiply_fusion
  191.0 0.5 fusion.1
  191.6 1.5 collective-permute-start.3
  193.2 0.1 fusion.11
  193.3 3.3 collective-permute-done.3
  196.7 0.7 fusion.12._
  197.4 0.0 all-gather.4.cloned.1.call-update
  197.4 0.2 reduce-scatter.5.cloned.1.call-start
  197.6 1.0 broadcast_in_dim.13.pert_ref
  198.6 0.7 broadcast_in_dim.14.point_ref
  199.3 43.5 %redraw.3 = (bf16[1024,7168]{1,0:T(8,128)(2,1)}, f32[8,128]{1,0:T(8,128)}) custom-call(s32[1]{0:T(128)} %bitcast.base_ref, s32[1024,128]{1,0:T(8,128)} %broadcast_in_dim.13.pert_ref, s32[64,128]{1,0:T(8,128)} %broadcast_in_dim.14.point_ref, bf16[1024,1024]{1,0:T(8,128)(2,1)} %get-tuple-element.16._), custom_call_target="tpu_custom_call" | custom-call | flops 29360128000 | bytes 14680064 | tf_op jit(solution)/shard_map/redraw/pallas_call | solution.py:282
  242.8 0.8 convolution_convert_fusion
  243.6 0.2 constant_dynamic-slice_fusion.7
  243.8 0.1 collective-permute-start
  243.9 1.5 collective-permute-start.1
  245.4 1.4 collective-permute-start.2
  246.8 33.2 %redraw.2 = (bf16[1024,5376]{1,0:T(8,128)(2,1)}, f32[8,128]{1,0:T(8,128)}) custom-call(s32[1]{0:T(128)} %bitcast.base_ref, s32[1024,128]{1,0:T(8,128)} %broadcast_in_dim.13.pert_ref, s32[64,128]{1,0:T(8,128)} %broadcast_in_dim.14.point_ref, bf16[272,512]{1,0:T(8,128)(2,1)} %fusion.12._), custom_call_target="tpu_custom_call" | custom-call | flops 22020096000 | bytes 11010048 | tf_op jit(solution)/shard_map/redraw/pallas_call | solution.py:282
  280.0 0.0 collective-permute-done
  280.0 0.0 collective-permute-done.1
  280.0 1.2 fusion.6
  281.2 0.0 reduce-scatter.5.cloned.1.call-update
  281.3 0.0 all-gather.4.cloned.1.call-done
  281.3 22.9 %gradient.3 = (bf16[7168,256]{1,0:T(8,128)(2,1)}, bf16[7168,256]{1,0:T(8,128)(2,1)}) custom-call(bf16[272,512]{1,0:T(8,128)(2,1)} %fusion.12._, bf16[8,272,512]{2,1,0:T(8,128)(2,1)} %bitcast.47, bf16[1024,12544]{1,0:T(8,128)(2,1)} %get-tuple-element.20.refs_0_, bf16[1024,7168]{1,0:T(8,128)(2,1)} %get-tuple-element.24.refs_1_), custom_call_target="tpu_custom_call" | custom-call | flops 15032385536 | bytes 29360128 | tf_op jit(solution)/shard_map/gradient/pallas_call | solution.py:310
  304.2 0.0 collective-permute-start.7
  304.2 37.1 %reduce-scatter.5.cloned.1.call-done._ = bf16[32,1024]{1,0:T(8,128)(2,1)} async-done(((bf16[256,1024]{1,0:T(8,128)(2,1)}), bf16[32,1024]{1,0:T(8,128)(2,1)}) %reduce-scatter.5.cloned.1.call-update) | async-done | bytes 65552 | tf_op jit(solution)/shard_map/reduce_scatter | solution.py:454
  341.3 20.0 %gradient.2 = (bf16[5332,256]{1,0:T(8,128)(2,1)}, bf16[5332,256]{1,0:T(8,128)(2,1)}) custom-call(bf16[32,1024]{1,0:T(8,128)(2,1)} %reduce-scatter.5.cloned.1.call-done._, bf16[8,272,512]{2,1,0:T(8,128)(2,1)} %bitcast.48, bf16[1024,12544]{1,0:T(8,128)(2,1)} %get-tuple-element.20.refs_0_, bf16[1024,5376]{1,0:T(8,128)(2,1)} %get-tuple-element.21.refs_1_), custom_call_target="tpu_custom_call" | custom-call | flops 11274289152 | bytes 22020096 | tf_op jit(solution)/shard_map/gradient/pallas_call | solution.py:310
  361.3 0.6 convert_element_type.78
  362.0 0.3 slice_reduce_fusion
  362.4 1.6 collective-permute-start.10
  364.0 0.0 collective-permute-start.8
  364.0 0.6 collective-permute-start.9
  364.6 6.2 %all_gather.19 = bf16[128,1024]{1,0:T(8,128)(2,1)S(1)} all-gather(bf16[32,1024]{1,0:T(8,128)(2,1)S(1)} %copy-done.4), channel_id=1, replica_groups=mesh['pts'=4,'coord'=8] {'pts'}, dimensions={0}, use_global_device_ids=true | all-gather | bytes 327680 | tf_op jit(solution)/shard_map/all_gather | solution.py:455
  370.8 0.8 convert_element_type.77
  371.6 0.0 collective-permute-done.10
  371.6 0.0 collective-permute-done.8
  371.7 0.6 dynamic_slice.50
  372.3 0.6 dynamic_slice.49
  372.8 5.5 %join.2.refs_2_ = bf16[12500,256]{1,0:T(8,128)(2,1)} custom-call(bf16[7168,256]{1,0:T(8,128)(2,1)} %get-tuple-element.25.refs_0_, bf16[7168,256]{1,0:T(8,128)(2,1)} %collective-permute-done.7.refs_1_), custom_call_target="tpu_custom_call" | custom-call | flops 1835008 | bytes 11010048 | tf_op jit(solution)/shard_map/join/pallas_call | solution.py:334
  378.4 5.2 %join.3 = bf16[12500,256]{1,0:T(8,128)(2,1)} custom-call(bf16[5332,256]{1,0:T(8,128)(2,1)} %get-tuple-element.22.refs_0_, bf16[5332,256]{1,0:T(8,128)(2,1)} %collective-permute-done.6.refs_1_, bf16[12500,256]{1,0:T(8,128)(2,1)} %join.2.refs_2_), custom_call_target="tpu_custom_call", output_to_operand_aliasing={{}: (2, {})} | custom-call | flops 1364992 | bytes 8189952 | tf_op jit(solution)/shard_map/join/pallas_call | solution.py:334
  (47 shorter events, 0.3 us)
Async XLA Ops:
  7.2 181.3 %copy-start = (bf16[1024,1024]{1,0:T(8,128)(2,1)S(1)}, bf16[1024,1024]{1,0:T(8,128)(2,1)}, u32[]{:S(2)}) copy-start(bf16[1024,1024]{1,0:T(8,128)(2,1)} %param.12) | copy-start | bytes 6291460
  7.2 181.2 %reduce-scatter.3.cloned.1.call-start = ((), (), s32[]{:S(2)}) async-start(), calls=%async_computation.2 | async-start | bytes 2359296 | tf_op jit(solution)/shard_map/reduce_scatter | solution.py:412
  12.0 105.8 %copy-start.6 = (s32[64,16]{0,1:T(8,128)S(1)}, s32[64,16]{0,1:T(8,128)}, u32[]{:S(2)}) copy-start(s32[64,16]{0,1:T(8,128)} %param.8) | copy-start | bytes 12292
  12.0 108.9 %copy-start.9 = (s32[64]{0:T(128)S(1)}, s32[64]{0:T(128)}, u32[]{:S(2)}) copy-start(s32[64]{0:T(128)} %param.7) | copy-start | bytes 772
  12.0 108.9 %copy-start.7 = (bf16[1024]{0:T(1024)(128)(2,1)S(1)}, bf16[1024]{0:T(1024)(128)(2,1)}, u32[]{:S(2)}) copy-start(bf16[1024]{0:T(1024)(128)(2,1)} %param.13) | copy-start | bytes 6148
  12.0 176.4 %copy-start.5 = (f32[1024]{0:T(1024)S(1)}, f32[1024]{0:T(1024)}, u32[]{:S(2)}) copy-start(f32[1024]{0:T(1024)} %param.11) | copy-start | bytes 12292
  117.8 163.5 %all-gather.4.cloned.1.call-start = ((), (), s32[]{:S(2)}) async-start(), calls=%async_computation.4 | async-start | bytes 2506752 | tf_op jit(solution)/shard_map/all_gather | solution.py:435
  117.9 34.9 %collective-permute-start.4 = (s32[64,16]{0,1:T(8,128)S(1)}, s32[64,16]{0,1:T(8,128)S(1)}, u32[]{:S(2)}, u32[]{:S(2)}) collective-permute-start(s32[64,16]{0,1:T(8,128)S(1)} %copy-done.6), channel_id=1, source_target_pairs={{0,16},{8,24},{16,0},{24,8},{1,17},{9,25},{17,1},{25,9},{2,18},{10... | collective-permute-start | bytes 12296 | tf_op jit(solution)/shard_map/ppermute | solution.py:400
  120.9 31.9 %collective-permute-start.5 = (s32[64]{0:T(128)S(1)}, s32[64]{0:T(128)S(1)}, u32[]{:S(2)}, u32[]{:S(2)}) collective-permute-start(s32[64]{0:T(128)S(1)} %copy-done.9), channel_id=1, source_target_pairs={{0,16},{8,24},{16,0},{24,8},{1,17},{9,25},{17,1},{25,9},{2,18},{10... | collective-permute-start | bytes 776 | tf_op jit(solution)/shard_map/ppermute | solution.py:400
  188.4 2.6 copy-start.3
  190.8 7.9 %copy-start.8 = (f32[8]{0:T(128)}, f32[8]{0:T(128)S(1)}, u32[]{:S(2)}) copy-start(f32[8]{0:T(128)S(1)} %fusion.16) | copy-start | bytes 100
  191.6 5.0 %collective-permute-start.3 = (bf16[128,512]{1,0:T(8,128)(2,1)S(1)}, bf16[128,512]{1,0:T(8,128)(2,1)S(1)}, u32[]{:S(2)}, u32[]{:S(2)}) collective-permute-start(bf16[128,512]{1,0:T(8,128)(2,1)S(1)} %pad_maximum_fusion), channel_id=1, source_target_pairs={{0,16},{8,24},{16,0},{24,8},{1,17},{9,25},{17,1},{25,9},{2,18},{10... | collective-permute-start | bytes 393224 | tf_op jit(solution)/shard_map/ppermute | solution.py:400
  197.4 144.0 %reduce-scatter.5.cloned.1.call-start = ((), (), s32[]{:S(2)}) async-start(), calls=%async_computation.3 | async-start | bytes 589824 | tf_op jit(solution)/shard_map/reduce_scatter | solution.py:454
  243.8 36.2 %collective-permute-start = (bf16[256,1024]{1,0:T(8,128)(2,1)S(1)}, bf16[256,1024]{1,0:T(8,128)(2,1)S(1)}, u32[]{:S(2)}, u32[]{:S(2)}) collective-permute-start(bf16[256,1024]{1,0:T(8,128)(2,1)S(1)} %bitcast.52), channel_id=1, source_target_pairs={{0,8},{8,16},{16,24},{24,0},{1,9},{9,17},{17,25},{25,1},{2,10},{10... | collective-permute-start | bytes 1572872 | tf_op jit(solution)/shard_map/ppermute | solution.py:439
  243.9 36.1 %collective-permute-start.1 = (bf16[256,1024]{1,0:T(8,128)(2,1)S(1)}, bf16[256,1024]{1,0:T(8,128)(2,1)S(1)}, u32[]{:S(2)}, u32[]{:S(2)}) collective-permute-start(bf16[256,1024]{1,0:T(8,128)(2,1)S(1)} %bitcast.51), channel_id=1, source_target_pairs={{0,16},{8,24},{16,0},{24,8},{1,17},{9,25},{17,1},{25,9},{2,18},{10... | collective-permute-start | bytes 1572872 | tf_op jit(solution)/shard_map/ppermute | solution.py:439
  245.4 34.6 %collective-permute-start.2 = (bf16[256,1024]{1,0:T(8,128)(2,1)S(1)}, bf16[256,1024]{1,0:T(8,128)(2,1)S(1)}, u32[]{:S(2)}, u32[]{:S(2)}) collective-permute-start(bf16[256,1024]{1,0:T(8,128)(2,1)S(1)} %bitcast.50), channel_id=1, source_target_pairs={{0,24},{8,0},{16,8},{24,16},{1,25},{9,1},{17,9},{25,17},{2,26},{10... | collective-permute-start | bytes 1572872 | tf_op jit(solution)/shard_map/ppermute | solution.py:439
  304.2 68.6 %collective-permute-start.7 = (bf16[7168,256]{1,0:T(8,128)(2,1)}, bf16[7168,256]{1,0:T(8,128)(2,1)}, u32[]{:S(2)}, u32[]{:S(2)}) collective-permute-start(bf16[7168,256]{1,0:T(8,128)(2,1)} %get-tuple-element.26), channel_id=1, source_target_pairs={{0,8},{8,0},{16,24},{24,16},{1,9},{9,1},{17,25},{25,17},{2,10},{10... | collective-permute-start | bytes 11010056 | tf_op jit(solution)/shard_map/ppermute | solution.py:474
  341.3 20.0 %copy-start.2 = (bf16[2176,512]{1,0:T(8,128)(2,1)S(1)}, bf16[2176,512]{1,0:T(8,128)(2,1)}, u32[]{:S(2)}) copy-start(bf16[2176,512]{1,0:T(8,128)(2,1)} %all-gather.4.cloned.1.call-done) | copy-start | bytes 6684676
  361.3 17.1 %collective-permute-start.6 = (bf16[5332,256]{1,0:T(8,128)(2,1)}, bf16[5332,256]{1,0:T(8,128)(2,1)}, u32[]{:S(2)}, u32[]{:S(2)}) collective-permute-start(bf16[5332,256]{1,0:T(8,128)(2,1)} %get-tuple-element.23), channel_id=1, source_target_pairs={{0,8},{8,0},{16,24},{24,16},{1,9},{9,1},{17,25},{25,17},{2,10},{10... | collective-permute-start | bytes 8189960 | tf_op jit(solution)/shard_map/ppermute | solution.py:474
  361.9 2.7 copy-start.4
  362.4 9.2 %collective-permute-start.10 = (f32[16,128]{1,0:T(8,128)S(1)}, f32[16,128]{1,0:T(8,128)S(1)}, u32[]{:S(2)}, u32[]{:S(2)}) collective-permute-start(f32[16,128]{1,0:T(8,128)S(1)} %reshape.108), channel_id=1, source_target_pairs={{0,24},{8,0},{16,8},{24,16},{1,25},{9,1},{17,9},{25,17},{2,26},{10... | collective-permute-start | bytes 24584 | tf_op jit(solution)/shard_map/ppermute | solution.py:439
  364.0 7.6 %collective-permute-start.8 = (f32[16,128]{1,0:T(8,128)S(1)}, f32[16,128]{1,0:T(8,128)S(1)}, u32[]{:S(2)}, u32[]{:S(2)}) collective-permute-start(f32[16,128]{1,0:T(8,128)S(1)} %reshape.108), channel_id=1, source_target_pairs={{0,8},{8,16},{16,24},{24,0},{1,9},{9,17},{17,25},{25,1},{2,10},{10... | collective-permute-start | bytes 24584 | tf_op jit(solution)/shard_map/ppermute | solution.py:439
  364.0 7.6 %collective-permute-start.9 = (f32[16,128]{1,0:T(8,128)S(1)}, f32[16,128]{1,0:T(8,128)S(1)}, u32[]{:S(2)}, u32[]{:S(2)}) collective-permute-start(f32[16,128]{1,0:T(8,128)S(1)} %reshape.108), channel_id=1, source_target_pairs={{0,16},{8,24},{16,0},{24,8},{1,17},{9,25},{17,1},{25,9},{2,18},{10... | collective-permute-start | bytes 24584 | tf_op jit(solution)/shard_map/ppermute | solution.py:439
  378.4 5.2 %copy-start.1 = (bf16[1024,1024]{1,0:T(8,128)(2,1)S(1)}, bf16[1024,1024]{1,0:T(8,128)(2,1)}, u32[]{:S(2)}) copy-start(bf16[1024,1024]{1,0:T(8,128)(2,1)} %param.12) | copy-start | bytes 6291460
Sparse Core Ops, SparseCore 0:
  117.9 70.4 reduce-scatter.2
  197.5 49.6 all-gather.3
  281.4 59.9 reduce-scatter.4

commit v3 on v2

--- a/solution.py
+++ b/solution.py
@@ -39,10 +39,10 @@
 
 
 def turn_wave(index):
-    y = jnp.abs(index.astype(jnp.float32) + (0.5 - 4194304.0)) - 2097152.0
+    y = 2097152.0 - jnp.abs(index.astype(jnp.float32) + (0.5 - 4194304.0))
     s = (y * y) * 2.0**-42
     m = ((s + B2) * s + B1) * s + B0
-    return y, -m
+    return y, m
 
 
 def tile_lanes(a, width):
@@ -82,9 +82,9 @@
 
 
 def forward_kernel(
-    valid, base_ref, pert_ref, point_ref, coef_ref, w_prev, w_now,
-    z_ref, pre_ref, sums_ref, held_a, held_b, acc, keys, xs, sq_ref, src_ref,
+    valid, base_ref, pert_ref, point_ref, coef_ref, w_prev, w_now, z_ref, *refs,
 ):
+    near_ref, far_ref, held_a, held_b, acc, keys, xs, sq_ref, src_ref, sums = refs
     step, last = pl.program_id(0), pl.num_programs(0) - 1
     rows, width = z_ref.shape
     points = point_ref.shape[0]
@@ -163,15 +163,50 @@
     def _():
         for part in range(parts):
             multiply(groups - 1, part, held_b, w_now, step)
-        pre_ref[...] = acc[...].astype(pre_ref.dtype)
-        sums_ref[...] = jnp.zeros_like(sums_ref)
+        sums[...] = jnp.zeros_like(sums)
+        source = jnp.sum(src_ref[...].T, axis=0, keepdims=True) / math.sqrt(D)
         for block in range(rows // LANES):
             square = jnp.sum(sq_ref[block * LANES:(block + 1) * LANES].T, axis=0, keepdims=True)
-            sums_ref[block:block + 1] = square / NOISE_SCALE**2
-        sums_ref[8:9, :points] = jnp.sum(src_ref[...].T, axis=0, keepdims=True) / math.sqrt(D)
-
-
-def redraw_kernel(first, base_ref, pert_ref, point_ref, _, z_ref, mark_ref, keys, xs):
+            for at, left in ((0, square / NOISE_SCALE**2), (LANES, source)):
+                sums[block * 16:block * 16 + 3, at:at + left.shape[1]] = three_terms(left)
+        per = near_ref.shape[1] - 16
+        outer = near_ref.shape[0]
+        for other, ref in enumerate((near_ref, far_ref)):
+            for shift in range(outer):
+                to = lax.rem(lax.div(base_ref[1], 2) + shift, outer) * 2 + (base_ref[1] + other) % 2
+                ref[shift, :per] = acc[pl.ds(pl.multiple_of(to * per, per), per), :].astype(ref.dtype)
+                ref[shift, per:] = jnp.zeros((16, ref.shape[2]), ref.dtype)
+                block = lax.div(to * per, LANES)
+                ref[shift, per:, :2 * LANES] = sums[pl.ds(pl.multiple_of(block * 16, 16), 16), :].astype(ref.dtype)
+
+
+def three_terms(left):
+    terms = []
+    for _ in range(3):
+        terms.append(left.astype(jnp.bfloat16).astype(jnp.float32))
+        left = left - terms[-1]
+    return jnp.concatenate(terms, axis=0)
+
+
+def combine_kernel(near_ref, got_ref, _, *out_refs):
+    per = near_ref.shape[1] - 16
+    for shift, ref in enumerate(out_refs):
+        both = near_ref[shift].astype(jnp.float32) + got_ref[shift].astype(jnp.float32)
+        ref[:per] = both[:per].astype(ref.dtype)
+        terms = three_terms(jnp.sum(both[per:per + 3, :2 * LANES], axis=0, keepdims=True))
+        ref[per:] = jnp.zeros((16, ref.shape[1]), ref.dtype)
+        ref[per:, :2 * LANES] = jnp.concatenate([terms, jnp.zeros((13, 2 * LANES), jnp.float32)], axis=0).astype(ref.dtype)
+
+
+def stack_kernel(_, *refs):
+    *in_refs, out_ref, mark_ref = refs
+    mark_ref[...] = jnp.zeros_like(mark_ref)
+    for number, ref in enumerate(in_refs):
+        out_ref[number] = ref[...]
+
+
+def redraw_kernel(first, base_ref, pert_ref, point_ref, *refs):
+    z_ref, mark_ref, keys, xs = refs[-4:]
     step = pl.program_id(0) + first
     rows, width = z_ref.shape
     points = point_ref.shape[0]
@@ -195,21 +230,20 @@
                 z_ref[pl.ds(row, samples), a:b] = (x + noise).astype(jnp.bfloat16)
 
 
-def gradient_kernel(count, per, _, d_ref, *refs):
+def gradient_kernel(count, places, base_ref, _, *refs):
+    d_refs, refs = refs[:len(places)], refs[len(places):]
+    blocks = len(places)
     z_refs, (keep_ref, send_ref, left) = refs[:count], refs[count:]
-    blocks, _, hidden = d_ref.shape
-    half = hidden // 2
-    together = LANES // per
+    half = keep_ref.shape[1]
 
     @pl.when(pl.program_id(0) == 0)
     def _():
-        for source in range(count):
-            for block in range(0, blocks, together):
-                at = source * blocks * per + block * per
-                rows = jnp.concatenate(
-                    [d_ref[block + i, source * per:(source + 1) * per] for i in range(together)], axis=0
-                )
-                left[:, at:at + LANES] = rows.T
+        outer = blocks // 2
+        for (other, shift), ref in zip(places, d_refs):
+            block = lax.rem(lax.div(base_ref[1], 2) + outer - shift, outer) * 2 + (base_ref[1] + other) % 2
+            for source in range(count):
+                at = pl.multiple_of((source * blocks + block) * LANES, LANES)
+                left[:, pl.ds(at, LANES)] = ref[source * LANES:(source + 1) * LANES, :].T
 
     width = keep_ref.shape[0]
     stride = 256 if width % 256 == 0 else LANES
@@ -237,7 +271,7 @@
     return jnp.broadcast_to(shuffle_bits(seeds.reshape(-1))[:, None], (seeds.size, LANES))
 
 
-def forward(base, pert, point, coef, w, width):
+def forward(base, pert, point, coef, w, width, parts):
     valid, hidden = w.shape
     rows, points = pert.shape[0], point.shape[0]
     steps = -(-valid // width)
@@ -253,13 +287,10 @@
         ],
         out_specs=[
             pl.BlockSpec((rows, width), lambda s: (0, s)),
-            whole((rows, hidden)), whole((16, LANES)),
-        ],
+        ] + [whole((parts // 2, rows // parts + 16, hidden))] * 2,
         out_shape=[
             jax.ShapeDtypeStruct((rows, steps * width), jnp.bfloat16),
-            jax.ShapeDtypeStruct((rows, hidden), jnp.bfloat16),
-            jax.ShapeDtypeStruct((16, LANES), jnp.float32),
-        ],
+        ] + [jax.ShapeDtypeStruct((parts // 2, rows // parts + 16, hidden), jnp.bfloat16)] * 2,
         scratch_shapes=[
             pltpu.VMEM((GROUP, width), jnp.bfloat16),
             pltpu.VMEM((GROUP, width), jnp.bfloat16),
@@ -268,6 +299,7 @@
             pltpu.VMEM((points, width), jnp.float32),
             pltpu.VMEM((rows, LANES), jnp.float32),
             pltpu.VMEM((points, LANES), jnp.float32),
+            pltpu.VMEM((rows // LANES * 16, 2 * LANES), jnp.float32),
         ],
         compiler_params=params(),
         cost_estimate=pl.CostEstimate(
@@ -277,20 +309,21 @@
     )(base, pert, point, coef, w, w)
 
 
-def redraw(base, pert, point, after, width, first, count):
+def redraw(base, pert, point, after, before, width, first, count, start, total):
     rows, points = pert.shape[0], point.shape[0]
+    anywhere = pl.BlockSpec(memory_space=pl.ANY)
+    extra = [] if before is None else [before]
     return pl.pallas_call(
         functools.partial(redraw_kernel, first),
         grid=(count,),
-        in_specs=[
-            pl.BlockSpec(memory_space=pltpu.SMEM), whole(pert.shape), whole(point.shape),
-            pl.BlockSpec(memory_space=pl.ANY),
-        ],
-        out_specs=[pl.BlockSpec((rows, width), lambda s: (0, s)), whole((8, LANES))],
+        in_specs=[pl.BlockSpec(memory_space=pltpu.SMEM), whole(pert.shape), whole(point.shape), anywhere]
+        + [anywhere] * len(extra),
+        out_specs=[pl.BlockSpec((rows, width), lambda s: (0, s + first - start)), whole((8, LANES))],
         out_shape=[
-            jax.ShapeDtypeStruct((rows, count * width), jnp.bfloat16),
+            jax.ShapeDtypeStruct((rows, total * width), jnp.bfloat16),
             jax.ShapeDtypeStruct((8, LANES), jnp.float32),
         ],
+        input_output_aliases={4: 0} if extra else {},
         scratch_shapes=[pltpu.VMEM((16, width), jnp.int32), pltpu.VMEM((points, width), jnp.float32)],
         compiler_params=params(),
         cost_estimate=pl.CostEstimate(
@@ -298,19 +331,52 @@
             transcendentals=2 * rows * width * count,
         ),
         name="redraw",
-    )(base, pert, point, after)
-
-
-def gradient(after, cotangent, per, own, others, width, first, count, valid):
+    )(base, pert, point, after, *extra)
+
+
+def combine(near, got, after):
+    parts, rows, hidden = near.shape
+    return pl.pallas_call(
+        combine_kernel,
+        grid=(1,),
+        in_specs=[whole(near.shape)] * 2 + [pl.BlockSpec(memory_space=pl.ANY)],
+        out_specs=[whole((rows, hidden))] * parts,
+        out_shape=[jax.ShapeDtypeStruct((rows, hidden), jnp.bfloat16)] * parts,
+        compiler_params=params(),
+        cost_estimate=pl.CostEstimate(flops=parts * rows * hidden, bytes_accessed=6 * parts * rows * hidden, transcendentals=0),
+        name="combine",
+    )(near, got, after)
+
+
+def stack(after, *arrays):
+    shape = arrays[0].shape
+    return pl.pallas_call(
+        stack_kernel,
+        grid=(1,),
+        in_specs=[pl.BlockSpec(memory_space=pl.ANY)] + [whole(shape)] * len(arrays),
+        out_specs=[whole((len(arrays), *shape)), whole((8, LANES))],
+        out_shape=[
+            jax.ShapeDtypeStruct((len(arrays), *shape), arrays[0].dtype),
+            jax.ShapeDtypeStruct((8, LANES), jnp.float32),
+        ],
+        compiler_params=params(),
+        cost_estimate=pl.CostEstimate(flops=0, bytes_accessed=4 * len(arrays) * math.prod(shape), transcendentals=0),
+        name="stack",
+    )(after, *arrays)
+
+
+def gradient(base, after, cotangent, places, own, others, width, first, count, valid):
     if count % 2 == 0 and first % 2 == 0:
         width, first, count = 2 * width, first // 2, count // 2
     rows = own.shape[0]
-    half = cotangent.shape[2] // 2
+    half = cotangent[0].shape[1] // 2
     height = min(valid, (first + count) * width) - first * width
     return pl.pallas_call(
-        functools.partial(gradient_kernel, 1 + len(others), per),
+        functools.partial(gradient_kernel, 1 + len(others), places),
         grid=(count,),
-        in_specs=[pl.BlockSpec(memory_space=pl.ANY), whole(cotangent.shape), pl.BlockSpec((rows, width), lambda s: (0, s + first))]
+        in_specs=[pl.BlockSpec(memory_space=pltpu.SMEM), pl.BlockSpec(memory_space=pl.ANY)]
+        + [whole(part.shape) for part in cotangent]
+        + [pl.BlockSpec((rows, width), lambda s: (0, s + first))]
         + [pl.BlockSpec((rows, width), lambda s: (0, s)) for _ in others],
         out_specs=[pl.BlockSpec((width, half), lambda s: (s, 0))] * 2,
         out_shape=[jax.ShapeDtypeStruct((height, half), jnp.bfloat16)] * 2,
@@ -321,7 +387,7 @@
             bytes_accessed=2 * rows * (1 + len(others)) * width * count, transcendentals=0,
         ),
         name="gradient",
-    )(after, cotangent, own, *others)
+    )(base, after, *cotangent, own, *others)
 
 
 def join(keep, got, before, width, first, valid):
@@ -375,10 +441,6 @@
     return best * LANES
 
 
-def tie(first, second):
-    return lax.optimization_barrier((first, second))
-
-
 def shards(point_seed, pert_seed, source_coef, w1, b1, w2, w3):
     coord_count = lax.axis_size("coord")
     pts_count = lax.axis_size("pts")
@@ -393,7 +455,7 @@
     share = hidden // pts_count
     width = block_width(valid)
     steps = -(-valid // width)
-    base = (coord_index * valid).astype(jnp.int32).reshape(1)
+    base = jnp.stack([coord_index * valid, coord_index]).astype(jnp.int32)
 
     def shift(a, by):
         return jax.tree.map(
@@ -405,20 +467,42 @@
     other_seeds = [shift((pert_seed, point_seed), by) for by in range(1, chips)]
 
     pert, point = lanes_of(pert_seed), lanes_of(point_seed)
-    own, pre, sums = forward(base, pert, point, source_coef[None, :], w1.T, width)
+    own, near, far = forward(base, pert, point, source_coef[None, :], w1.T, width, coord_count)
     others_in = [(lanes_of(a), lanes_of(b)) for a, b in other_seeds]
-
-    sums = lax.all_gather(sums, "coord", axis=0)
-    pre_local = lax.psum_scatter(pre, "coord", scatter_dimension=0, tiled=True)
+    outer = coord_count // 2
+
+    def across(a):
+        return lax.ppermute(a, "coord", [(i, i ^ 1) for i in range(coord_count)])
+
+    def along(a, by):
+        return lax.ppermute(a, "coord", [(i, (i + 2 * by) % coord_count) for i in range(coord_count)])
 
     early = steps // 2 + (steps // 2) % 2
     cuts = [(0, early), (early, steps - early)]
-    drawn = [[redraw(base, a, b, pre, width, *cuts[0]) for a, b in others_in]]
-    (pre_local, sums), _ = tie((pre_local, sums), [mark for _, mark in drawn[0]])
-
-    sums = jnp.sum(sums, axis=0)
-    squares_local = lax.dynamic_slice_in_dim(sums[:8].reshape(-1), coord_index * rows_local, rows_local, 0)
-    source_local = lax.dynamic_slice_in_dim(sums[8], coord_index * points_local, points_local, 0)
+
+    def redraws(number, after):
+        first, count = cuts[number]
+        held = [None] * len(others_in)
+        for at, size in ((0, -(-count // 2)), (-(-count // 2), count // 2)):
+            made = [
+                redraw(base, a, b, after, z, width, first + at, size, first, count)
+                for (a, b), z in zip(others_in, held)
+            ]
+            held = [z for z, _ in made]
+            after = yield held, sum(mark for _, mark in made)
+
+    draws = redraws(0, near)
+    _, mark = next(draws)
+    parts = combine(near, across(far), mark)
+    drawn_first, mark = draws.send(parts[0])
+    total = parts[0].astype(jnp.float32)
+    for by in range(1, outer):
+        total += along(parts[by], by).astype(jnp.float32)
+    pre_local = total[:rows_local]
+    sums = jnp.sum(total[rows_local:rows_local + 3], axis=0)
+    squares_local = lax.dynamic_slice_in_dim(sums, coord_index * rows_local % LANES, rows_local, 0)
+    source_local = lax.dynamic_slice_in_dim(sums, LANES + coord_index * points_local, points_local, 0)
+    b1 = b1 + mark[0, 0]
     residual, grad_pre_one, grad_readout, hidden_one, grad_pre_two = hidden_pass(
         pre_local.astype(jnp.float32) + b1[None, :], squares_local, source_local, w2, w3, samples
     )
@@ -432,15 +516,29 @@
     readout_rows = grad_readout.astype(jnp.bfloat16).reshape(-1, 2 * share)
     readout_rows = jnp.pad(readout_rows, ((0, 16 - readout_rows.shape[0]), (0, 0)))
     mine = jnp.concatenate([sent[0]] + [shift(sent[by], by) for by in range(1, chips)] + [readout_rows], axis=0)
-    cotangent = lax.all_gather(mine, "coord", axis=0)
-    drawn.append([redraw(base, a, b, mine, width, *cuts[1]) for a, b in others_in])
+    draws = redraws(1, mine)
+    _, mark = next(draws)
+    if rows_local == LANES:
+        cotangent = [mine] + [along(mine, by) for by in range(1, outer)] + [across(mine)]
+        got, mark = stack(mark, *cotangent[1:outer])
+        got = across(got)
+        cotangent += [got[i] for i in range(outer - 1)]
+        places = [(other, shift) for other in range(2) for shift in range(outer)]
+        turn = base
+    else:
+        gathered = lax.all_gather(mine, "coord", axis=0)
+        cotangent = [gathered[i] for i in range(coord_count)]
+        turn = jnp.zeros_like(base)
+    drawn_second, _ = draws.send(mark)
+    drawn = [drawn_first, drawn_second]
 
     def rotate(a, by):
         return lax.ppermute(a, "pts", [(i, (i + by) % pts_count) for i in range(pts_count)])
 
     grad_second = lax.dot_general(
         grad_pre_two, hidden_one, (((0,), (0,)), ((), ())), preferred_element_type=jnp.float32
-    ).astype(jnp.bfloat16)
+    )
+    grad_second = (grad_second + mark[0, 0]).astype(jnp.bfloat16)
     quarter = hidden // coord_count // pts_count
     grad_second = grad_second.reshape(coord_count, pts_count, quarter, hidden)
 
@@ -450,13 +548,12 @@
     second = second_part(pts_index).astype(jnp.float32)
     for by in range(1, pts_count):
         second += rotate(second_part((pts_index + by) % pts_count), by).astype(jnp.float32)
-    second, _ = tie(second.astype(jnp.bfloat16), cotangent[0, :16])
-    scattered = lax.psum_scatter(second, "coord", scatter_dimension=0, tiled=True)
+    scattered = lax.psum_scatter(second.astype(jnp.bfloat16), "coord", scatter_dimension=0, tiled=True)
     second = lax.all_gather(scattered, "pts", axis=0, tiled=True).astype(jnp.float32)
 
-    wide = cotangent.astype(jnp.float32)
-    bias_half = jnp.sum(wide[:, :chips * rows_local], axis=(0, 1))
-    readout = jnp.sum(wide[:, chips * rows_local:chips * rows_local + pts_count // 2], axis=0).reshape(-1)
+    summed = sum(part.astype(jnp.float32) for part in cotangent)
+    bias_half = jnp.sum(summed[:chips * rows_local], axis=0)
+    readout = summed[chips * rows_local:chips * rows_local + pts_count // 2].reshape(-1)
     bias = jnp.zeros((hidden,), jnp.float32)
     for number, index in enumerate((pts_index, pts_index ^ 1)):
         bias = lax.dynamic_update_slice_in_dim(bias, bias_half[number * share:(number + 1) * share], index * share, 0)
@@ -467,10 +564,17 @@
         for v in vectors.reshape(2, hidden)
     )
 
+    if rows_local != LANES:
+        rows = jnp.stack(cotangent)[:, :chips * rows_local].reshape(coord_count, chips, rows_local, -1)
+        rows = rows.transpose(1, 0, 2, 3).reshape(chips, -1, LANES, 2 * share).transpose(1, 0, 2, 3)
+        rows = rows.reshape(-1, chips * LANES, 2 * share)
+        cotangent = [rows[i] for i in range(rows.shape[0])]
+        places = [(i % 2, -(i // 2) % (len(cotangent) // 2)) for i in range(len(cotangent))]
+
     out = None
     swap = [(i, i ^ 1) for i in range(pts_count)]
-    for (first, count), z, after in zip(cuts, drawn, (mine, scattered)):
-        keep, send = gradient(after, cotangent, rows_local, own, [a for a, _ in z], width, first, count, valid)
+    for (first, count), z, after in zip(cuts, drawn, (mine, mine)):
+        keep, send = gradient(turn, after, cotangent, places, own, z, width, first, count, valid)
         got = lax.ppermute(send, "pts", swap)
         wide = 2 * width if count % 2 == 0 and first % 2 == 0 else width
         out = join(keep, got, out, wide, first * width // wide, valid)

time: 390 us -> 394 us (1.010)
  blocking collectives: 37.9 us -> 5.98 us
  starting transfers between devices: 10.2 us -> 24 us
  waiting for transfers between devices: 76 us -> 86.9 us
  local copies, waits for them, and re-layouts: 7.74 us -> 14.1 us
    all_gather x1 -> x0, blocking collectives: 31.7 us -> none  [shards(): sums = lax.all_gather(sums, 'coord', axis=0)]
    ppermute x6, waiting for transfers between devices: 0.02 us -> 24 us  [rotate(): lax.ppermute(a, 'pts', [(i, (i + by) % pts_count) for i in range(pts_coun...]
    reduce_scatter x2 -> x1, waiting for transfers between devices: 72.6 us -> 56.6 us  [shards(): lax.psum_scatter(second.astype(jnp.bfloat16), 'coord', scatter_dimension=...]
    ppermute x0 -> x9, starting transfers between devices: none -> 13.6 us  [the longest x6 9.57 us: along(): lax.ppermute(a, 'coord', [(i, (i + 2 * by) % coord_count) for i in range(...]
    pallas_call x2 -> x4, Pallas kernels: 42.9 us -> 44.9 us  [the longest x2 40.1 us: gradient(): pl.pallas_call(functools.partial(gradient_kernel, 1 + len(others), places...]
    pallas_call x2 -> x4, Pallas kernels: 76.7 us -> 78.3 us  [redraw(): pl.pallas_call(functools.partial(redraw_kernel, first), grid=(count,), in...]
  transfers between devices with their start and end apart: 14 -> 21, of which waited for: 3 -> 9; matrix products, arithmetic and copies ran while one was open for 2% -> 5% of each run, Pallas kernels for 32% -> 53%
where the time goes in v3:
time: 394 us
  Pallas kernels  237 us (60%)
  waiting for transfers between devices  86.9 us (22%)
  starting transfers between devices  24 us (6%)
  between operations  14.5 us (4%)
  local copies, waits for them, and re-layouts  14.1 us (4%)
  other arithmetic  7.83 us (2%)
  blocking collectives  5.98 us (2%)
    pallas_call x1, Pallas kernels, forward(): pl.pallas_call(functools.partial(forward_kernel, valid), grid=(steps,), i...  104 us
    pallas_call x4, Pallas kernels, redraw(): pl.pallas_call(functools.partial(redraw_kernel, first), grid=(count,), in...  78.3 us
    reduce_scatter x1, waiting for transfers between devices, shards(): lax.psum_scatter(second.astype(jnp.bfloat16), 'coord', scatter_dimension=...  56.6 us
    pallas_call x2, Pallas kernels, gradient(): pl.pallas_call(functools.partial(gradient_kernel, 1 + len(others), places...  40.1 us
    ppermute x6, waiting for transfers between devices, rotate(): lax.ppermute(a, 'pts', [(i, (i + by) % pts_count) for i in range(pts_coun...  24 us
    pallas_call x2, Pallas kernels, join(): pl.pallas_call(join_kernel, grid=(count,), in_specs=specs, out_specs=pl.B...  10.7 us
    ppermute x6, starting transfers between devices, along(): lax.ppermute(a, 'coord', [(i, (i + 2 * by) % coord_count) for i in range(...  9.57 us
  transfers between devices with their start and end apart: 21, of which 9 were waited for; matrix products, arithmetic and copies ran while one was open for 5% of the time, Pallas kernels for 53%

profile of v3, /device:TPU:0, one launch (start us, length us, event | category | flops | bytes accessed | tf_op | source)
XLA Modules:
  0.0 393.8 jit_solution(14586172088539452141)
XLA Ops:
  7.2 3.0 collective-permute-start.1
  10.3 0.8 copy.15
  11.1 0.7 shift-right-logical_xor_fusion.3
  11.8 1.5 broadcast_in_dim.12.coef_ref
  13.3 0.7 pad_add_fusion.base_ref
  13.9 1.0 broadcast_in_dim.10.pert_ref
  14.9 0.7 broadcast_in_dim.11.point_ref
  15.6 103.6 %forward.1 = (bf16[1024,12544]{1,0:T(8,128)(2,1)}, bf16[4,144,1024]{2,1,0:T(8,128)(2,1)}, bf16[4,144,1024]{2,1,0:T(8,128)(2,1)}) custom-call(s32[2]{0:T(128)} %pad_add_fusion.base_ref, s32[1024,128]{1,0:T(8,128)} %broadcast_in_dim.10.pert_ref, s32[64,128]{1,0:T(8,128)} %broadcast_in_dim.11.point_ref, f32[1,12500]{1,0:T(1,128)} %broadcast_in_dim.12.coef_ref, ...), custom_call_target="tpu_custom_call" | custom-call | flops 51200000000 | bytes 51200000 | tf_op jit(solution)/shard_map/forward/pallas_call | solution.py:279
  119.2 2.0 collective-permute-start
  121.5 1.0 broadcast_in_dim.13.pert_ref
  122.5 0.7 broadcast_in_dim.14.point_ref
  123.1 22.0 %redraw.4 = (bf16[1024,7168]{1,0:T(8,128)(2,1)}, f32[8,128]{1,0:T(8,128)}) custom-call(s32[2]{0:T(128)} %pad_add_fusion.base_ref, s32[1024,128]{1,0:T(8,128)} %broadcast_in_dim.13.pert_ref, s32[64,128]{1,0:T(8,128)} %broadcast_in_dim.14.point_ref, bf16[4,144,1024]{2,1,0:T(8,128)(2,1)} %get-tuple-element.25.refs_0_.near_ref), custom_call_target="tpu_custom_call" | custom-call | flops 14680064000 | bytes 7340032 | tf_op jit(solution)/shard_map/redraw/pallas_call | solution.py:316
  145.1 1.7 collective-permute-done.got_ref
  146.8 1.1 copy-done.2
  147.9 2.7 combine.1
  150.6 1.8 collective-permute-start.3
  152.4 2.6 collective-permute-start.4
  155.0 1.4 collective-permute-start.5
  156.3 22.1 %redraw.5 = (bf16[1024,7168]{1,0:T(8,128)(2,1)}, f32[8,128]{1,0:T(8,128)}) custom-call(s32[2]{0:T(128)} %pad_add_fusion.base_ref, s32[1024,128]{1,0:T(8,128)} %broadcast_in_dim.13.pert_ref, s32[64,128]{1,0:T(8,128)} %broadcast_in_dim.14.point_ref, bf16[144,1024]{1,0:T(8,128)(2,1)} %get-tuple-element.28.refs_0_, ...), custom_call_target="tpu_custom_call", output_to_operand_aliasing={{0}: (4, {})} | custom-call | flops 14680064000 | bytes 7340032 | tf_op jit(solution)/shard_map/redraw/pallas_call | solution.py:316
  178.4 1.2 slice.37
  179.6 0.6 broadcast_add_fusion
  180.3 0.2 convert_add_fusion.1
  180.6 0.8 fusion
  181.4 0.2 fusion.3
  182.1 0.3 copy-done.16
  182.4 0.5 fusion.1
  183.0 1.6 collective-permute-start.6
  184.7 3.3 collective-permute-done.6
  188.1 0.8 fusion.14.refs_0_._
  188.8 0.7 collective-permute-start.7
  189.5 0.4 collective-permute-start.8
  189.9 2.8 collective-permute-start.9
  192.7 17.1 %redraw.6 = (bf16[1024,5376]{1,0:T(8,128)(2,1)}, f32[8,128]{1,0:T(8,128)}) custom-call(s32[2]{0:T(128)} %pad_add_fusion.base_ref, s32[1024,128]{1,0:T(8,128)} %broadcast_in_dim.13.pert_ref, s32[64,128]{1,0:T(8,128)} %broadcast_in_dim.14.point_ref, bf16[272,512]{1,0:T(8,128)(2,1)} %fusion.14.refs_0_._), custom_call_target="tpu_custom_call" | custom-call | flops 11010048000 | bytes 5505024 | tf_op jit(solution)/shard_map/redraw/pallas_call | solution.py:316
  209.9 1.5 collective-permute-start.10
  211.4 0.7 copy-done.3
  212.3 2.1 stack.27
  214.3 0.5 collective-permute-start.11
  214.8 17.1 %redraw.7 = (bf16[1024,5376]{1,0:T(8,128)(2,1)}, f32[8,128]{1,0:T(8,128)}) custom-call(s32[2]{0:T(128)} %pad_add_fusion.base_ref, s32[1024,128]{1,0:T(8,128)} %broadcast_in_dim.13.pert_ref, s32[64,128]{1,0:T(8,128)} %broadcast_in_dim.14.point_ref, f32[8,128]{1,0:T(8,128)} %get-tuple-element.37.refs_0_, ...), custom_call_target="tpu_custom_call", output_to_operand_aliasing={{0}: (4, {})} | custom-call | flops 11010048000 | bytes 5505024 | tf_op jit(solution)/shard_map/redraw/pallas_call | solution.py:316
  231.9 1.2 slice.41
  233.1 1.3 collective-permute-done.11
  234.4 0.9 slice_bitcast_fusion
  235.3 21.9 %gradient.3 = (bf16[7168,256]{1,0:T(8,128)(2,1)}, bf16[7168,256]{1,0:T(8,128)(2,1)}) custom-call(s32[2]{0:T(128)} %pad_add_fusion.base_ref, bf16[272,512]{1,0:T(8,128)(2,1)} %fusion.14.refs_0_._, bf16[272,512]{1,0:T(8,128)(2,1)} %fusion.14.refs_0_._, bf16[272,512]{1,0:T(8,128)(2,1)} %copy-done.3, bf16[272,512]{1,0:T(8,128)(2,1)} %copy-done.5, ...), custom_call_target="tpu_custom_call" | custom-call | flops 15032385536 | bytes 29360128 | tf_op jit(solution)/shard_map/gradient/pallas_call | solution.py:374
  257.2 18.2 %gradient.2 = (bf16[5332,256]{1,0:T(8,128)(2,1)}, bf16[5332,256]{1,0:T(8,128)(2,1)}) custom-call(s32[2]{0:T(128)} %pad_add_fusion.base_ref, bf16[272,512]{1,0:T(8,128)(2,1)} %fusion.14.refs_0_._, bf16[272,512]{1,0:T(8,128)(2,1)} %fusion.14.refs_0_._, bf16[272,512]{1,0:T(8,128)(2,1)} %copy-done.3, bf16[272,512]{1,0:T(8,128)(2,1)} %copy-done.5, ...), custom_call_target="tpu_custom_call" | custom-call | flops 11274289152 | bytes 22020096 | tf_op jit(solution)/shard_map/gradient/pallas_call | solution.py:374
  275.4 0.5 collective-permute-start.12
  275.9 1.5 add_convert_fusion
  277.4 1.2 constant_dynamic-slice_fusion.3
  278.6 1.5 collective-permute-start.15
  280.1 1.4 collective-permute-start.16
  281.6 10.9 %collective-permute-done.14 = bf16[256,1024]{1,0:T(8,128)(2,1)S(1)} collective-permute-done((bf16[256,1024]{1,0:T(8,128)(2,1)}, bf16[256,1024]{1,0:T(8,128)(2,1)S(1)}, u32[]{:S(2)}, u32[]{:S(2)}) %collective-permute-start.14) | collective-permute-done | bytes 524320 | tf_op jit(solution)/shard_map/ppermute | solution.py:536
  292.5 1.1 collective-permute-done.15
  293.6 9.8 %collective-permute-done.16 = bf16[256,1024]{1,0:T(8,128)(2,1)} collective-permute-done((bf16[256,1024]{1,0:T(8,128)(2,1)}, bf16[256,1024]{1,0:T(8,128)(2,1)}, u32[]{:S(2)}, u32[]{:S(2)}) %collective-permute-start.16) | collective-permute-done | bytes 524320 | tf_op jit(solution)/shard_map/ppermute | solution.py:536
  303.4 2.2 fusion.6
  305.7 1.2 convert_add_fusion.2
  307.1 0.9 collective-permute-start.17
  307.9 1.5 collective-permute-start.18
  309.4 0.9 collective-permute-done.17
  310.4 1.2 collective-permute-done.18
  311.6 0.6 dynamic_slice.47
  312.2 0.6 dynamic_slice.46
  312.8 56.6 %reduce-scatter.2.cloned.1.call-done = bf16[32,1024]{1,0:T(8,128)(2,1)} async-done(((bf16[256,1024]{1,0:T(8,128)(2,1)}), bf16[32,1024]{1,0:T(8,128)(2,1)}) %reduce-scatter.2.cloned.1.call-update) | async-done | bytes 65552 | tf_op jit(solution)/shard_map/reduce_scatter | solution.py:551
  369.4 6.0 %all_gather.3 = bf16[128,1024]{1,0:T(8,128)(2,1)S(1)} all-gather(bf16[32,1024]{1,0:T(8,128)(2,1)} %reduce-scatter.2.cloned.1.call-done), channel_id=1, replica_groups=mesh['pts'=4,'coord'=8] {'pts'}, dimensions={0}, use_global_device_ids=true | all-gather | bytes 327680 | tf_op jit(solution)/shard_map/all_gather | solution.py:552
  375.4 0.8 convert_element_type.110
  376.2 5.5 %join.2.refs_2_ = bf16[12500,256]{1,0:T(8,128)(2,1)} custom-call(bf16[7168,256]{1,0:T(8,128)(2,1)} %get-tuple-element.43.refs_0_, bf16[7168,256]{1,0:T(8,128)(2,1)} %collective-permute-done.13.refs_1_), custom_call_target="tpu_custom_call" | custom-call | flops 1835008 | bytes 11010048 | tf_op jit(solution)/shard_map/join/pallas_call | solution.py:400
  381.8 5.2 %join.3 = bf16[12500,256]{1,0:T(8,128)(2,1)} custom-call(bf16[5332,256]{1,0:T(8,128)(2,1)} %get-tuple-element.40.refs_0_, bf16[5332,256]{1,0:T(8,128)(2,1)} %collective-permute-done.12.refs_1_, bf16[12500,256]{1,0:T(8,128)(2,1)} %join.2.refs_2_), custom_call_target="tpu_custom_call", output_to_operand_aliasing={{}: (2, {})} | custom-call | flops 1364992 | bytes 8189952 | tf_op jit(solution)/shard_map/join/pallas_call | solution.py:400
  (81 shorter events, 1.7 us)
Async XLA Ops:
  7.2 173.4 %copy-start = (bf16[1024,1024]{1,0:T(8,128)(2,1)S(1)}, bf16[1024,1024]{1,0:T(8,128)(2,1)}, u32[]{:S(2)}) copy-start(bf16[1024,1024]{1,0:T(8,128)(2,1)} %param.12) | copy-start | bytes 6291460
  7.2 362.2 %reduce-scatter.2.cloned.1.call-start = ((), (), s32[]{:S(2)}) async-start(), calls=%async_computation.1 | async-start | bytes 589824 | tf_op jit(solution)/shard_map/reduce_scatter | solution.py:551
  7.2 114.1 %collective-permute-start.1 = (s32[64,16]{0,1:T(8,128)}, s32[64,16]{0,1:T(8,128)S(1)}, u32[]{:S(2)}, u32[]{:S(2)}) collective-permute-start(s32[64,16]{0,1:T(8,128)} %param.8), channel_id=1, source_target_pairs={{0,16},{8,24},{16,0},{24,8},{1,17},{9,25},{17,1},{25,9},{2,18},{10... | collective-permute-start | bytes 12296 | tf_op jit(solution)/shard_map/ppermute | solution.py:462
  10.2 111.0 %collective-permute-start.2 = (s32[64]{0:T(128)}, s32[64]{0:T(128)S(1)}, u32[]{:S(2)}, u32[]{:S(2)}) collective-permute-start(s32[64]{0:T(128)} %param.7), channel_id=1, source_target_pairs={{0,16},{8,24},{16,0},{24,8},{1,17},{9,25},{17,1},{25,9},{2,18},{10... | collective-permute-start | bytes 776 | tf_op jit(solution)/shard_map/ppermute | solution.py:462
  15.6 105.5 %copy-start.14 = (bf16[1024]{0:T(1024)(128)(2,1)S(1)}, bf16[1024]{0:T(1024)(128)(2,1)}, u32[]{:S(2)}) copy-start(bf16[1024]{0:T(1024)(128)(2,1)} %param.13) | copy-start | bytes 6148
  119.2 27.6 %collective-permute-start = (bf16[4,144,1024]{2,1,0:T(8,128)(2,1)}, bf16[4,144,1024]{2,1,0:T(8,128)(2,1)S(1)}, u32[]{:S(2)}, u32[]{:S(2)}) collective-permute-start(bf16[4,144,1024]{2,1,0:T(8,128)(2,1)} %get-tuple-element.26), channel_id=1, source_target_pairs={{0,1},{1,0},{2,3},{3,2},{4,5},{5,4},{6,7},{7,6},{8,9},{9,8},{10,11... | collective-permute-start | bytes 3538952 | tf_op jit(solution)/shard_map/ppermute | solution.py:475
  146.8 1.1 copy-start.2
  150.6 29.6 %collective-permute-start.3 = (bf16[144,1024]{1,0:T(8,128)(2,1)}, bf16[144,1024]{1,0:T(8,128)(2,1)S(1)}, u32[]{:S(2)}, u32[]{:S(2)}) collective-permute-start(bf16[144,1024]{1,0:T(8,128)(2,1)} %get-tuple-element.29), channel_id=1, source_target_pairs={{0,2},{1,3},{2,4},{3,5},{4,6},{5,7},{6,0},{7,1},{8,10},{9,11},{10,... | collective-permute-start | bytes 884744 | tf_op jit(solution)/shard_map/ppermute | solution.py:478
  152.4 27.9 %collective-permute-start.4 = (bf16[144,1024]{1,0:T(8,128)(2,1)}, bf16[144,1024]{1,0:T(8,128)(2,1)S(1)}, u32[]{:S(2)}, u32[]{:S(2)}) collective-permute-start(bf16[144,1024]{1,0:T(8,128)(2,1)} %get-tuple-element.30), channel_id=1, source_target_pairs={{0,4},{1,5},{2,6},{3,7},{4,0},{5,1},{6,2},{7,3},{8,12},{9,13},{10,... | collective-permute-start | bytes 884744 | tf_op jit(solution)/shard_map/ppermute | solution.py:478
  155.0 25.3 %collective-permute-start.5 = (bf16[144,1024]{1,0:T(8,128)(2,1)}, bf16[144,1024]{1,0:T(8,128)(2,1)S(1)}, u32[]{:S(2)}, u32[]{:S(2)}) collective-permute-start(bf16[144,1024]{1,0:T(8,128)(2,1)} %get-tuple-element.31), channel_id=1, source_target_pairs={{0,6},{1,7},{2,0},{3,1},{4,2},{5,3},{6,4},{7,5},{8,14},{9,15},{10,... | collective-permute-start | bytes 884744 | tf_op jit(solution)/shard_map/ppermute | solution.py:478
  156.3 23.3 %copy-start.15 = (f32[1024]{0:T(1024)S(1)}, f32[1024]{0:T(1024)}, u32[]{:S(2)}) copy-start(f32[1024]{0:T(1024)} %param.11) | copy-start | bytes 12292
  156.3 23.9 %copy-start.11 = (bf16[144,1024]{1,0:T(8,128)(2,1)S(1)}, bf16[144,1024]{1,0:T(8,128)(2,1)}, u32[]{:S(2)}) copy-start(bf16[144,1024]{1,0:T(8,128)(2,1)} %get-tuple-element.28.refs_0_) | copy-start | bytes 884740
  181.9 0.5 copy-start.16
  183.0 5.0 %collective-permute-start.6 = (bf16[128,512]{1,0:T(8,128)(2,1)S(1)}, bf16[128,512]{1,0:T(8,128)(2,1)S(1)}, u32[]{:S(2)}, u32[]{:S(2)}) collective-permute-start(bf16[128,512]{1,0:T(8,128)(2,1)S(1)} %pad_maximum_fusion), channel_id=1, source_target_pairs={{0,16},{8,24},{16,0},{24,8},{1,17},{9,25},{17,1},{25,9},{2,18},{10... | collective-permute-start | bytes 393224 | tf_op jit(solution)/shard_map/ppermute | solution.py:462
  184.7 4.8 %copy-start.12 = (bf16[2,512]{1,0:T(2,128)(2,1)}, bf16[2,512]{1,0:T(2,128)(2,1)S(1)}, u32[]{:S(2)}) copy-start(bf16[2,512]{1,0:T(2,128)(2,1)S(1)} %convert_element_type.102) | copy-start | bytes 6148
  188.1 1.5 copy-start.9
  188.8 22.5 %collective-permute-start.7 = (bf16[272,512]{1,0:T(8,128)(2,1)}, bf16[272,512]{1,0:T(8,128)(2,1)S(1)}, u32[]{:S(2)}, u32[]{:S(2)}) collective-permute-start(bf16[272,512]{1,0:T(8,128)(2,1)} %fusion.14.refs_0_._), channel_id=1, source_target_pairs={{0,2},{1,3},{2,4},{3,5},{4,6},{5,7},{6,0},{7,1},{8,10},{9,11},{10,... | collective-permute-start | bytes 835592 | tf_op jit(solution)/shard_map/ppermute | solution.py:478
  189.5 21.9 %collective-permute-start.8 = (bf16[272,512]{1,0:T(8,128)(2,1)}, bf16[272,512]{1,0:T(8,128)(2,1)S(1)}, u32[]{:S(2)}, u32[]{:S(2)}) collective-permute-start(bf16[272,512]{1,0:T(8,128)(2,1)} %fusion.14.refs_0_._), channel_id=1, source_target_pairs={{0,4},{1,5},{2,6},{3,7},{4,0},{5,1},{6,2},{7,3},{8,12},{9,13},{10,... | collective-permute-start | bytes 835592 | tf_op jit(solution)/shard_map/ppermute | solution.py:478
  189.9 21.5 %collective-permute-start.9 = (bf16[272,512]{1,0:T(8,128)(2,1)}, bf16[272,512]{1,0:T(8,128)(2,1)S(1)}, u32[]{:S(2)}, u32[]{:S(2)}) collective-permute-start(bf16[272,512]{1,0:T(8,128)(2,1)} %fusion.14.refs_0_._), channel_id=1, source_target_pairs={{0,6},{1,7},{2,0},{3,1},{4,2},{5,3},{6,4},{7,5},{8,14},{9,15},{10,... | collective-permute-start | bytes 835592 | tf_op jit(solution)/shard_map/ppermute | solution.py:478
  209.9 25.4 %collective-permute-start.10 = (bf16[272,512]{1,0:T(8,128)(2,1)}, bf16[272,512]{1,0:T(8,128)(2,1)}, u32[]{:S(2)}, u32[]{:S(2)}) collective-permute-start(bf16[272,512]{1,0:T(8,128)(2,1)} %fusion.14.refs_0_._), channel_id=1, source_target_pairs={{0,1},{1,0},{2,3},{3,2},{4,5},{5,4},{6,7},{7,6},{8,9},{9,8},{10,11... | collective-permute-start | bytes 835592 | tf_op jit(solution)/shard_map/ppermute | solution.py:475
  211.4 0.7 copy-start.3
  211.4 0.8 copy-start.5
  211.4 0.8 copy-start.7
  214.3 20.0 %collective-permute-start.11 = (bf16[3,272,512]{2,1,0:T(8,128)(2,1)}, bf16[3,272,512]{2,1,0:T(8,128)(2,1)S(1)}, u32[]{:S(2)}, u32[]{:S(2)}) collective-permute-start(bf16[3,272,512]{2,1,0:T(8,128)(2,1)} %get-tuple-element.35), channel_id=1, source_target_pairs={{0,1},{1,0},{2,3},{3,2},{4,5},{5,4},{6,7},{7,6},{8,9},{9,8},{10,11... | collective-permute-start | bytes 2506760 | tf_op jit(solution)/shard_map/ppermute | solution.py:475
  257.2 119.0 %collective-permute-start.13 = (bf16[7168,256]{1,0:T(8,128)(2,1)}, bf16[7168,256]{1,0:T(8,128)(2,1)}, u32[]{:S(2)}, u32[]{:S(2)}) collective-permute-start(bf16[7168,256]{1,0:T(8,128)(2,1)} %get-tuple-element.44), channel_id=1, source_target_pairs={{0,8},{8,0},{16,24},{24,16},{1,9},{9,1},{17,25},{25,17},{2,10},{10... | collective-permute-start | bytes 11010056 | tf_op jit(solution)/shard_map/ppermute | solution.py:578
  275.4 106.3 %collective-permute-start.12 = (bf16[5332,256]{1,0:T(8,128)(2,1)}, bf16[5332,256]{1,0:T(8,128)(2,1)}, u32[]{:S(2)}, u32[]{:S(2)}) collective-permute-start(bf16[5332,256]{1,0:T(8,128)(2,1)} %get-tuple-element.41), channel_id=1, source_target_pairs={{0,8},{8,0},{16,24},{24,16},{1,9},{9,1},{17,25},{25,17},{2,10},{10... | collective-permute-start | bytes 8189960 | tf_op jit(solution)/shard_map/ppermute | solution.py:578
  277.3 28.3 %copy-start.4 = (bf16[272,512]{1,0:T(8,128)(2,1)S(1)}, bf16[272,512]{1,0:T(8,128)(2,1)}, u32[]{:S(2)}) copy-start(bf16[272,512]{1,0:T(8,128)(2,1)} %copy-done.3) | copy-start | bytes 835588
  277.4 28.3 %copy-start.6 = (bf16[272,512]{1,0:T(8,128)(2,1)S(1)}, bf16[272,512]{1,0:T(8,128)(2,1)}, u32[]{:S(2)}) copy-start(bf16[272,512]{1,0:T(8,128)(2,1)} %copy-done.5) | copy-start | bytes 835588
  277.4 28.3 %copy-start.8 = (bf16[272,512]{1,0:T(8,128)(2,1)S(1)}, bf16[272,512]{1,0:T(8,128)(2,1)}, u32[]{:S(2)}) copy-start(bf16[272,512]{1,0:T(8,128)(2,1)} %copy-done.7) | copy-start | bytes 835588
  277.4 28.3 %copy-start.10 = (bf16[128,512]{1,0:T(8,128)(2,1)S(1)}, bf16[128,512]{1,0:T(8,128)(2,1)}, u32[]{:S(2)}) copy-start(bf16[128,512]{1,0:T(8,128)(2,1)} %copy-done.9) | copy-start | bytes 393220
  277.4 28.3 %copy-start.13 = (bf16[2,512]{1,0:T(2,128)(2,1)S(1)}, bf16[2,512]{1,0:T(2,128)(2,1)}, u32[]{:S(2)}) copy-start(bf16[2,512]{1,0:T(2,128)(2,1)} %copy-done.12) | copy-start | bytes 6148
  278.6 13.9 %collective-permute-start.14 = (bf16[256,1024]{1,0:T(8,128)(2,1)}, bf16[256,1024]{1,0:T(8,128)(2,1)S(1)}, u32[]{:S(2)}, u32[]{:S(2)}) collective-permute-start(bf16[256,1024]{1,0:T(8,128)(2,1)} %bitcast.12), channel_id=1, source_target_pairs={{0,8},{8,16},{16,24},{24,0},{1,9},{9,17},{17,25},{25,1},{2,10},{10... | collective-permute-start | bytes 1572872 | tf_op jit(solution)/shard_map/ppermute | solution.py:536
  278.6 15.0 %collective-permute-start.15 = (bf16[256,1024]{1,0:T(8,128)(2,1)}, bf16[256,1024]{1,0:T(8,128)(2,1)S(1)}, u32[]{:S(2)}, u32[]{:S(2)}) collective-permute-start(bf16[256,1024]{1,0:T(8,128)(2,1)} %bitcast.13), channel_id=1, source_target_pairs={{0,16},{8,24},{16,0},{24,8},{1,17},{9,25},{17,1},{25,9},{2,18},{10... | collective-permute-start | bytes 1572872 | tf_op jit(solution)/shard_map/ppermute | solution.py:536
  280.1 23.3 %collective-permute-start.16 = (bf16[256,1024]{1,0:T(8,128)(2,1)}, bf16[256,1024]{1,0:T(8,128)(2,1)}, u32[]{:S(2)}, u32[]{:S(2)}) collective-permute-start(bf16[256,1024]{1,0:T(8,128)(2,1)} %bitcast.14), channel_id=1, source_target_pairs={{0,24},{8,0},{16,8},{24,16},{1,25},{9,1},{17,9},{25,17},{2,26},{10... | collective-permute-start | bytes 1572872 | tf_op jit(solution)/shard_map/ppermute | solution.py:536
  307.1 3.3 collective-permute-start.17
  307.9 3.7 collective-permute-start.18
  309.4 2.2 collective-permute-start.19
  381.8 5.2 %copy-start.1 = (bf16[1024,1024]{1,0:T(8,128)(2,1)S(1)}, bf16[1024,1024]{1,0:T(8,128)(2,1)}, u32[]{:S(2)}) copy-start(bf16[1024,1024]{1,0:T(8,128)(2,1)} %param.12) | copy-start | bytes 6291460
Sparse Core Ops, SparseCore 0:
  305.7 63.5 reduce-scatter.1

commit v4 on v3

--- a/solution.py
+++ b/solution.py
@@ -22,7 +22,7 @@
 C0, C1, C2, C3 = 6.283164044286755, -2.583571398038591, 0.3177373780982648, -0.017332380925367475
 B0, B1, B2 = C0 / C3, C1 / C3, C2 / C3
 SINE_SCALE = -C3 * 2.0**-23
-LOG_SCALE = -2.0 * math.log(2.0) * (NOISE_SCALE * SINE_SCALE) ** 2
+LOG_SCALE = -2.0 * (NOISE_SCALE * SINE_SCALE) ** 2
 
 
 def shuffle_bits(bits):
@@ -43,6 +43,14 @@
     s = (y * y) * 2.0**-42
     m = ((s + B2) * s + B1) * s + B0
     return y, m
+
+
+def spread_seeds(seeds_ref, point_ref, pert, point):
+    samples, points = seeds_ref.shape
+    seeds = shuffle_bits(seeds_ref[...])
+    for number in range(points):
+        pert[number * samples:(number + 1) * samples] = jnp.broadcast_to(seeds[:, number:number + 1], (samples, LANES))
+    point[...] = jnp.broadcast_to(shuffle_bits(point_ref[...]), (LANES, points)).T
 
 
 def tile_lanes(a, width):
@@ -61,7 +69,7 @@
     first = mix_tail(seeds ^ jnp.concatenate([key_zero] * 2, axis=0))
     second = mix_tail(seeds ^ jnp.concatenate([key_one] * 2, axis=0))
     u0 = ((first & MASK).astype(jnp.float32) + 0.5) * 2.0**-23
-    n = jnp.log2(u0) * LOG_SCALE
+    n = jnp.log(u0) * LOG_SCALE
     y, m = turn_wave(second & MASK)
     return ((n * lax.rsqrt(n)) * y) * m
 
@@ -82,9 +90,9 @@
 
 
 def forward_kernel(
-    valid, base_ref, pert_ref, point_ref, coef_ref, w_prev, w_now, z_ref, *refs,
+    valid, base_ref, seeds_ref, spots_ref, coef_ref, w_prev, w_now, z_ref, *refs,
 ):
-    near_ref, far_ref, held_a, held_b, acc, keys, xs, sq_ref, src_ref, sums = refs
+    near_ref, far_ref, held_a, held_b, acc, keys, xs, sq_ref, src_ref, sums, pert_ref, point_ref = refs
     step, last = pl.program_id(0), pl.num_programs(0) - 1
     rows, width = z_ref.shape
     points = point_ref.shape[0]
@@ -99,6 +107,7 @@
         held_b[...] = jnp.zeros_like(held_b)
         sq_ref[...] = jnp.zeros_like(sq_ref)
         src_ref[...] = jnp.zeros_like(src_ref)
+        spread_seeds(seeds_ref, spots_ref, pert_ref, point_ref)
 
     columns, (key_zero, key_one, key_two) = column_keys(base_ref[0], step, width)
     keys[0:8] = key_zero
@@ -205,8 +214,13 @@
         out_ref[number] = ref[...]
 
 
-def redraw_kernel(first, base_ref, pert_ref, point_ref, *refs):
-    z_ref, mark_ref, keys, xs = refs[-4:]
+def redraw_kernel(first, base_ref, seeds_ref, spots_ref, *refs):
+    z_ref, mark_ref, keys, xs, pert_ref, point_ref = refs[-6:]
+
+    @pl.when(pl.program_id(0) == 0)
+    def _():
+        spread_seeds(seeds_ref, spots_ref, pert_ref, point_ref)
+
     step = pl.program_id(0) + first
     rows, width = z_ref.shape
     points = point_ref.shape[0]
@@ -230,7 +244,12 @@
                 z_ref[pl.ds(row, samples), a:b] = (x + noise).astype(jnp.bfloat16)
 
 
-def gradient_kernel(count, places, base_ref, _, *refs):
+def gradient_kernel(count, places, skip, joins, base_ref, *refs):
+    refs = refs[skip:]
+    if joins:
+        keep, got, *refs, out_ref, left = refs
+        out_ref[...] = (keep[...].astype(jnp.float32) + got[...].astype(jnp.float32)).astype(jnp.bfloat16)
+        refs = [*refs, left]
     d_refs, refs = refs[:len(places)], refs[len(places):]
     blocks = len(places)
     z_refs, (keep_ref, send_ref, left) = refs[:count], refs[count:]
@@ -246,12 +265,12 @@
                 left[:, pl.ds(at, LANES)] = ref[source * LANES:(source + 1) * LANES, :].T
 
     width = keep_ref.shape[0]
-    stride = 256 if width % 256 == 0 else LANES
-    for a in range(0, width, stride):
-        z = jnp.concatenate([ref[:, a:a + stride] for ref in z_refs], axis=0)
+    for a in range(0, width, 1024):
+        b = min(a + 1024, width)
+        z = jnp.concatenate([ref[:, a:b] for ref in z_refs], axis=0)
         part = jnp.dot(left[...], z, preferred_element_type=jnp.float32).astype(jnp.bfloat16).T
-        keep_ref[a:a + stride, :] = part[:, :half]
-        send_ref[a:a + stride, :] = part[:, half:]
+        keep_ref[a:b, :] = part[:, :half]
+        send_ref[a:b, :] = part[:, half:]
 
 
 def join_kernel(*refs):
@@ -267,13 +286,9 @@
     return pl.BlockSpec(shape, lambda s: (0,) * len(shape))
 
 
-def lanes_of(seeds):
-    return jnp.broadcast_to(shuffle_bits(seeds.reshape(-1))[:, None], (seeds.size, LANES))
-
-
 def forward(base, pert, point, coef, w, width, parts):
     valid, hidden = w.shape
-    rows, points = pert.shape[0], point.shape[0]
+    rows, points = pert.size, point.size
     steps = -(-valid // width)
     smem = pl.BlockSpec(memory_space=pltpu.SMEM)
     return pl.pallas_call(
@@ -300,6 +315,8 @@
             pltpu.VMEM((rows, LANES), jnp.float32),
             pltpu.VMEM((points, LANES), jnp.float32),
             pltpu.VMEM((rows // LANES * 16, 2 * LANES), jnp.float32),
+            pltpu.VMEM((rows, LANES), jnp.int32),
+            pltpu.VMEM((points, LANES), jnp.int32),
         ],
         compiler_params=params(),
         cost_estimate=pl.CostEstimate(
@@ -310,28 +327,31 @@
 
 
 def redraw(base, pert, point, after, before, width, first, count, start, total):
-    rows, points = pert.shape[0], point.shape[0]
+    rows, points = pert.size, point.size
     anywhere = pl.BlockSpec(memory_space=pl.ANY)
     extra = [] if before is None else [before]
     return pl.pallas_call(
         functools.partial(redraw_kernel, first),
         grid=(count,),
-        in_specs=[pl.BlockSpec(memory_space=pltpu.SMEM), whole(pert.shape), whole(point.shape), anywhere]
-        + [anywhere] * len(extra),
+        in_specs=[pl.BlockSpec(memory_space=pltpu.SMEM), whole(pert.shape), whole(point.shape)]
+        + [anywhere] * (len(after) + len(extra)),
         out_specs=[pl.BlockSpec((rows, width), lambda s: (0, s + first - start)), whole((8, LANES))],
         out_shape=[
             jax.ShapeDtypeStruct((rows, total * width), jnp.bfloat16),
             jax.ShapeDtypeStruct((8, LANES), jnp.float32),
         ],
-        input_output_aliases={4: 0} if extra else {},
-        scratch_shapes=[pltpu.VMEM((16, width), jnp.int32), pltpu.VMEM((points, width), jnp.float32)],
+        input_output_aliases={3 + len(after): 0} if extra else {},
+        scratch_shapes=[
+            pltpu.VMEM((16, width), jnp.int32), pltpu.VMEM((points, width), jnp.float32),
+            pltpu.VMEM((rows, LANES), jnp.int32), pltpu.VMEM((points, LANES), jnp.int32),
+        ],
         compiler_params=params(),
         cost_estimate=pl.CostEstimate(
             flops=100 * rows * width * count * 40, bytes_accessed=2 * rows * width * count,
             transcendentals=2 * rows * width * count,
         ),
         name="redraw",
-    )(base, pert, point, after, *extra)
+    )(base, pert, point, *after, *extra)
 
 
 def combine(near, got, after):
@@ -365,21 +385,29 @@
     )(after, *arrays)
 
 
-def gradient(base, after, cotangent, places, own, others, width, first, count, valid):
-    if count % 2 == 0 and first % 2 == 0:
-        width, first, count = 2 * width, first // 2, count // 2
+def gradient(base, after, cotangent, places, own, others, width, first, count, start, valid, joined=None):
+    if all(n % 2 == 0 for n in (count, first, start)):
+        width, first, count, start = 2 * width, first // 2, count // 2, start // 2
     rows = own.shape[0]
     half = cotangent[0].shape[1] // 2
     height = min(valid, (first + count) * width) - first * width
+    out_specs = [pl.BlockSpec((width, half), lambda s: (s, 0))] * 2
+    out_shape = [jax.ShapeDtypeStruct((height, half), jnp.bfloat16)] * 2
+    joins, spec = [], None
+    if joined is not None:
+        joins = list(joined)
+        spec = pl.BlockSpec((joins[0].shape[0] // count, half), lambda s: (s, 0))
+        out_specs, out_shape = out_specs + [spec], out_shape + [jax.ShapeDtypeStruct((valid, half), jnp.bfloat16)]
     return pl.pallas_call(
-        functools.partial(gradient_kernel, 1 + len(others), places),
+        functools.partial(gradient_kernel, 1 + len(others), places, len(after), len(joins) > 0),
         grid=(count,),
-        in_specs=[pl.BlockSpec(memory_space=pltpu.SMEM), pl.BlockSpec(memory_space=pl.ANY)]
+        in_specs=[pl.BlockSpec(memory_space=pltpu.SMEM)] + [pl.BlockSpec(memory_space=pl.ANY)] * len(after)
+        + [spec] * len(joins)
         + [whole(part.shape) for part in cotangent]
         + [pl.BlockSpec((rows, width), lambda s: (0, s + first))]
-        + [pl.BlockSpec((rows, width), lambda s: (0, s)) for _ in others],
-        out_specs=[pl.BlockSpec((width, half), lambda s: (s, 0))] * 2,
-        out_shape=[jax.ShapeDtypeStruct((height, half), jnp.bfloat16)] * 2,
+        + [pl.BlockSpec((rows, width), lambda s: (0, s + first - start)) for _ in others],
+        out_specs=out_specs,
+        out_shape=out_shape,
         scratch_shapes=[pltpu.VMEM((2 * half, (1 + len(others)) * rows), jnp.bfloat16)],
         compiler_params=params(),
         cost_estimate=pl.CostEstimate(
@@ -387,16 +415,17 @@
             bytes_accessed=2 * rows * (1 + len(others)) * width * count, transcendentals=0,
         ),
         name="gradient",
-    )(base, after, *cotangent, own, *others)
-
-
-def join(keep, got, before, width, first, valid):
+    )(base, *after, *joins, *cotangent, own, *others)
+
+
+def join(after, keep, got, before, width, first, valid):
     height, half = keep.shape
     count = -(-height // width)
-    specs = [pl.BlockSpec((width, half), lambda s: (s, 0))] * 2
-    operands, aliases = [keep, got], {}
+    anywhere = pl.BlockSpec(memory_space=pl.ANY)
+    specs = [pl.BlockSpec((width, half), lambda s: (s, 0))] * 2 + [anywhere] * len(after)
+    operands, aliases = [keep, got, *after], {}
     if before is not None:
-        specs, operands, aliases = specs + [pl.BlockSpec(memory_space=pl.ANY)], operands + [before], {2: 0}
+        specs, operands, aliases = specs + [anywhere], operands + [before], {len(operands): 0}
     return pl.pallas_call(
         join_kernel,
         grid=(count,),
@@ -466,9 +495,9 @@
 
     other_seeds = [shift((pert_seed, point_seed), by) for by in range(1, chips)]
 
-    pert, point = lanes_of(pert_seed), lanes_of(point_seed)
+    pert, point = pert_seed.T, point_seed[None, :]
     own, near, far = forward(base, pert, point, source_coef[None, :], w1.T, width, coord_count)
-    others_in = [(lanes_of(a), lanes_of(b)) for a, b in other_seeds]
+    others_in = [(a.T, b[None, :]) for a, b in other_seeds]
     outer = coord_count // 2
 
     def across(a):
@@ -491,10 +520,10 @@
             held = [z for z, _ in made]
             after = yield held, sum(mark for _, mark in made)
 
-    draws = redraws(0, near)
+    draws = redraws(0, [near])
     _, mark = next(draws)
     parts = combine(near, across(far), mark)
-    drawn_first, mark = draws.send(parts[0])
+    drawn_first, mark = draws.send([parts[0]])
     total = parts[0].astype(jnp.float32)
     for by in range(1, outer):
         total += along(parts[by], by).astype(jnp.float32)
@@ -516,7 +545,7 @@
     readout_rows = grad_readout.astype(jnp.bfloat16).reshape(-1, 2 * share)
     readout_rows = jnp.pad(readout_rows, ((0, 16 - readout_rows.shape[0]), (0, 0)))
     mine = jnp.concatenate([sent[0]] + [shift(sent[by], by) for by in range(1, chips)] + [readout_rows], axis=0)
-    draws = redraws(1, mine)
+    draws = redraws(1, [mine])
     _, mark = next(draws)
     if rows_local == LANES:
         cotangent = [mine] + [along(mine, by) for by in range(1, outer)] + [across(mine)]
@@ -529,27 +558,30 @@
         gathered = lax.all_gather(mine, "coord", axis=0)
         cotangent = [gathered[i] for i in range(coord_count)]
         turn = jnp.zeros_like(base)
-    drawn_second, _ = draws.send(mark)
-    drawn = [drawn_first, drawn_second]
+    def add(kept, *received):
+        return sum((a.astype(jnp.float32) for a in received), kept.astype(jnp.float32)).astype(jnp.bfloat16)
+
+    def pick(a, index, axis):
+        return lax.dynamic_index_in_dim(a, index, axis, keepdims=False)
 
     def rotate(a, by):
         return lax.ppermute(a, "pts", [(i, (i + by) % pts_count) for i in range(pts_count)])
 
-    grad_second = lax.dot_general(
+    chip, core = pts_index // 2, pts_index % 2
+    place, parity = coord_index // 2, coord_index % 2
+    swap = [(i, i ^ 1) for i in range(pts_count)]
+    quarter = hidden // coord_count // pts_count
+    second = lax.dot_general(
         grad_pre_two, hidden_one, (((0,), (0,)), ((), ())), preferred_element_type=jnp.float32
-    )
-    grad_second = (grad_second + mark[0, 0]).astype(jnp.bfloat16)
-    quarter = hidden // coord_count // pts_count
-    grad_second = grad_second.reshape(coord_count, pts_count, quarter, hidden)
-
-    def second_part(index):
-        return lax.dynamic_slice_in_dim(grad_second, index, 1, 1).reshape(coord_count * quarter, hidden)
-
-    second = second_part(pts_index).astype(jnp.float32)
-    for by in range(1, pts_count):
-        second += rotate(second_part((pts_index + by) % pts_count), by).astype(jnp.float32)
-    scattered = lax.psum_scatter(second.astype(jnp.bfloat16), "coord", scatter_dimension=0, tiled=True)
-    second = lax.all_gather(scattered, "pts", axis=0, tiled=True).astype(jnp.float32)
+    ).astype(jnp.bfloat16).reshape(coord_count, chips, 2, quarter, hidden)
+    second = add(pick(second, core, 2), lax.ppermute(pick(second, 1 - core, 2), "pts", swap))
+    drawn_second, last_mark = draws.send([mark, second])
+    drawn = [drawn_first, drawn_second]
+    second = add(
+        pick(second, chip, 1), *[shift(pick(second, (chip + by) % chips, 1), by) for by in range(1, chips)]
+    ).reshape(outer, 2, quarter, hidden)
+    marks = [[second, last_mark]]
+    second = add(pick(second, parity, 1), across(pick(second, 1 - parity, 1)))
 
     summed = sum(part.astype(jnp.float32) for part in cotangent)
     bias_half = jnp.sum(summed[:chips * rows_local], axis=0)
@@ -559,6 +591,16 @@
         bias = lax.dynamic_update_slice_in_dim(bias, bias_half[number * share:(number + 1) * share], index * share, 0)
     vectors = jnp.stack([bias, readout]).reshape(-1, LANES)
     vectors = vectors + sum(rotate(vectors, by) for by in range(1, pts_count))
+    marks.append([second, vectors])
+    second = add(
+        pick(second, place, 0), *[along(pick(second, (place + by) % outer, 0), by) for by in range(1, outer)]
+    )
+    marks.append([second])
+    blocks = jnp.zeros((pts_count, quarter, hidden), jnp.float32)
+    for by in range(pts_count):
+        block = rotate(second, by) if by else second
+        blocks = lax.dynamic_update_index_in_dim(blocks, block.astype(jnp.float32), (pts_index - by) % pts_count, 0)
+    second = blocks.reshape(pts_count * quarter, hidden)
     bias, readout = (
         lax.dynamic_slice_in_dim(v, coord_index * (hidden // coord_count), hidden // coord_count, 0)
         for v in vectors.reshape(2, hidden)
@@ -571,13 +613,20 @@
         cotangent = [rows[i] for i in range(rows.shape[0])]
         places = [(i % 2, -(i // 2) % (len(cotangent) // 2)) for i in range(len(cotangent))]
 
-    out = None
-    swap = [(i, i ^ 1) for i in range(pts_count)]
-    for (first, count), z, after in zip(cuts, drawn, (mine, mine)):
-        keep, send = gradient(turn, after, cotangent, places, own, z, width, first, count, valid)
-        got = lax.ppermute(send, "pts", swap)
-        wide = 2 * width if count % 2 == 0 and first % 2 == 0 else width
-        out = join(keep, got, out, wide, first * width // wide, valid)
+    def part(after, number, first, count, joined=None):
+        keep, send, *out = gradient(
+            turn, after, cotangent, places, own, drawn[number], width, first, count, cuts[number][0], valid, joined
+        )
+        return keep, lax.ppermute(send, "pts", swap), *out
+
+    late = 2 if cuts[1][1] % 2 == 0 else 1
+    middle = cuts[1][1] - late
+    one = part(marks[0], 0, *cuts[0])
+    two = part(marks[1], 1, early, middle)
+    *three, out = part(marks[2], 1, early + middle, late, one)
+    for (keep, got), first, size in ((two, early, middle), (three, early + middle, late)):
+        wide = width * math.gcd(size, first, 2)
+        out = join([], keep, got, out, wide, first * width // wide, valid)
     return (residual, out.T, second, bias, readout)
 
 

time: 394 us -> 326 us (0.83)
  waiting for transfers between devices: 86.9 us -> 21.3 us
  between operations: 14.5 us -> 1.35 us
  Pallas kernels: 237 us -> 247 us
  starting transfers between devices: 24 us -> 32.5 us
  blocking collectives: 5.98 us -> 0 us
    reduce_scatter x1 -> x0, waiting for transfers between devices: 56.6 us -> none  [shards(): lax.psum_scatter(second.astype(jnp.bfloat16), 'coord', scatter_dimension=...]
    ppermute x6, waiting for transfers between devices: 24 us -> 5.92 us  [rotate(): lax.ppermute(a, 'pts', [(i, (i + by) % pts_count) for i in range(pts_coun...]
    pallas_call x2 -> x3, Pallas kernels: 40.1 us -> 51.1 us  [gradient(): pl.pallas_call(functools.partial(gradient_kernel, 1 + len(others), places...]
    ppermute x6 -> x9, starting transfers between devices: 9.57 us -> 16.6 us  [along(): lax.ppermute(a, 'coord', [(i, (i + 2 * by) % coord_count) for i in range(...]
    ppermute x6 -> x9, waiting for transfers between devices: 0.02 us -> 6.63 us  [along(): lax.ppermute(a, 'coord', [(i, (i + 2 * by) % coord_count) for i in range(...]
    all_gather x1 -> x0, blocking collectives: 5.98 us -> none  [shards(): lax.all_gather(scattered, 'pts', axis=0, tiled=True).astype(jnp.float32)]
    pallas_call x2, Pallas kernels: 10.7 us -> 5.86 us  [join(): pl.pallas_call(join_kernel, grid=(count,), in_specs=specs, out_specs=pl.B...]
    unnamed x38 -> x57, local copies, waits for them, and re-layouts: 3.04 us -> 7.35 us
  transfers between devices with their start and end apart: 21 -> 27, of which waited for: 9 -> 10; matrix products, arithmetic and copies ran while one was open for 5% -> 4% of each run, Pallas kernels for 53% -> 67%
where the time goes in v4:
time: 326 us; the launch traced here: 325 us
  Pallas kernels  247 us (76%)
  starting transfers between devices  32.5 us (10%)
  waiting for transfers between devices  21.3 us (7%)
  local copies, waits for them, and re-layouts  12.7 us (4%)
  other arithmetic  8.51 us (3%)
    pallas_call x1, Pallas kernels, forward(): pl.pallas_call(functools.partial(forward_kernel, valid), grid=(steps,), i...  105 us
    pallas_call x4, Pallas kernels, redraw(): pl.pallas_call(functools.partial(redraw_kernel, first), grid=(count,), in...  79.4 us
    pallas_call x3, Pallas kernels, gradient(): pl.pallas_call(functools.partial(gradient_kernel, 1 + len(others), places...  51.1 us
    ppermute x9, starting transfers between devices, along(): lax.ppermute(a, 'coord', [(i, (i + 2 * by) % coord_count) for i in range(...  16.6 us
    unnamed x57, local copies, waits for them, and re-layouts  7.35 us
    ppermute x9, waiting for transfers between devices, along(): lax.ppermute(a, 'coord', [(i, (i + 2 * by) % coord_count) for i in range(...  6.63 us
  transfers between devices with their start and end apart: 27, of which 10 were waited for; matrix products, arithmetic and copies ran while one was open for 4% of the time, Pallas kernels for 67%

profile of v4, /device:TPU:0, one launch (start us, length us, event | category | flops | bytes accessed | tf_op | source)
XLA Modules:
  0.0 325.3 jit_solution(17643798674024349692)
XLA Ops:
  0.6 3.0 collective-permute-start.1
  3.7 1.5 broadcast_in_dim.42.coef_ref
  5.2 0.7 pad_add_fusion.base_ref
  5.8 105.5 %forward.1 = (bf16[1024,12544]{1,0:T(8,128)(2,1)}, bf16[4,144,1024]{2,1,0:T(8,128)(2,1)}, bf16[4,144,1024]{2,1,0:T(8,128)(2,1)}) custom-call(s32[2]{0:T(128)} %pad_add_fusion.base_ref, s32[16,64]{1,0:T(8,128)} %bitcast.99, s32[1,64]{1,0:T(1,128)} %bitcast.104, f32[1,12500]{1,0:T(1,128)} %broadcast_in_dim.42.coef_ref, bf16[12500,1024]{1,0:T(8,128)(2,1)} %bitcast.97, ...), custom_call_target="tpu_custom_call" | custom-call | flops 51200000000 | bytes 51200000 | tf_op jit(solution)/shard_map/forward/pallas_call | solution.py:294
  111.3 2.0 collective-permute-start
  113.5 0.5 copy-done.26
  114.0 22.3 %redraw.4 = (bf16[1024,7168]{1,0:T(8,128)(2,1)}, f32[8,128]{1,0:T(8,128)}) custom-call(s32[2]{0:T(128)} %pad_add_fusion.base_ref, s32[16,64]{1,0:T(8,128)} %bitcast.100, s32[1,64]{1,0:T(1,128)} %bitcast.105, bf16[4,144,1024]{2,1,0:T(8,128)(2,1)} %get-tuple-element.29.refs_0_.near_ref), custom_call_target="tpu_custom_call" | custom-call | flops 14680064000 | bytes 7340032 | tf_op jit(solution)/shard_map/redraw/pallas_call | solution.py:333
  136.4 2.6 collective-permute-done.got_ref
  139.0 1.1 copy-done.16
  140.0 2.7 combine.1
  142.7 3.8 %collective-permute-start.5 = (bf16[144,1024]{1,0:T(8,128)(2,1)}, bf16[144,1024]{1,0:T(8,128)(2,1)S(1)}, u32[]{:S(2)}, u32[]{:S(2)}) collective-permute-start(bf16[144,1024]{1,0:T(8,128)(2,1)} %get-tuple-element.35), channel_id=1, source_target_pairs={{0,6},{1,7},{2,0},{3,1},{4,2},{5,3},{6,4},{7,5},{8,14},{9,15},{10,... | collective-permute-start | bytes 884744 | tf_op jit(solution)/shard_map/ppermute | solution.py:507
  146.5 1.0 collective-permute-start.3
  147.5 22.4 %redraw.5 = (bf16[1024,7168]{1,0:T(8,128)(2,1)}, f32[8,128]{1,0:T(8,128)}) custom-call(s32[2]{0:T(128)} %pad_add_fusion.base_ref, s32[16,64]{1,0:T(8,128)} %bitcast.101, s32[1,64]{1,0:T(1,128)} %bitcast.106, bf16[144,1024]{1,0:T(8,128)(2,1)} %get-tuple-element.32.refs_0_, bf16[1024,7168]{1,0:T(8,128)(2,1)} %get-tuple-element.36.refs_1_), custom_call_target="tpu_custom_call", output_to_operand_aliasing={{0}: (4, {})} | custom-call | flops 14680064000 | bytes 7340032 | tf_op jit(solution)/shard_map/redraw/pallas_call | solution.py:333
  169.9 1.2 slice.34
  171.1 0.6 broadcast_add_fusion
  172.2 0.8 fusion.1
  173.5 0.5 copy-done.24
  174.2 0.8 convolution_convert_fusion
  175.1 0.5 fusion.2
  175.7 0.7 copy-done.2
  176.6 1.6 collective-permute-start.12
  178.2 4.4 %collective-permute-done.12 = bf16[128,512]{1,0:T(8,128)(2,1)S(1)} collective-permute-done((bf16[128,512]{1,0:T(8,128)(2,1)S(1)}, bf16[128,512]{1,0:T(8,128)(2,1)S(1)}, u32[]{:S(2)}, u32[]{:S(2)}) %collective-permute-start.12) | collective-permute-done | bytes 131104 | tf_op jit(solution)/shard_map/ppermute | solution.py:491
  182.6 2.5 collective-permute-start.13
  185.1 0.9 collective-permute-start.14
  186.0 1.5 collective-permute-start.15
  187.6 17.4 %redraw.6 = (bf16[1024,5376]{1,0:T(8,128)(2,1)}, f32[8,128]{1,0:T(8,128)}) custom-call(s32[2]{0:T(128)} %pad_add_fusion.base_ref, s32[16,64]{1,0:T(8,128)} %bitcast.102, s32[1,64]{1,0:T(1,128)} %bitcast.107, bf16[272,512]{1,0:T(8,128)(2,1)} %copy-done.12), custom_call_target="tpu_custom_call" | custom-call | flops 11010048000 | bytes 5505024 | tf_op jit(solution)/shard_map/redraw/pallas_call | solution.py:333
  205.0 1.5 collective-permute-start.16
  206.5 0.7 copy-done.4
  207.4 2.1 stack.27
  209.5 0.5 collective-permute-start.17
  210.0 1.6 fusion.refs_1_
  211.7 1.6 collective-permute-start.7
  213.3 17.3 %redraw.7 = (bf16[1024,5376]{1,0:T(8,128)(2,1)}, f32[8,128]{1,0:T(8,128)}) custom-call(s32[2]{0:T(128)} %pad_add_fusion.base_ref, s32[16,64]{1,0:T(8,128)} %bitcast.103, s32[1,64]{1,0:T(1,128)} %bitcast.108, f32[8,128]{1,0:T(8,128)} %get-tuple-element.39.refs_0_, bf16[8,2,32,1024]{3,2,1,0:T(8,128)(2,1)} %copy-done.10, ...), custom_call_target="tpu_custom_call", output_to_operand_aliasing={{0}: (5, {})} | custom-call | flops 11010048000 | bytes 5505024 | tf_op jit(solution)/shard_map/redraw/pallas_call | solution.py:333
  230.8 0.9 slice_bitcast_fusion
  231.7 2.0 fusion.5
  233.8 0.7 copy-done.11
  234.5 21.9 %gradient.3 = (bf16[7168,256]{1,0:T(8,128)(2,1)}, bf16[7168,256]{1,0:T(8,128)(2,1)}) custom-call(s32[2]{0:T(128)} %pad_add_fusion.base_ref, bf16[4,2,32,1024]{3,2,1,0:T(8,128)(2,1)} %bitcast.90, f32[8,128]{1,0:T(8,128)} %get-tuple-element.41.refs_1_, bf16[272,512]{1,0:T(8,128)(2,1)} %copy-done.12, bf16[272,512]{1,0:T(8,128)(2,1)} %copy-done.4, ...), custom_call_target="tpu_custom_call" | custom-call | flops 15032385536 | bytes 29360128 | tf_op jit(solution)/shard_map/gradient/pallas_call | solution.py:401
  256.5 1.3 convert_add_fusion.3
  258.0 1.6 collective-permute-start.8
  259.6 1.3 collective-permute-start.22
  260.9 0.8 collective-permute-start.21
  261.6 1.2 collective-permute-done.22
  262.9 1.1 collective-permute-done.20
  263.9 0.6 collective-permute-done.21
  264.6 0.6 add_add_fusion.refs_1_
  265.2 1.5 collective-permute-done.8
  266.7 0.8 fusion.13.refs_0_
  267.4 13.9 %gradient.5 = (bf16[3584,256]{1,0:T(8,128)(2,1)}, bf16[3584,256]{1,0:T(8,128)(2,1)}) custom-call(s32[2]{0:T(128)} %pad_add_fusion.base_ref, bf16[4,32,1024]{2,1,0:T(8,128)(2,1)} %fusion.13.refs_0_, f32[16,128]{1,0:T(8,128)} %add_add_fusion.refs_1_, bf16[272,512]{1,0:T(8,128)(2,1)} %copy-done.12, bf16[272,512]{1,0:T(8,128)(2,1)} %copy-done.4, ...), custom_call_target="tpu_custom_call" | custom-call | flops 7516192768 | bytes 14680064 | tf_op jit(solution)/shard_map/gradient/pallas_call | solution.py:401
  281.5 6.2 %collective-permute-start.11 = (bf16[32,1024]{1,0:T(8,128)(2,1)S(1)}, bf16[32,1024]{1,0:T(8,128)(2,1)S(1)}, u32[]{:S(2)}, u32[]{:S(2)}) collective-permute-start(bf16[32,1024]{1,0:T(8,128)(2,1)S(1)} %get-tuple-element.65), channel_id=1, source_target_pairs={{0,6},{1,7},{2,0},{3,1},{4,2},{5,3},{6,4},{7,5},{8,14},{9,15},{10,... | collective-permute-start | bytes 196616 | tf_op jit(solution)/shard_map/ppermute | solution.py:507
  287.7 0.7 collective-permute-start.10
  288.4 1.8 collective-permute-done.11
  290.1 4.8 %collective-permute-done.10 = bf16[32,1024]{1,0:T(8,128)(2,1)S(1)} collective-permute-done((bf16[32,1024]{1,0:T(8,128)(2,1)S(1)}, bf16[32,1024]{1,0:T(8,128)(2,1)S(1)}, u32[]{:S(2)}, u32[]{:S(2)}) %collective-permute-start.10) | collective-permute-done | bytes 65568 | tf_op jit(solution)/shard_map/ppermute | solution.py:507
  295.2 0.5 copy-done.20
  295.7 15.3 %gradient.4 = (bf16[1748,256]{1,0:T(8,128)(2,1)}, bf16[1748,256]{1,0:T(8,128)(2,1)}, bf16[12500,256]{1,0:T(8,128)(2,1)}) custom-call(s32[2]{0:T(128)} %pad_add_fusion.base_ref, bf16[32,1024]{1,0:T(8,128)(2,1)} %copy-done.20, bf16[7168,256]{1,0:T(8,128)(2,1)} %get-tuple-element.45.refs_1_, bf16[7168,256]{1,0:T(8,128)(2,1)} %collective-permute-done.18.refs_2_, ...), custom_call_target="tpu_custom_call" | custom-call | flops 3758096384 | bytes 7340032 | tf_op jit(solution)/shard_map/gradient/pallas_call | solution.py:401
  311.0 0.4 collective-permute-start.19
  311.4 0.6 dynamic_slice.74
  312.0 0.6 dynamic_slice.75
  312.6 1.2 collective-permute-start.25
  313.8 0.3 collective-permute-start.26
  314.1 3.0 collective-permute-done.25
  317.1 1.3 copy-done.15
  318.4 3.1 join.2.refs_2_
  321.6 0.9 copy-done.17
  322.5 2.7 join.3
  (108 shorter events, 2.6 us)
Async XLA Ops:
  0.6 171.5 %copy-start = (bf16[1024,1024]{1,0:T(8,128)(2,1)S(1)}, bf16[1024,1024]{1,0:T(8,128)(2,1)}, u32[]{:S(2)}) copy-start(bf16[1024,1024]{1,0:T(8,128)(2,1)} %param.12) | copy-start | bytes 6291460
  0.6 112.8 %collective-permute-start.1 = (s32[64,16]{0,1:T(8,128)}, s32[64,16]{0,1:T(8,128)S(1)}, u32[]{:S(2)}, u32[]{:S(2)}) collective-permute-start(s32[64,16]{0,1:T(8,128)} %param.8), channel_id=1, source_target_pairs={{0,16},{8,24},{16,0},{24,8},{1,17},{9,25},{17,1},{25,9},{2,18},{10... | collective-permute-start | bytes 12296 | tf_op jit(solution)/shard_map/ppermute | solution.py:491
  3.7 109.8 %collective-permute-start.2 = (s32[64]{0:T(128)}, s32[64]{0:T(128)S(1)}, u32[]{:S(2)}, u32[]{:S(2)}) collective-permute-start(s32[64]{0:T(128)} %param.7), channel_id=1, source_target_pairs={{0,16},{8,24},{16,0},{24,8},{1,17},{9,25},{17,1},{25,9},{2,18},{10... | collective-permute-start | bytes 776 | tf_op jit(solution)/shard_map/ppermute | solution.py:491
  5.8 107.4 %copy-start.22 = (bf16[1024]{0:T(1024)(128)(2,1)S(1)}, bf16[1024]{0:T(1024)(128)(2,1)}, u32[]{:S(2)}) copy-start(bf16[1024]{0:T(1024)(128)(2,1)} %param.13) | copy-start | bytes 6148
  111.3 27.6 %collective-permute-start = (bf16[4,144,1024]{2,1,0:T(8,128)(2,1)}, bf16[4,144,1024]{2,1,0:T(8,128)(2,1)S(1)}, u32[]{:S(2)}, u32[]{:S(2)}) collective-permute-start(bf16[4,144,1024]{2,1,0:T(8,128)(2,1)} %get-tuple-element.30), channel_id=1, source_target_pairs={{0,1},{1,0},{2,3},{3,2},{4,5},{5,4},{6,7},{7,6},{8,9},{9,8},{10,11... | collective-permute-start | bytes 3538952 | tf_op jit(solution)/shard_map/ppermute | solution.py:504
  113.4 0.5 copy-start.26
  113.4 0.6 copy-start.25
  139.0 1.1 copy-start.16
  142.7 29.1 %collective-permute-start.5 = (bf16[144,1024]{1,0:T(8,128)(2,1)}, bf16[144,1024]{1,0:T(8,128)(2,1)S(1)}, u32[]{:S(2)}, u32[]{:S(2)}) collective-permute-start(bf16[144,1024]{1,0:T(8,128)(2,1)} %get-tuple-element.35), channel_id=1, source_target_pairs={{0,6},{1,7},{2,0},{3,1},{4,2},{5,3},{6,4},{7,5},{8,14},{9,15},{10,... | collective-permute-start | bytes 884744 | tf_op jit(solution)/shard_map/ppermute | solution.py:507
  146.5 25.3 %collective-permute-start.4 = (bf16[144,1024]{1,0:T(8,128)(2,1)}, bf16[144,1024]{1,0:T(8,128)(2,1)S(1)}, u32[]{:S(2)}, u32[]{:S(2)}) collective-permute-start(bf16[144,1024]{1,0:T(8,128)(2,1)} %get-tuple-element.34), channel_id=1, source_target_pairs={{0,4},{1,5},{2,6},{3,7},{4,0},{5,1},{6,2},{7,3},{8,12},{9,13},{10,... | collective-permute-start | bytes 884744 | tf_op jit(solution)/shard_map/ppermute | solution.py:507
  146.5 25.3 %collective-permute-start.3 = (bf16[144,1024]{1,0:T(8,128)(2,1)}, bf16[144,1024]{1,0:T(8,128)(2,1)S(1)}, u32[]{:S(2)}, u32[]{:S(2)}) collective-permute-start(bf16[144,1024]{1,0:T(8,128)(2,1)} %get-tuple-element.33), channel_id=1, source_target_pairs={{0,2},{1,3},{2,4},{3,5},{4,6},{5,7},{6,0},{7,1},{8,10},{9,11},{10,... | collective-permute-start | bytes 884744 | tf_op jit(solution)/shard_map/ppermute | solution.py:507
  147.5 23.6 %copy-start.23 = (f32[1024]{0:T(1024)S(1)}, f32[1024]{0:T(1024)}, u32[]{:S(2)}) copy-start(f32[1024]{0:T(1024)} %param.11) | copy-start | bytes 12292
  147.5 24.3 %copy-start.19 = (bf16[144,1024]{1,0:T(8,128)(2,1)S(1)}, bf16[144,1024]{1,0:T(8,128)(2,1)}, u32[]{:S(2)}) copy-start(bf16[144,1024]{1,0:T(8,128)(2,1)} %get-tuple-element.32.refs_0_) | copy-start | bytes 884740
  173.5 0.5 copy-start.24
  175.0 1.3 copy-start.2
  176.4 33.7 %collective-permute-start.6 = (bf16[8,2,32,1024]{3,2,1,0:T(8,128)(2,1)S(1)}, bf16[8,2,32,1024]{3,2,1,0:T(8,128)(2,1)}, u32[]{:S(2)}, u32[]{:S(2)}) collective-permute-start(bf16[8,2,32,1024]{3,2,1,0:T(8,128)(2,1)S(1)} %dynamic-slice_bitcast_fusion), channel_id=1, source_target_pairs={{0,8},{8,0},{16,24},{24,16},{1,9},{9,1},{17,25},{25,17},{2,10},{10... | collective-permute-start | bytes 3145736 | tf_op jit(solution)/shard_map/ppermute | solution.py:577
  176.6 6.0 %collective-permute-start.12 = (bf16[128,512]{1,0:T(8,128)(2,1)S(1)}, bf16[128,512]{1,0:T(8,128)(2,1)S(1)}, u32[]{:S(2)}, u32[]{:S(2)}) collective-permute-start(bf16[128,512]{1,0:T(8,128)(2,1)S(1)} %pad_maximum_fusion), channel_id=1, source_target_pairs={{0,16},{8,24},{16,0},{24,8},{1,17},{9,25},{17,1},{25,9},{2,18},{10... | collective-permute-start | bytes 393224 | tf_op jit(solution)/shard_map/ppermute | solution.py:491
  182.6 5.0 %copy-start.12 = (bf16[272,512]{1,0:T(8,128)(2,1)}, bf16[272,512]{1,0:T(8,128)(2,1)S(1)}, u32[]{:S(2)}) copy-start(bf16[272,512]{1,0:T(8,128)(2,1)S(1)} %fusion.14.refs_0_.refs_2_.refs_3_) | copy-start | bytes 835588
  182.6 27.5 %copy-start.3 = (bf16[1024,1024]{1,0:T(8,128)(2,1)S(1)}, bf16[1024,1024]{1,0:T(8,128)(2,1)}, u32[]{:S(2)}) copy-start(bf16[1024,1024]{1,0:T(8,128)(2,1)} %copy-done.2) | copy-start | bytes 6291460
  182.6 23.9 %collective-permute-start.13 = (bf16[272,512]{1,0:T(8,128)(2,1)S(1)}, bf16[272,512]{1,0:T(8,128)(2,1)S(1)}, u32[]{:S(2)}, u32[]{:S(2)}) collective-permute-start(bf16[272,512]{1,0:T(8,128)(2,1)S(1)} %fusion.14.refs_0_.refs_2_.refs_3_), channel_id=1, source_target_pairs={{0,2},{1,3},{2,4},{3,5},{4,6},{5,7},{6,0},{7,1},{8,10},{9,11},{10,... | collective-permute-start | bytes 835592 | tf_op jit(solution)/shard_map/ppermute | solution.py:507
  185.1 21.4 %collective-permute-start.14 = (bf16[272,512]{1,0:T(8,128)(2,1)S(1)}, bf16[272,512]{1,0:T(8,128)(2,1)S(1)}, u32[]{:S(2)}, u32[]{:S(2)}) collective-permute-start(bf16[272,512]{1,0:T(8,128)(2,1)S(1)} %fusion.14.refs_0_.refs_2_.refs_3_), channel_id=1, source_target_pairs={{0,4},{1,5},{2,6},{3,7},{4,0},{5,1},{6,2},{7,3},{8,12},{9,13},{10,... | collective-permute-start | bytes 835592 | tf_op jit(solution)/shard_map/ppermute | solution.py:507
  186.0 20.5 %collective-permute-start.15 = (bf16[272,512]{1,0:T(8,128)(2,1)S(1)}, bf16[272,512]{1,0:T(8,128)(2,1)S(1)}, u32[]{:S(2)}, u32[]{:S(2)}) collective-permute-start(bf16[272,512]{1,0:T(8,128)(2,1)S(1)} %fusion.14.refs_0_.refs_2_.refs_3_), channel_id=1, source_target_pairs={{0,6},{1,7},{2,0},{3,1},{4,2},{5,3},{6,4},{7,5},{8,14},{9,15},{10,... | collective-permute-start | bytes 835592 | tf_op jit(solution)/shard_map/ppermute | solution.py:507
  205.0 28.8 %collective-permute-start.16 = (bf16[272,512]{1,0:T(8,128)(2,1)}, bf16[272,512]{1,0:T(8,128)(2,1)S(1)}, u32[]{:S(2)}, u32[]{:S(2)}) collective-permute-start(bf16[272,512]{1,0:T(8,128)(2,1)} %copy-done.12), channel_id=1, source_target_pairs={{0,1},{1,0},{2,3},{3,2},{4,5},{5,4},{6,7},{7,6},{8,9},{9,8},{10,11... | collective-permute-start | bytes 835592 | tf_op jit(solution)/shard_map/ppermute | solution.py:504
  206.5 0.7 copy-start.4
  206.5 0.8 copy-start.6
  206.5 0.9 copy-start.8
  209.5 21.3 %collective-permute-start.17 = (bf16[3,272,512]{2,1,0:T(8,128)(2,1)}, bf16[3,272,512]{2,1,0:T(8,128)(2,1)S(1)}, u32[]{:S(2)}, u32[]{:S(2)}) collective-permute-start(bf16[3,272,512]{2,1,0:T(8,128)(2,1)} %get-tuple-element.42), channel_id=1, source_target_pairs={{0,1},{1,0},{2,3},{3,2},{4,5},{5,4},{6,7},{7,6},{8,9},{9,8},{10,11... | collective-permute-start | bytes 2506760 | tf_op jit(solution)/shard_map/ppermute | solution.py:504
  211.7 1.6 copy-start.10
  211.7 20.0 %collective-permute-start.7 = (bf16[8,32,1024]{2,1,0:T(8,128)(2,1)S(1)}, bf16[8,32,1024]{2,1,0:T(8,128)(2,1)S(1)}, u32[]{:S(2)}, u32[]{:S(2)}) collective-permute-start(bf16[8,32,1024]{2,1,0:T(8,128)(2,1)S(1)} %dynamic-slice_bitcast_fusion.1), channel_id=1, source_target_pairs={{0,16},{8,24},{16,0},{24,8},{1,17},{9,25},{17,1},{25,9},{2,18},{10... | collective-permute-start | bytes 1572872 | tf_op jit(solution)/shard_map/ppermute | solution.py:491
  233.8 0.7 copy-start.11
  234.5 22.0 %copy-start.5 = (bf16[272,512]{1,0:T(8,128)(2,1)S(1)}, bf16[272,512]{1,0:T(8,128)(2,1)}, u32[]{:S(2)}) copy-start(bf16[272,512]{1,0:T(8,128)(2,1)} %copy-done.4) | copy-start | bytes 835588
  234.5 22.0 %copy-start.7 = (bf16[272,512]{1,0:T(8,128)(2,1)S(1)}, bf16[272,512]{1,0:T(8,128)(2,1)}, u32[]{:S(2)}) copy-start(bf16[272,512]{1,0:T(8,128)(2,1)} %copy-done.6) | copy-start | bytes 835588
  234.5 22.0 %copy-start.9 = (bf16[272,512]{1,0:T(8,128)(2,1)S(1)}, bf16[272,512]{1,0:T(8,128)(2,1)}, u32[]{:S(2)}) copy-start(bf16[272,512]{1,0:T(8,128)(2,1)} %copy-done.8) | copy-start | bytes 835588
  256.4 1.5 copy-start.14
  256.4 38.8 %collective-permute-start.18 = (bf16[7168,256]{1,0:T(8,128)(2,1)}, bf16[7168,256]{1,0:T(8,128)(2,1)}, u32[]{:S(2)}, u32[]{:S(2)}) collective-permute-start(bf16[7168,256]{1,0:T(8,128)(2,1)} %get-tuple-element.46), channel_id=1, source_target_pairs={{0,8},{8,0},{16,24},{24,16},{1,9},{9,1},{17,25},{25,17},{2,10},{10... | collective-permute-start | bytes 11010056 | tf_op jit(solution)/shard_map/ppermute | solution.py:620
  258.0 8.7 %collective-permute-start.8 = (bf16[4,32,1024]{2,1,0:T(8,128)(2,1)S(1)}, bf16[4,32,1024]{2,1,0:T(8,128)(2,1)S(1)}, u32[]{:S(2)}, u32[]{:S(2)}) collective-permute-start(bf16[4,32,1024]{2,1,0:T(8,128)(2,1)S(1)} %dynamic-slice_bitcast_fusion.2), channel_id=1, source_target_pairs={{0,1},{1,0},{2,3},{3,2},{4,5},{5,4},{6,7},{7,6},{8,9},{9,8},{10,11... | collective-permute-start | bytes 786440 | tf_op jit(solution)/shard_map/ppermute | solution.py:504
  259.6 3.3 %collective-permute-start.22 = (f32[16,128]{1,0:T(8,128)S(1)}, f32[16,128]{1,0:T(8,128)S(1)}, u32[]{:S(2)}, u32[]{:S(2)}) collective-permute-start(f32[16,128]{1,0:T(8,128)S(1)} %reshape.65), channel_id=1, source_target_pairs={{0,24},{8,0},{16,8},{24,16},{1,25},{9,1},{17,9},{25,17},{2,26},{10... | collective-permute-start | bytes 24584 | tf_op jit(solution)/shard_map/ppermute | solution.py:568
  260.9 3.1 collective-permute-start.20
  260.9 3.7 %collective-permute-start.21 = (f32[16,128]{1,0:T(8,128)S(1)}, f32[16,128]{1,0:T(8,128)S(1)}, u32[]{:S(2)}, u32[]{:S(2)}) collective-permute-start(f32[16,128]{1,0:T(8,128)S(1)} %reshape.65), channel_id=1, source_target_pairs={{0,16},{8,24},{16,0},{24,8},{1,17},{9,25},{17,1},{25,9},{2,18},{10... | collective-permute-start | bytes 24584 | tf_op jit(solution)/shard_map/ppermute | solution.py:568
  267.4 14.0 %copy-start.13 = (bf16[4,32,1024]{2,1,0:T(8,128)(2,1)S(1)}, bf16[4,32,1024]{2,1,0:T(8,128)(2,1)}, u32[]{:S(2)}) copy-start(bf16[4,32,1024]{2,1,0:T(8,128)(2,1)} %fusion.13.refs_0_) | copy-start | bytes 786436
  281.4 35.8 %collective-permute-start.23 = (bf16[3584,256]{1,0:T(8,128)(2,1)}, bf16[3584,256]{1,0:T(8,128)(2,1)S(1)}, u32[]{:S(2)}, u32[]{:S(2)}) collective-permute-start(bf16[3584,256]{1,0:T(8,128)(2,1)} %get-tuple-element.51), channel_id=1, source_target_pairs={{0,8},{8,0},{16,24},{24,16},{1,9},{9,1},{17,25},{25,17},{2,10},{10... | collective-permute-start | bytes 5505032 | tf_op jit(solution)/shard_map/ppermute | solution.py:620
  281.5 8.6 %collective-permute-start.11 = (bf16[32,1024]{1,0:T(8,128)(2,1)S(1)}, bf16[32,1024]{1,0:T(8,128)(2,1)S(1)}, u32[]{:S(2)}, u32[]{:S(2)}) collective-permute-start(bf16[32,1024]{1,0:T(8,128)(2,1)S(1)} %get-tuple-element.65), channel_id=1, source_target_pairs={{0,6},{1,7},{2,0},{3,1},{4,2},{5,3},{6,4},{7,5},{8,14},{9,15},{10,... | collective-permute-start | bytes 196616 | tf_op jit(solution)/shard_map/ppermute | solution.py:507
  287.7 7.3 %collective-permute-start.10 = (bf16[32,1024]{1,0:T(8,128)(2,1)S(1)}, bf16[32,1024]{1,0:T(8,128)(2,1)S(1)}, u32[]{:S(2)}, u32[]{:S(2)}) collective-permute-start(bf16[32,1024]{1,0:T(8,128)(2,1)S(1)} %get-tuple-element.66), channel_id=1, source_target_pairs={{0,4},{1,5},{2,6},{3,7},{4,0},{5,1},{6,2},{7,3},{8,12},{9,13},{10,... | collective-permute-start | bytes 196616 | tf_op jit(solution)/shard_map/ppermute | solution.py:507
  288.4 6.6 %collective-permute-start.9 = (bf16[32,1024]{1,0:T(8,128)(2,1)S(1)}, bf16[32,1024]{1,0:T(8,128)(2,1)S(1)}, u32[]{:S(2)}, u32[]{:S(2)}) collective-permute-start(bf16[32,1024]{1,0:T(8,128)(2,1)S(1)} %get-tuple-element.64), channel_id=1, source_target_pairs={{0,2},{1,3},{2,4},{3,5},{4,6},{5,7},{6,0},{7,1},{8,10},{9,11},{10,... | collective-permute-start | bytes 196616 | tf_op jit(solution)/shard_map/ppermute | solution.py:507
  295.1 0.6 copy-start.20
  295.1 19.0 %collective-permute-start.24 = (bf16[32,1024]{1,0:T(8,128)(2,1)S(1)}, bf16[32,1024]{1,0:T(8,128)(2,1)S(1)}, u32[]{:S(2)}, u32[]{:S(2)}) collective-permute-start(bf16[32,1024]{1,0:T(8,128)(2,1)S(1)} %get-tuple-element.54.refs_0_), channel_id=1, source_target_pairs={{0,8},{8,16},{16,24},{24,0},{1,9},{9,17},{17,25},{25,1},{2,10},{10... | collective-permute-start | bytes 196616 | tf_op jit(solution)/shard_map/ppermute | solution.py:568
  295.7 15.7 %copy-start.21 = (f32[16,128]{1,0:T(8,128)S(1)}, f32[16,128]{1,0:T(8,128)}, u32[]{:S(2)}) copy-start(f32[16,128]{1,0:T(8,128)} %add_add_fusion.refs_1_) | copy-start | bytes 24580
  311.0 10.6 %collective-permute-start.19 = (bf16[1748,256]{1,0:T(8,128)(2,1)}, bf16[1748,256]{1,0:T(8,128)(2,1)S(1)}, u32[]{:S(2)}, u32[]{:S(2)}) collective-permute-start(bf16[1748,256]{1,0:T(8,128)(2,1)} %get-tuple-element.49), channel_id=1, source_target_pairs={{0,8},{8,0},{16,24},{24,16},{1,9},{9,1},{17,25},{25,17},{2,10},{10... | collective-permute-start | bytes 2684936 | tf_op jit(solution)/shard_map/ppermute | solution.py:620
  312.6 4.5 %collective-permute-start.25 = (bf16[32,1024]{1,0:T(8,128)(2,1)}, bf16[32,1024]{1,0:T(8,128)(2,1)S(1)}, u32[]{:S(2)}, u32[]{:S(2)}) collective-permute-start(bf16[32,1024]{1,0:T(8,128)(2,1)} %copy-done.20), channel_id=1, source_target_pairs={{0,16},{8,24},{16,0},{24,8},{1,17},{9,25},{17,1},{25,9},{2,18},{10... | collective-permute-start | bytes 196616 | tf_op jit(solution)/shard_map/ppermute | solution.py:568
  313.8 3.3 %collective-permute-start.26 = (bf16[32,1024]{1,0:T(8,128)(2,1)}, bf16[32,1024]{1,0:T(8,128)(2,1)S(1)}, u32[]{:S(2)}, u32[]{:S(2)}) collective-permute-start(bf16[32,1024]{1,0:T(8,128)(2,1)} %copy-done.20), channel_id=1, source_target_pairs={{0,24},{8,0},{16,8},{24,16},{1,25},{9,1},{17,9},{25,17},{2,26},{10... | collective-permute-start | bytes 196616 | tf_op jit(solution)/shard_map/ppermute | solution.py:568
  317.1 4.5 %copy-start.18 = (f32[4,32,1024]{2,1,0:T(8,128)}, f32[4,32,1024]{2,1,0:T(8,128)S(1)}, u32[]{:S(2)}) copy-start(f32[4,32,1024]{2,1,0:T(8,128)S(1)} %convert_dynamic-update-slice_fusion) | copy-start | bytes 1572868
  317.1 1.3 copy-start.15
  321.6 0.9 copy-start.17
  322.5 2.7 copy-start.1

commit v5 on v4

--- a/solution.py
+++ b/solution.py
@@ -247,12 +247,13 @@
 def gradient_kernel(count, places, skip, joins, base_ref, *refs):
     refs = refs[skip:]
     if joins:
-        keep, got, *refs, out_ref, left = refs
+        keep, got, *refs, out_ref, mark_ref, left = refs
         out_ref[...] = (keep[...].astype(jnp.float32) + got[...].astype(jnp.float32)).astype(jnp.bfloat16)
-        refs = [*refs, left]
+        refs = [*refs, mark_ref, left]
     d_refs, refs = refs[:len(places)], refs[len(places):]
     blocks = len(places)
-    z_refs, (keep_ref, send_ref, left) = refs[:count], refs[count:]
+    z_refs, (keep_ref, send_ref, mark_ref, left) = refs[:count], refs[count:]
+    mark_ref[...] = jnp.zeros_like(mark_ref)
     half = keep_ref.shape[1]
 
     @pl.when(pl.program_id(0) == 0)
@@ -347,8 +348,7 @@
         ],
         compiler_params=params(),
         cost_estimate=pl.CostEstimate(
-            flops=100 * rows * width * count * 40, bytes_accessed=2 * rows * width * count,
-            transcendentals=2 * rows * width * count,
+            flops=100 * rows * width * count * 40, bytes_accessed=2 * rows * width * count, transcendentals=0,
         ),
         name="redraw",
     )(base, pert, point, *after, *extra)
@@ -386,7 +386,7 @@
 
 
 def gradient(base, after, cotangent, places, own, others, width, first, count, start, valid, joined=None):
-    if all(n % 2 == 0 for n in (count, first, start)):
+    if joined is None and all(n % 2 == 0 for n in (count, first, start)):
         width, first, count, start = 2 * width, first // 2, count // 2, start // 2
     rows = own.shape[0]
     half = cotangent[0].shape[1] // 2
@@ -398,6 +398,7 @@
         joins = list(joined)
         spec = pl.BlockSpec((joins[0].shape[0] // count, half), lambda s: (s, 0))
         out_specs, out_shape = out_specs + [spec], out_shape + [jax.ShapeDtypeStruct((valid, half), jnp.bfloat16)]
+    out_specs, out_shape = out_specs + [whole((8, LANES))], out_shape + [jax.ShapeDtypeStruct((8, LANES), jnp.float32)]
     return pl.pallas_call(
         functools.partial(gradient_kernel, 1 + len(others), places, len(after), len(joins) > 0),
         grid=(count,),
@@ -411,8 +412,7 @@
         scratch_shapes=[pltpu.VMEM((2 * half, (1 + len(others)) * rows), jnp.bfloat16)],
         compiler_params=params(),
         cost_estimate=pl.CostEstimate(
-            flops=4 * half * rows * (1 + len(others)) * width * count,
-            bytes_accessed=2 * rows * (1 + len(others)) * width * count, transcendentals=0,
+            flops=100 * rows * width * count * 40, bytes_accessed=2 * rows * width * count, transcendentals=0,
         ),
         name="gradient",
     )(base, *after, *joins, *cotangent, own, *others)
@@ -439,29 +439,85 @@
     )(*operands)
 
 
-def hidden_pass(pre_first, squares, source, w2, w3, count_samples):
-    hidden_one = jnp.tanh(pre_first).astype(jnp.bfloat16)
-    pre_second = lax.dot_general(
-        hidden_one, w2, (((1,), (1,)), ((), ())), preferred_element_type=jnp.float32
-    )
-    hidden_two = jnp.tanh(pre_second).astype(jnp.bfloat16)
-    values_out = READOUT * jnp.dot(hidden_two, w3, preferred_element_type=jnp.float32)
-    stein_weight = (squares - D) / (NOISE_SCALE * NOISE_SCALE * count_samples)
-    per_point = (stein_weight * values_out).reshape(-1, count_samples)
-    residual = jnp.sum(per_point, axis=1) - source
-    grad_values = (residual[:, None] * stein_weight.reshape(-1, count_samples)).reshape(-1)
-    two_float = hidden_two.astype(jnp.float32)
-    grad_readout = READOUT * jnp.sum(grad_values[:, None] * two_float, axis=0)
-    grad_pre_two = (
-        READOUT
-        * grad_values[:, None]
-        * w3.astype(jnp.float32)[None, :]
-        * (1.0 - two_float * two_float)
-    ).astype(jnp.bfloat16)
-    grad_hidden = jnp.dot(grad_pre_two, w2, preferred_element_type=jnp.float32)
-    one_float = hidden_one.astype(jnp.float32)
-    grad_pre_one = (grad_hidden * (1.0 - one_float * one_float)).astype(jnp.bfloat16)
-    return (residual, grad_pre_one, grad_readout, hidden_one, grad_pre_two)
+def hidden_kernel(samples, count, chips, base_ref, _, *refs):
+    part_refs, (b1_ref, w2_ref, w3_ref), refs = refs[:count], refs[count:count + 3], refs[count + 3:]
+    residual_ref, kept_ref, sent_ref, *share_refs, first, second = refs
+    rows = part_refs[0].shape[0] - 16
+    coord, pts = base_ref[1], base_ref[2]
+    total = sum(ref[...].astype(jnp.float32) for ref in part_refs)
+    sums = jnp.sum(total[rows:rows + 3, :2 * LANES], axis=0, keepdims=True)
+    row = lax.broadcasted_iota(jnp.int32, (rows, LANES), 0)
+    lane = lax.broadcasted_iota(jnp.int32, (rows, LANES), 1)
+
+    def choose(values, index):
+        return jnp.sum(jnp.where(lane == index, values, 0.0), axis=1, keepdims=True)
+
+    point = lax.div(row, samples)
+    squares = choose(sums[:, :LANES], row + lax.rem(coord * rows, LANES))
+    source = choose(sums[:, LANES:], point + coord * (rows // samples))
+    one = jnp.tanh(total[:rows] + b1_ref[...]).astype(jnp.bfloat16)
+    two = jnp.tanh(
+        lax.dot_general(one, w2_ref[...], (((1,), (1,)), ((), ())), preferred_element_type=jnp.float32)
+    ).astype(jnp.bfloat16).astype(jnp.float32)
+    w3 = w3_ref[...]
+    values = READOUT * jnp.sum(two * w3, axis=1, keepdims=True)
+    stein = (squares - D) / (NOISE_SCALE * NOISE_SCALE * samples)
+    terms = jnp.broadcast_to(stein * values, (rows, LANES))
+    if rows < LANES:
+        terms = jnp.concatenate([terms, jnp.zeros((LANES - rows, LANES), jnp.float32)], axis=0)
+    terms = jnp.where(lax.div(lane, samples) == point, terms.T[:rows], 0.0)
+    residual = jnp.sum(terms, axis=1, keepdims=True) - source
+    for number in range(rows // samples):
+        residual_ref[number:number + 1] = jnp.broadcast_to(residual[number * samples:number * samples + 1], (1, LANES))
+    cotangent = residual * stein
+    readout = READOUT * jnp.sum(cotangent * two, axis=0, keepdims=True)
+    pre_two = (READOUT * cotangent * w3 * (1.0 - two * two)).astype(jnp.bfloat16)
+    wide = one.astype(jnp.float32)
+    pre_one = jnp.dot(pre_two, w2_ref[...], preferred_element_type=jnp.float32) * (1.0 - wide * wide)
+    first[...] = pre_one.astype(jnp.bfloat16)
+    bias = jnp.sum(first[...].astype(jnp.float32), axis=0, keepdims=True)
+    share = first.shape[1] // (2 * chips)
+    for by, ref in enumerate(share_refs):
+        chip = lax.rem(lax.div(pts, 2) + by, chips)
+        for half in range(2):
+            index = chip * 2 + (pts + half) % 2
+            ref[:, half * share:(half + 1) * share] = first[:, pl.ds(pl.multiple_of(index * share, share), share)]
+    height, wide = kept_ref.shape[3] - 16, first.shape[1]
+    outer = kept_ref.shape[2]
+    second[:wide] = jnp.dot(pre_two.T, one, preferred_element_type=jnp.float32).astype(jnp.bfloat16)
+    second[wide:] = jnp.concatenate([readout, bias, jnp.zeros((14, wide), jnp.float32)], axis=0).astype(jnp.bfloat16)
+    for other_core, ref in enumerate((kept_ref, sent_ref)):
+        for by in range(chips):
+            index = lax.rem(lax.div(pts, 2) + by, chips) * 2 + (pts + other_core) % 2
+            lanes = pl.ds(pl.multiple_of(index * share, share), share)
+            for other in range(2):
+                for shift in range(outer):
+                    block = lax.rem(lax.div(coord, 2) + shift, outer) * 2 + (coord + other) % 2
+                    rows_of = pl.ds(pl.multiple_of(block * height, height), height)
+                    ref[by, other, shift, :height] = second[rows_of, lanes]
+                    ref[by, other, shift, height:] = second[wide:, lanes]
+
+
+def hidden_layers(base, after, parts, b1, w2, w3, samples, chips, blocks):
+    rows, hidden = parts[0].shape[0] - 16, parts[0].shape[1]
+    shapes = [(rows // samples, LANES)] + [(chips, 2, blocks // 2, hidden // blocks + 16, hidden // chips // 2)] * 2
+    shapes += [(rows, hidden // chips)] * chips
+    types = [jnp.float32] + [jnp.bfloat16] * (2 + chips)
+    operands = [*parts, b1[None, :], w2, w3.astype(jnp.float32)[None, :]]
+    return pl.pallas_call(
+        functools.partial(hidden_kernel, samples, len(parts), chips),
+        grid=(1,),
+        in_specs=[pl.BlockSpec(memory_space=pltpu.SMEM), pl.BlockSpec(memory_space=pl.ANY)]
+        + [whole(a.shape) for a in operands],
+        out_specs=[whole(shape) for shape in shapes],
+        out_shape=[jax.ShapeDtypeStruct(shape, kind) for shape, kind in zip(shapes, types)],
+        scratch_shapes=[pltpu.VMEM((rows, hidden), jnp.bfloat16), pltpu.VMEM((hidden + 16, hidden), jnp.bfloat16)],
+        compiler_params=params(),
+        cost_estimate=pl.CostEstimate(
+            flops=6 * rows * hidden * hidden, bytes_accessed=4 * hidden * hidden, transcendentals=2 * rows * hidden
+        ),
+        name="hidden",
+    )(base, after, *operands)
 
 
 def block_width(valid):
@@ -484,7 +540,7 @@
     share = hidden // pts_count
     width = block_width(valid)
     steps = -(-valid // width)
-    base = jnp.stack([coord_index * valid, coord_index]).astype(jnp.int32)
+    base = jnp.stack([coord_index * valid, coord_index, pts_index]).astype(jnp.int32)
 
     def shift(a, by):
         return jax.tree.map(
@@ -524,27 +580,10 @@
     _, mark = next(draws)
     parts = combine(near, across(far), mark)
     drawn_first, mark = draws.send([parts[0]])
-    total = parts[0].astype(jnp.float32)
-    for by in range(1, outer):
-        total += along(parts[by], by).astype(jnp.float32)
-    pre_local = total[:rows_local]
-    sums = jnp.sum(total[rows_local:rows_local + 3], axis=0)
-    squares_local = lax.dynamic_slice_in_dim(sums, coord_index * rows_local % LANES, rows_local, 0)
-    source_local = lax.dynamic_slice_in_dim(sums, LANES + coord_index * points_local, points_local, 0)
-    b1 = b1 + mark[0, 0]
-    residual, grad_pre_one, grad_readout, hidden_one, grad_pre_two = hidden_pass(
-        pre_local.astype(jnp.float32) + b1[None, :], squares_local, source_local, w2, w3, samples
-    )
-
-    def share_of(index):
-        return jnp.concatenate(
-            [lax.dynamic_slice_in_dim(grad_pre_one, i * share, share, 1) for i in (index, index ^ 1)], axis=1
-        )
-
-    sent = [share_of((pts_index + 2 * by) % pts_count) for by in range(chips)]
-    readout_rows = grad_readout.astype(jnp.bfloat16).reshape(-1, 2 * share)
-    readout_rows = jnp.pad(readout_rows, ((0, 16 - readout_rows.shape[0]), (0, 0)))
-    mine = jnp.concatenate([sent[0]] + [shift(sent[by], by) for by in range(1, chips)] + [readout_rows], axis=0)
+    parts = [parts[0]] + [along(parts[by], by) for by in range(1, outer)]
+    residual, kept, given, *sent = hidden_layers(base, mark, parts, b1, w2, w3, samples, chips, coord_count)
+    residual = residual[:, 0]
+    mine = jnp.concatenate([sent[0]] + [shift(sent[by], by) for by in range(1, chips)], axis=0)
     draws = redraws(1, [mine])
     _, mark = next(draws)
     if rows_local == LANES:
@@ -558,54 +597,14 @@
         gathered = lax.all_gather(mine, "coord", axis=0)
         cotangent = [gathered[i] for i in range(coord_count)]
         turn = jnp.zeros_like(base)
-    def add(kept, *received):
-        return sum((a.astype(jnp.float32) for a in received), kept.astype(jnp.float32)).astype(jnp.bfloat16)
-
-    def pick(a, index, axis):
-        return lax.dynamic_index_in_dim(a, index, axis, keepdims=False)
-
-    def rotate(a, by):
-        return lax.ppermute(a, "pts", [(i, (i + by) % pts_count) for i in range(pts_count)])
-
-    chip, core = pts_index // 2, pts_index % 2
-    place, parity = coord_index // 2, coord_index % 2
+    def add(own_part, *received):
+        return sum((a.astype(jnp.float32) for a in received), own_part.astype(jnp.float32)).astype(jnp.bfloat16)
+
     swap = [(i, i ^ 1) for i in range(pts_count)]
-    quarter = hidden // coord_count // pts_count
-    second = lax.dot_general(
-        grad_pre_two, hidden_one, (((0,), (0,)), ((), ())), preferred_element_type=jnp.float32
-    ).astype(jnp.bfloat16).reshape(coord_count, chips, 2, quarter, hidden)
-    second = add(pick(second, core, 2), lax.ppermute(pick(second, 1 - core, 2), "pts", swap))
+    second = add(kept, lax.ppermute(given, "pts", swap))
     drawn_second, last_mark = draws.send([mark, second])
     drawn = [drawn_first, drawn_second]
-    second = add(
-        pick(second, chip, 1), *[shift(pick(second, (chip + by) % chips, 1), by) for by in range(1, chips)]
-    ).reshape(outer, 2, quarter, hidden)
-    marks = [[second, last_mark]]
-    second = add(pick(second, parity, 1), across(pick(second, 1 - parity, 1)))
-
-    summed = sum(part.astype(jnp.float32) for part in cotangent)
-    bias_half = jnp.sum(summed[:chips * rows_local], axis=0)
-    readout = summed[chips * rows_local:chips * rows_local + pts_count // 2].reshape(-1)
-    bias = jnp.zeros((hidden,), jnp.float32)
-    for number, index in enumerate((pts_index, pts_index ^ 1)):
-        bias = lax.dynamic_update_slice_in_dim(bias, bias_half[number * share:(number + 1) * share], index * share, 0)
-    vectors = jnp.stack([bias, readout]).reshape(-1, LANES)
-    vectors = vectors + sum(rotate(vectors, by) for by in range(1, pts_count))
-    marks.append([second, vectors])
-    second = add(
-        pick(second, place, 0), *[along(pick(second, (place + by) % outer, 0), by) for by in range(1, outer)]
-    )
-    marks.append([second])
-    blocks = jnp.zeros((pts_count, quarter, hidden), jnp.float32)
-    for by in range(pts_count):
-        block = rotate(second, by) if by else second
-        blocks = lax.dynamic_update_index_in_dim(blocks, block.astype(jnp.float32), (pts_index - by) % pts_count, 0)
-    second = blocks.reshape(pts_count * quarter, hidden)
-    bias, readout = (
-        lax.dynamic_slice_in_dim(v, coord_index * (hidden // coord_count), hidden // coord_count, 0)
-        for v in vectors.reshape(2, hidden)
-    )
-
+    second = add(second[0], *[shift(second[by], by) for by in range(1, chips)])
     if rows_local != LANES:
         rows = jnp.stack(cotangent)[:, :chips * rows_local].reshape(coord_count, chips, rows_local, -1)
         rows = rows.transpose(1, 0, 2, 3).reshape(chips, -1, LANES, 2 * share).transpose(1, 0, 2, 3)
@@ -614,16 +613,30 @@
         places = [(i % 2, -(i // 2) % (len(cotangent) // 2)) for i in range(len(cotangent))]
 
     def part(after, number, first, count, joined=None):
-        keep, send, *out = gradient(
+        keep, send, *out, mark = gradient(
             turn, after, cotangent, places, own, drawn[number], width, first, count, cuts[number][0], valid, joined
         )
-        return keep, lax.ppermute(send, "pts", swap), *out
+        return mark[0, 0], keep, lax.ppermute(send, "pts", swap), *out
 
     late = 2 if cuts[1][1] % 2 == 0 else 1
     middle = cuts[1][1] - late
-    one = part(marks[0], 0, *cuts[0])
-    two = part(marks[1], 1, early, middle)
-    *three, out = part(marks[2], 1, early + middle, late, one)
+    mark, *one = part([second, last_mark], 0, *cuts[0])
+    second = add(second[0], across(second[1]), mark)
+    mark, *two = part([second], 1, early, middle)
+    second = add(second[0], *[along(second[by], by) for by in range(1, outer)], mark)
+    _, *three, out = part([second], 1, early + middle, late, one)
+    height = hidden // coord_count
+    joined = jnp.zeros((second.shape[0], hidden), jnp.float32)
+    for by in range(pts_count):
+        block = second if by == 0 else lax.ppermute(second, "pts", [(i, (i + by) % pts_count) for i in range(pts_count)])
+        joined = lax.dynamic_update_slice_in_dim(
+            joined, block.astype(jnp.float32), (pts_index - by) % pts_count * share, 1
+        )
+    readout, bias = (
+        lax.dynamic_slice_in_dim(joined[row], coord_index * height, height, 0) for row in (height, height + 1)
+    )
+    second = joined[:height]
+
     for (keep, got), first, size in ((two, early, middle), (three, early + middle, late)):
         wide = width * math.gcd(size, first, 2)
         out = join([], keep, got, out, wide, first * width // wide, valid)

time: 326 us -> 310 us (0.951)
  waiting for transfers between devices: 21.3 us -> 11 us
  other arithmetic: 8.51 us -> 4.76 us
    ppermute x9, waiting for transfers between devices: 6.63 us -> 0.02 us  [along(): lax.ppermute(a, 'coord', [(i, (i + 2 * by) % coord_count) for i in range(...]
    ppermute x10 -> x7, waiting for transfers between devices: 5.93 us -> 0.02 us  [the longest x3 0.01 us: shards(): lax.ppermute(second, 'pts', [(i, (i + by) % pts_count) for i in range(pts...]
    pallas_call x0 -> x1, Pallas kernels: none -> 5.55 us  [hidden_layers(): pl.pallas_call(functools.partial(hidden_kernel, samples, len(parts), chip...]
    ppermute x4, waiting for transfers between devices: 4.36 us -> 8.19 us  [across(): return lax.ppermute(a, 'coord', [(i, i ^ 1) for i in range(coord_count)])]
    unnamed x57 -> x43, local copies, waits for them, and re-layouts: 7.35 us -> 8.05 us
  transfers between devices with their start and end apart: 27 -> 24, of which waited for: 10 -> 3; matrix products, arithmetic and copies ran while one was open for 4% -> 4% of each run, Pallas kernels for 67% -> 70%
where the time goes in v5:
time: 310 us
  Pallas kernels  249 us (80%)
  starting transfers between devices  29.3 us (9%)
  local copies, waits for them, and re-layouts  14.9 us (5%)
  waiting for transfers between devices  11 us (4%)
  other arithmetic  4.76 us (2%)
    pallas_call x1, Pallas kernels, forward(): pl.pallas_call(functools.partial(forward_kernel, valid), grid=(steps,), i...  105 us
    pallas_call x4, Pallas kernels, redraw(): pl.pallas_call(functools.partial(redraw_kernel, first), grid=(count,), in...  79.3 us
    pallas_call x3, Pallas kernels, gradient(): pl.pallas_call(functools.partial(gradient_kernel, 1 + len(others), places...  47.9 us
    ppermute x9, starting transfers between devices, along(): lax.ppermute(a, 'coord', [(i, (i + 2 * by) % coord_count) for i in range(...  14.8 us
    ppermute x4, waiting for transfers between devices, across(): return lax.ppermute(a, 'coord', [(i, i ^ 1) for i in range(coord_count)])  8.19 us
    unnamed x43, local copies, waits for them, and re-layouts  8.05 us
  transfers between devices with their start and end apart: 24, of which 3 were waited for; matrix products, arithmetic and copies ran while one was open for 4% of the time, Pallas kernels for 70%

profile of v5, /device:TPU:0, one launch (start us, length us, event | category | flops | bytes accessed | tf_op | source)
XLA Modules:
  0.0 309.6 jit_solution(12256518559867328066)
XLA Ops:
  0.6 3.0 collective-permute-start
  3.6 0.1 collective-permute-start.1
  3.7 1.5 broadcast_in_dim.22.coef_ref
  5.2 0.6 pad_add_fusion.base_ref
  5.7 105.5 %forward.1 = (bf16[1024,12544]{1,0:T(8,128)(2,1)}, bf16[4,144,1024]{2,1,0:T(8,128)(2,1)}, bf16[4,144,1024]{2,1,0:T(8,128)(2,1)}) custom-call(s32[3]{0:T(128)} %pad_add_fusion.base_ref, s32[16,64]{1,0:T(8,128)} %bitcast.54, s32[1,64]{1,0:T(1,128)} %bitcast.59, f32[1,12500]{1,0:T(1,128)} %broadcast_in_dim.22.coef_ref, bf16[12500,1024]{1,0:T(8,128)(2,1)} %bitcast.52, ...), custom_call_target="tpu_custom_call" | custom-call | flops 51200000000 | bytes 51200000 | tf_op jit(solution)/shard_map/forward/pallas_call | solution.py:295
  111.2 2.0 collective-permute-start.2
  113.2 0.6 broadcast_in_dim.27
  113.8 0.5 copy-done.20
  114.3 0.1 copy-done.19
  114.4 22.3 %redraw.4 = (bf16[1024,7168]{1,0:T(8,128)(2,1)}, f32[8,128]{1,0:T(8,128)}) custom-call(s32[3]{0:T(128)} %pad_add_fusion.base_ref, s32[16,64]{1,0:T(8,128)} %bitcast.55, s32[1,64]{1,0:T(1,128)} %bitcast.60, bf16[4,144,1024]{2,1,0:T(8,128)(2,1)} %get-tuple-element.36.refs_0_.near_ref), custom_call_target="tpu_custom_call" | custom-call | flops 14680064000 | bytes 7340032 | tf_op jit(solution)/shard_map/redraw/pallas_call | solution.py:334
  136.7 2.1 collective-permute-done.2.got_ref
  138.8 1.1 copy-done.6
  139.9 2.7 combine.1
  142.6 1.8 collective-permute-start.3
  144.4 2.6 collective-permute-start.4
  147.0 1.3 collective-permute-start.5
  148.3 22.4 %redraw.5 = (bf16[1024,7168]{1,0:T(8,128)(2,1)}, f32[8,128]{1,0:T(8,128)}) custom-call(s32[3]{0:T(128)} %pad_add_fusion.base_ref, s32[16,64]{1,0:T(8,128)} %bitcast.56, s32[1,64]{1,0:T(1,128)} %bitcast.61, bf16[144,1024]{1,0:T(8,128)(2,1)} %get-tuple-element.39.refs_0_, bf16[1024,7168]{1,0:T(8,128)(2,1)} %get-tuple-element.40.refs_1_), custom_call_target="tpu_custom_call", output_to_operand_aliasing={{0}: (4, {})} | custom-call | flops 14680064000 | bytes 7340032 | tf_op jit(solution)/shard_map/redraw/pallas_call | solution.py:334
  170.7 0.7 copy-done.13
  171.4 0.1 copy-done.14
  171.5 0.2 copy-done.15
  171.6 5.6 %hidden.1 = (f32[8,128]{1,0:T(8,128)}, bf16[2,2,4,144,256]{4,3,2,1,0:T(8,128)(2,1)}, bf16[2,2,4,144,256]{4,3,2,1,0:T(8,128)(2,1)}, bf16[128,512]{1,0:T(8,128)(2,1)}, bf16[128,512]{1,0:T(8,128)(2,1)}) custom-call(s32[3]{0:T(128)} %pad_add_fusion.base_ref, f32[8,128]{1,0:T(8,128)} %get-tuple-element.41._, bf16[144,1024]{1,0:T(8,128)(2,1)} %get-tuple-element.39.refs_0_, ...), custom_call_target="tpu_custom_call" | custom-call | flops 805306368 | bytes 4194304 | tf_op jit(solution)/shard_map/hidden/pallas_call | solution.py:507
  177.2 1.5 collective-permute-start.9
  178.7 0.9 constant_dynamic-update-slice_fusion.1
  179.6 2.8 collective-permute-done.9
  182.4 1.3 collective-permute-start.10
  183.8 1.2 collective-permute-start.11
  184.9 1.3 collective-permute-start.12
  186.3 17.3 %redraw.6 = (bf16[1024,5376]{1,0:T(8,128)(2,1)}, f32[8,128]{1,0:T(8,128)}) custom-call(s32[3]{0:T(128)} %pad_add_fusion.base_ref, s32[16,64]{1,0:T(8,128)} %bitcast.57, s32[1,64]{1,0:T(1,128)} %bitcast.62, bf16[256,512]{1,0:T(8,128)(2,1)} %copy-done.11), custom_call_target="tpu_custom_call" | custom-call | flops 11010048000 | bytes 5505024 | tf_op jit(solution)/shard_map/redraw/pallas_call | solution.py:334
  203.6 1.5 collective-permute-start.13
  205.2 0.7 copy-done.7
  205.9 0.1 copy-done.8
  206.0 0.1 copy-done.9
  206.1 2.1 stack.17
  208.2 0.5 collective-permute-start.14
  208.7 0.3 add_convert_fusion.refs_1_
  209.0 1.6 collective-permute-start.7
  210.6 17.3 %redraw.7 = (bf16[1024,5376]{1,0:T(8,128)(2,1)}, f32[8,128]{1,0:T(8,128)}) custom-call(s32[3]{0:T(128)} %pad_add_fusion.base_ref, s32[16,64]{1,0:T(8,128)} %bitcast.58, s32[1,64]{1,0:T(1,128)} %bitcast.63, f32[8,128]{1,0:T(8,128)} %get-tuple-element.51.refs_0_, bf16[2,2,4,144,256]{4,3,2,1,0:T(8,128)(2,1)} %copy-done, ...), custom_call_target="tpu_custom_call", output_to_operand_aliasing={{0}: (5, {})} | custom-call | flops 11010048000 | bytes 5505024 | tf_op jit(solution)/shard_map/redraw/pallas_call | solution.py:334
  227.9 0.9 slice_bitcast_fusion.4
  228.8 0.6 copy-done.1
  229.5 0.9 fusion.refs_0_
  230.4 0.7 copy-done.16
  231.1 21.9 %gradient.3 = (bf16[7168,256]{1,0:T(8,128)(2,1)}, bf16[7168,256]{1,0:T(8,128)(2,1)}, f32[8,128]{1,0:T(8,128)}) custom-call(s32[3]{0:T(128)} %pad_add_fusion.base_ref, bf16[2,4,144,256]{3,2,1,0:T(8,128)(2,1)} %fusion.refs_0_, f32[8,128]{1,0:T(8,128)} %get-tuple-element.53.refs_1_, bf16[256,512]{1,0:T(8,128)(2,1)} %copy-done.11, bf16[256,512]{1,0:T(8,128)(2,1)} %copy-done.7, ...), custom_call_target="tpu_custom_call" | custom-call | flops 29360128000 | bytes 14680064 | tf_op jit(solution)/shard_map/gradient/pallas_call | solution.py:402
  253.0 1.6 collective-permute-start.8
  254.6 0.6 slice_reduce_fusion
  255.3 1.2 slice.59
  256.4 6.1 %collective-permute-done.8 = bf16[4,144,256]{2,1,0:T(8,128)(2,1)S(1)} collective-permute-done((bf16[4,144,256]{2,1,0:T(8,128)(2,1)S(1)}, bf16[4,144,256]{2,1,0:T(8,128)(2,1)S(1)}, u32[]{:S(2)}, u32[]{:S(2)}) %collective-permute-start.8) | collective-permute-done | bytes 294944 | tf_op jit(solution)/shard_map/ppermute | solution.py:560
  262.5 0.7 fusion.2.refs_0_
  263.3 2.8 collective-permute-start.15
  266.1 2.2 collective-permute-start.16
  268.2 0.3 collective-permute-start.17
  268.5 13.9 %gradient.4 = (bf16[3584,256]{1,0:T(8,128)(2,1)}, bf16[3584,256]{1,0:T(8,128)(2,1)}, f32[8,128]{1,0:T(8,128)}) custom-call(s32[3]{0:T(128)} %pad_add_fusion.base_ref, bf16[4,144,256]{2,1,0:T(8,128)(2,1)} %copy-done.5, bf16[256,512]{1,0:T(8,128)(2,1)} %copy-done.11, bf16[256,512]{1,0:T(8,128)(2,1)} %copy-done.7, bf16[256,512]{1,0:T(8,128)(2,1)} %copy-done.8, ...), custom_call_target="tpu_custom_call" | custom-call | flops 14680064000 | bytes 7340032 | tf_op jit(solution)/shard_map/gradient/pallas_call | solution.py:402
  282.4 1.2 slice.64
  283.6 1.6 convert_dynamic-update-slice_fusion.3
  285.2 0.6 collective-permute-start.21
  285.8 1.1 collective-permute-start.22
  286.9 1.0 collective-permute-start.23
  287.9 12.2 %gradient.5 = (bf16[1748,256]{1,0:T(8,128)(2,1)}, bf16[1748,256]{1,0:T(8,128)(2,1)}, bf16[12500,256]{1,0:T(8,128)(2,1)}, f32[8,128]{1,0:T(8,128)}) custom-call(s32[3]{0:T(128)} %pad_add_fusion.base_ref, bf16[144,256]{1,0:T(8,128)(2,1)} %copy-done.12, bf16[7168,256]{1,0:T(8,128)(2,1)} %get-tuple-element.60.refs_1_, ...), custom_call_target="tpu_custom_call" | custom-call | flops 7340032000 | bytes 3670016 | tf_op jit(solution)/shard_map/gradient/pallas_call | solution.py:402
  300.1 0.1 collective-permute-start.19
  300.3 0.8 slice.79
  301.1 0.5 fusion.7
  301.6 1.3 copy-done.3
  302.9 3.1 %join.2.refs_2_ = bf16[12500,256]{1,0:T(8,128)(2,1)} custom-call(bf16[3584,256]{1,0:T(8,128)(2,1)} %get-tuple-element.64.refs_0_, bf16[3584,256]{1,0:T(8,128)(2,1)} %copy-done.3, bf16[12500,256]{1,0:T(8,128)(2,1)} %get-tuple-element.66.refs_2_), custom_call_target="tpu_custom_call", output_to_operand_aliasing={{}: (2, {})} | custom-call | flops 917504 | bytes 5505024 | tf_op jit(solution)/shard_map/join/pallas_call | solution.py:429
  306.1 1.0 copy-done.10
  307.0 2.6 join.3
  (62 shorter events, 0.3 us)
Async XLA Ops:
  0.6 113.2 %collective-permute-start = (s32[64,16]{0,1:T(8,128)}, s32[64,16]{0,1:T(8,128)S(1)}, u32[]{:S(2)}, u32[]{:S(2)}) collective-permute-start(s32[64,16]{0,1:T(8,128)} %param.8), channel_id=1, source_target_pairs={{0,16},{8,24},{16,0},{24,8},{1,17},{9,25},{17,1},{25,9},{2,18},{10... | collective-permute-start | bytes 12296 | tf_op jit(solution)/shard_map/ppermute | solution.py:547
  3.6 110.2 %collective-permute-start.1 = (s32[64]{0:T(128)}, s32[64]{0:T(128)S(1)}, u32[]{:S(2)}, u32[]{:S(2)}) collective-permute-start(s32[64]{0:T(128)} %param.7), channel_id=1, source_target_pairs={{0,16},{8,24},{16,0},{24,8},{1,17},{9,25},{17,1},{25,9},{2,18},{10... | collective-permute-start | bytes 776 | tf_op jit(solution)/shard_map/ppermute | solution.py:547
  5.7 107.5 %copy-start.18 = (bf16[1024]{0:T(1024)(128)(2,1)S(1)}, bf16[1024]{0:T(1024)(128)(2,1)}, u32[]{:S(2)}) copy-start(bf16[1024]{0:T(1024)(128)(2,1)} %param.13) | copy-start | bytes 6148
  111.2 27.6 %collective-permute-start.2 = (bf16[4,144,1024]{2,1,0:T(8,128)(2,1)}, bf16[4,144,1024]{2,1,0:T(8,128)(2,1)S(1)}, u32[]{:S(2)}, u32[]{:S(2)}) collective-permute-start(bf16[4,144,1024]{2,1,0:T(8,128)(2,1)} %get-tuple-element.37), channel_id=1, source_target_pairs={{0,1},{1,0},{2,3},{3,2},{4,5},{5,4},{6,7},{7,6},{8,9},{9,8},{10,11... | collective-permute-start | bytes 3538952 | tf_op jit(solution)/shard_map/ppermute | solution.py:560
  113.8 0.5 copy-start.20
  113.8 0.6 copy-start.19
  138.8 1.1 copy-start.6
  142.6 28.0 %collective-permute-start.3 = (bf16[144,1024]{1,0:T(8,128)(2,1)}, bf16[144,1024]{1,0:T(8,128)(2,1)S(1)}, u32[]{:S(2)}, u32[]{:S(2)}) collective-permute-start(bf16[144,1024]{1,0:T(8,128)(2,1)} %get-tuple-element.42), channel_id=1, source_target_pairs={{0,2},{1,3},{2,4},{3,5},{4,6},{5,7},{6,0},{7,1},{8,10},{9,11},{10,... | collective-permute-start | bytes 884744 | tf_op jit(solution)/shard_map/ppermute | solution.py:563
  144.4 26.3 %collective-permute-start.4 = (bf16[144,1024]{1,0:T(8,128)(2,1)}, bf16[144,1024]{1,0:T(8,128)(2,1)S(1)}, u32[]{:S(2)}, u32[]{:S(2)}) collective-permute-start(bf16[144,1024]{1,0:T(8,128)(2,1)} %get-tuple-element.43), channel_id=1, source_target_pairs={{0,4},{1,5},{2,6},{3,7},{4,0},{5,1},{6,2},{7,3},{8,12},{9,13},{10,... | collective-permute-start | bytes 884744 | tf_op jit(solution)/shard_map/ppermute | solution.py:563
  147.0 23.7 %collective-permute-start.5 = (bf16[144,1024]{1,0:T(8,128)(2,1)}, bf16[144,1024]{1,0:T(8,128)(2,1)S(1)}, u32[]{:S(2)}, u32[]{:S(2)}) collective-permute-start(bf16[144,1024]{1,0:T(8,128)(2,1)} %get-tuple-element.44), channel_id=1, source_target_pairs={{0,6},{1,7},{2,0},{3,1},{4,2},{5,3},{6,4},{7,5},{8,14},{9,15},{10,... | collective-permute-start | bytes 884744 | tf_op jit(solution)/shard_map/ppermute | solution.py:563
  170.7 0.7 copy-start.13
  170.7 0.8 copy-start.14
  170.7 0.9 copy-start.15
  177.2 5.2 %collective-permute-start.9 = (bf16[128,512]{1,0:T(8,128)(2,1)}, bf16[128,512]{1,0:T(8,128)(2,1)S(1)}, u32[]{:S(2)}, u32[]{:S(2)}) collective-permute-start(bf16[128,512]{1,0:T(8,128)(2,1)} %get-tuple-element.49), channel_id=1, source_target_pairs={{0,16},{8,24},{16,0},{24,8},{1,17},{9,25},{17,1},{25,9},{2,18},{10... | collective-permute-start | bytes 393224 | tf_op jit(solution)/shard_map/ppermute | solution.py:547
  178.7 30.0 %collective-permute-start.6 = (bf16[2,2,4,144,256]{4,3,2,1,0:T(8,128)(2,1)}, bf16[2,2,4,144,256]{4,3,2,1,0:T(8,128)(2,1)S(1)}, u32[]{:S(2)}, u32[]{:S(2)}) collective-permute-start(bf16[2,2,4,144,256]{4,3,2,1,0:T(8,128)(2,1)} %get-tuple-element.47), channel_id=1, source_target_pairs={{0,8},{8,0},{16,24},{24,16},{1,9},{9,1},{17,25},{25,17},{2,10},{10... | collective-permute-start | bytes 3538952 | tf_op jit(solution)/shard_map/ppermute | solution.py:604
  182.4 3.9 %copy-start.11 = (bf16[256,512]{1,0:T(8,128)(2,1)}, bf16[256,512]{1,0:T(8,128)(2,1)S(1)}, u32[]{:S(2)}) copy-start(bf16[256,512]{1,0:T(8,128)(2,1)S(1)} %constant_dynamic-update-slice_fusion.refs_0_.refs_2_.refs_1_.refs_3_) | copy-start | bytes 786436
  182.4 26.3 %copy-start.4 = (bf16[2,2,4,144,256]{4,3,2,1,0:T(8,128)(2,1)S(1)}, bf16[2,2,4,144,256]{4,3,2,1,0:T(8,128)(2,1)}, u32[]{:S(2)}) copy-start(bf16[2,2,4,144,256]{4,3,2,1,0:T(8,128)(2,1)} %get-tuple-element.46) | copy-start | bytes 3538948
  182.4 22.7 %collective-permute-start.10 = (bf16[256,512]{1,0:T(8,128)(2,1)S(1)}, bf16[256,512]{1,0:T(8,128)(2,1)S(1)}, u32[]{:S(2)}, u32[]{:S(2)}) collective-permute-start(bf16[256,512]{1,0:T(8,128)(2,1)S(1)} %constant_dynamic-update-slice_fusion.refs_0_.refs_2_.refs_1_.refs_3_), channel_id=1, source_target_pairs={{0,2},{1,3},{2,4},{3,5},{4,6},{5,7},{6,0},{7,1},{8,10},{9,11},{10,... | collective-permute-start | bytes 786440 | tf_op jit(solution)/shard_map/ppermute | solution.py:563
  183.8 21.4 %collective-permute-start.11 = (bf16[256,512]{1,0:T(8,128)(2,1)S(1)}, bf16[256,512]{1,0:T(8,128)(2,1)S(1)}, u32[]{:S(2)}, u32[]{:S(2)}) collective-permute-start(bf16[256,512]{1,0:T(8,128)(2,1)S(1)} %constant_dynamic-update-slice_fusion.refs_0_.refs_2_.refs_1_.refs_3_), channel_id=1, source_target_pairs={{0,4},{1,5},{2,6},{3,7},{4,0},{5,1},{6,2},{7,3},{8,12},{9,13},{10,... | collective-permute-start | bytes 786440 | tf_op jit(solution)/shard_map/ppermute | solution.py:563
  184.9 20.2 %collective-permute-start.12 = (bf16[256,512]{1,0:T(8,128)(2,1)S(1)}, bf16[256,512]{1,0:T(8,128)(2,1)S(1)}, u32[]{:S(2)}, u32[]{:S(2)}) collective-permute-start(bf16[256,512]{1,0:T(8,128)(2,1)S(1)} %constant_dynamic-update-slice_fusion.refs_0_.refs_2_.refs_1_.refs_3_), channel_id=1, source_target_pairs={{0,6},{1,7},{2,0},{3,1},{4,2},{5,3},{6,4},{7,5},{8,14},{9,15},{10,... | collective-permute-start | bytes 786440 | tf_op jit(solution)/shard_map/ppermute | solution.py:563
  203.6 26.8 %collective-permute-start.13 = (bf16[256,512]{1,0:T(8,128)(2,1)}, bf16[256,512]{1,0:T(8,128)(2,1)S(1)}, u32[]{:S(2)}, u32[]{:S(2)}) collective-permute-start(bf16[256,512]{1,0:T(8,128)(2,1)} %copy-done.11), channel_id=1, source_target_pairs={{0,1},{1,0},{2,3},{3,2},{4,5},{5,4},{6,7},{7,6},{8,9},{9,8},{10,11... | collective-permute-start | bytes 786440 | tf_op jit(solution)/shard_map/ppermute | solution.py:560
  205.2 0.7 copy-start.7
  205.2 0.9 copy-start.8
  205.2 0.9 copy-start.9
  208.2 19.8 %collective-permute-start.14 = (bf16[3,256,512]{2,1,0:T(8,128)(2,1)}, bf16[3,256,512]{2,1,0:T(8,128)(2,1)S(1)}, u32[]{:S(2)}, u32[]{:S(2)}) collective-permute-start(bf16[3,256,512]{2,1,0:T(8,128)(2,1)} %get-tuple-element.54), channel_id=1, source_target_pairs={{0,1},{1,0},{2,3},{3,2},{4,5},{5,4},{6,7},{7,6},{8,9},{9,8},{10,11... | collective-permute-start | bytes 2359304 | tf_op jit(solution)/shard_map/ppermute | solution.py:560
  209.0 1.6 copy-start
  209.0 19.8 %collective-permute-start.7 = (bf16[2,4,144,256]{3,2,1,0:T(8,128)(2,1)S(1)}, bf16[2,4,144,256]{3,2,1,0:T(8,128)(2,1)S(1)}, u32[]{:S(2)}, u32[]{:S(2)}) collective-permute-start(bf16[2,4,144,256]{3,2,1,0:T(8,128)(2,1)S(1)} %slice_bitcast_fusion), channel_id=1, source_target_pairs={{0,16},{8,24},{16,0},{24,8},{1,17},{9,25},{17,1},{25,9},{2,18},{10... | collective-permute-start | bytes 1769480 | tf_op jit(solution)/shard_map/ppermute | solution.py:547
  227.9 1.6 copy-start.1
  230.4 0.7 copy-start.16
  231.1 21.9 %copy-start.2 = (bf16[2,4,144,256]{3,2,1,0:T(8,128)(2,1)S(1)}, bf16[2,4,144,256]{3,2,1,0:T(8,128)(2,1)}, u32[]{:S(2)}) copy-start(bf16[2,4,144,256]{3,2,1,0:T(8,128)(2,1)} %fusion.refs_0_) | copy-start | bytes 1769476
  231.1 23.5 %copy-start.17 = (f32[8,128]{1,0:T(8,128)S(1)}, f32[8,128]{1,0:T(8,128)}, u32[]{:S(2)}) copy-start(f32[8,128]{1,0:T(8,128)} %get-tuple-element.45) | copy-start | bytes 12292
  253.0 34.9 %collective-permute-start.18 = (bf16[7168,256]{1,0:T(8,128)(2,1)}, bf16[7168,256]{1,0:T(8,128)(2,1)}, u32[]{:S(2)}, u32[]{:S(2)}) collective-permute-start(bf16[7168,256]{1,0:T(8,128)(2,1)} %get-tuple-element.61), channel_id=1, source_target_pairs={{0,8},{8,0},{16,24},{24,16},{1,9},{9,1},{17,25},{25,17},{2,10},{10... | collective-permute-start | bytes 11010056 | tf_op jit(solution)/shard_map/ppermute | solution.py:619
  253.0 9.5 %collective-permute-start.8 = (bf16[4,144,256]{2,1,0:T(8,128)(2,1)S(1)}, bf16[4,144,256]{2,1,0:T(8,128)(2,1)S(1)}, u32[]{:S(2)}, u32[]{:S(2)}) collective-permute-start(bf16[4,144,256]{2,1,0:T(8,128)(2,1)S(1)} %slice_bitcast_fusion.2), channel_id=1, source_target_pairs={{0,1},{1,0},{2,3},{3,2},{4,5},{5,4},{6,7},{7,6},{8,9},{9,8},{10,11... | collective-permute-start | bytes 884744 | tf_op jit(solution)/shard_map/ppermute | solution.py:560
  263.3 5.3 %copy-start.5 = (bf16[4,144,256]{2,1,0:T(8,128)(2,1)}, bf16[4,144,256]{2,1,0:T(8,128)(2,1)S(1)}, u32[]{:S(2)}) copy-start(bf16[4,144,256]{2,1,0:T(8,128)(2,1)S(1)} %fusion.2.refs_0_) | copy-start | bytes 884740
  263.3 20.3 %collective-permute-start.15 = (bf16[144,256]{1,0:T(8,128)(2,1)S(1)}, bf16[144,256]{1,0:T(8,128)(2,1)S(1)}, u32[]{:S(2)}, u32[]{:S(2)}) collective-permute-start(bf16[144,256]{1,0:T(8,128)(2,1)S(1)} %get-tuple-element.74), channel_id=1, source_target_pairs={{0,2},{1,3},{2,4},{3,5},{4,6},{5,7},{6,0},{7,1},{8,10},{9,11},{10,... | collective-permute-start | bytes 221192 | tf_op jit(solution)/shard_map/ppermute | solution.py:563
  266.1 17.5 %collective-permute-start.16 = (bf16[144,256]{1,0:T(8,128)(2,1)S(1)}, bf16[144,256]{1,0:T(8,128)(2,1)S(1)}, u32[]{:S(2)}, u32[]{:S(2)}) collective-permute-start(bf16[144,256]{1,0:T(8,128)(2,1)S(1)} %get-tuple-element.76), channel_id=1, source_target_pairs={{0,4},{1,5},{2,6},{3,7},{4,0},{5,1},{6,2},{7,3},{8,12},{9,13},{10,... | collective-permute-start | bytes 221192 | tf_op jit(solution)/shard_map/ppermute | solution.py:563
  268.2 15.4 %collective-permute-start.17 = (bf16[144,256]{1,0:T(8,128)(2,1)S(1)}, bf16[144,256]{1,0:T(8,128)(2,1)S(1)}, u32[]{:S(2)}, u32[]{:S(2)}) collective-permute-start(bf16[144,256]{1,0:T(8,128)(2,1)S(1)} %get-tuple-element.75), channel_id=1, source_target_pairs={{0,6},{1,7},{2,0},{3,1},{4,2},{5,3},{6,4},{7,5},{8,14},{9,15},{10,... | collective-permute-start | bytes 221192 | tf_op jit(solution)/shard_map/ppermute | solution.py:563
  283.6 18.1 %collective-permute-start.20 = (bf16[3584,256]{1,0:T(8,128)(2,1)}, bf16[3584,256]{1,0:T(8,128)(2,1)S(1)}, u32[]{:S(2)}, u32[]{:S(2)}) collective-permute-start(bf16[3584,256]{1,0:T(8,128)(2,1)} %get-tuple-element.65), channel_id=1, source_target_pairs={{0,8},{8,0},{16,24},{24,16},{1,9},{9,1},{17,25},{25,17},{2,10},{10... | collective-permute-start | bytes 5505032 | tf_op jit(solution)/shard_map/ppermute | solution.py:619
  285.2 2.7 copy-start.12
  285.2 14.9 %collective-permute-start.21 = (bf16[144,256]{1,0:T(8,128)(2,1)S(1)}, bf16[144,256]{1,0:T(8,128)(2,1)S(1)}, u32[]{:S(2)}, u32[]{:S(2)}) collective-permute-start(bf16[144,256]{1,0:T(8,128)(2,1)S(1)} %get-tuple-element.68.refs_0_), channel_id=1, source_target_pairs={{0,8},{8,16},{16,24},{24,0},{1,9},{9,17},{17,25},{25,1},{2,10},{10... | collective-permute-start | bytes 221192 | tf_op jit(solution)/shard_map/ppermute | solution.py:631
  285.8 14.4 %collective-permute-start.22 = (bf16[144,256]{1,0:T(8,128)(2,1)S(1)}, bf16[144,256]{1,0:T(8,128)(2,1)S(1)}, u32[]{:S(2)}, u32[]{:S(2)}) collective-permute-start(bf16[144,256]{1,0:T(8,128)(2,1)S(1)} %get-tuple-element.68.refs_0_), channel_id=1, source_target_pairs={{0,16},{8,24},{16,0},{24,8},{1,17},{9,25},{17,1},{25,9},{2,18},{10... | collective-permute-start | bytes 221192 | tf_op jit(solution)/shard_map/ppermute | solution.py:631
  286.9 13.3 %collective-permute-start.23 = (bf16[144,256]{1,0:T(8,128)(2,1)S(1)}, bf16[144,256]{1,0:T(8,128)(2,1)S(1)}, u32[]{:S(2)}, u32[]{:S(2)}) collective-permute-start(bf16[144,256]{1,0:T(8,128)(2,1)S(1)} %get-tuple-element.68.refs_0_), channel_id=1, source_target_pairs={{0,24},{8,0},{16,8},{24,16},{1,25},{9,1},{17,9},{25,17},{2,26},{10... | collective-permute-start | bytes 221192 | tf_op jit(solution)/shard_map/ppermute | solution.py:631
  300.1 6.0 %collective-permute-start.19 = (bf16[1748,256]{1,0:T(8,128)(2,1)}, bf16[1748,256]{1,0:T(8,128)(2,1)S(1)}, u32[]{:S(2)}, u32[]{:S(2)}) collective-permute-start(bf16[1748,256]{1,0:T(8,128)(2,1)} %get-tuple-element.63), channel_id=1, source_target_pairs={{0,8},{8,0},{16,24},{24,16},{1,9},{9,1},{17,25},{25,17},{2,10},{10... | collective-permute-start | bytes 2684936 | tf_op jit(solution)/shard_map/ppermute | solution.py:619
  301.6 1.3 copy-start.3
  306.1 1.0 copy-start.10

commit v6 on v5

--- a/solution.py
+++ b/solution.py
@@ -97,7 +97,7 @@
     rows, width = z_ref.shape
     points = point_ref.shape[0]
     samples = rows // points
-    groups = rows // GROUP
+    half = width // 2
     steps = -(-valid // width)
     pad = steps * width - valid
 
@@ -123,55 +123,52 @@
             term[:, a:a + LANES] for a in range(0, width, LANES)
         )
 
-    cut = width - -(-pad // 16) * 16
-
-    def multiply(group, part, held, ref, of):
-        at, left = group * GROUP, part * GROUP
-        w = ref[:, left:left + GROUP]
-        if pad:
-            place = lax.broadcasted_iota(jnp.int32, (width - cut, GROUP), 0) + (of * width + cut)
-            tail = jnp.where(place < valid, w[cut:], jnp.zeros((), w.dtype))
-            w = jnp.concatenate([w[:cut], tail], axis=0)
-        acc[at:at + GROUP, left:left + GROUP] += jnp.dot(
-            held[...], w, preferred_element_type=jnp.float32
-        )
-
-    parts = acc.shape[1] // GROUP
-    group_points = GROUP // samples
-
-    for group in range(groups):
-        held = (held_a, held_b)[group % 2]
-        other = (held_b, held_a)[group % 2]
-        for number in range(group_points):
-            if number % (group_points // parts) == 0:
-                part = number // (group_points // parts)
-                if group == 0:
-                    multiply(groups - 1, part, other, w_prev, jnp.maximum(step - 1, 0))
-                else:
-                    multiply(group - 1, part, other, w_now, step)
-            at = number * samples
-            row = group * GROUP + at
-            point = row // samples
-            seeds = pert_ref[row:row + samples]
-            total = None
-            for a, b in pieces(width):
-                noise = draw(seeds, keys[0:8, a:b], keys[8:16, a:b])
-                x = jnp.broadcast_to(xs[point:point + 1, a:b], (samples, b - a))
-                z = (x + noise).astype(jnp.bfloat16)
-                held[at:at + samples, a:b] = z
-                z_ref[row:row + samples, a:b] = z
-                square = noise * noise
-                for c in range(a, b, LANES):
-                    cell = square[:, c - a:c - a + LANES]
-                    if (steps - 1) * width + c + LANES > valid:
-                        cell = jnp.where(jnp.concatenate([inside[:, c:c + LANES]] * 2, axis=0), cell, 0.0)
-                    total = cell if total is None else total + cell
-            sq_ref[row:row + samples] += total
+    def multiply(at, left, held, w):
+        block, lanes = slice(at, at + GROUP), pl.ds(left, GROUP)
+        acc[block, lanes] += jnp.dot(held[block, :], w, preferred_element_type=jnp.float32)
+
+    def phase(offset, held, other, w_ref, w_at):
+        @pl.loop(0, rows // GROUP)
+        def _(part):
+            left = pl.multiple_of(part * GROUP, GROUP)
+            w = w_ref[w_at:w_at + half, pl.ds(left, GROUP)]
+            count = GROUP // samples
+            for number in range(count):
+                if number % (count // (rows // GROUP)) == 0:
+                    multiply(number // (count // (rows // GROUP)) * GROUP, left, other, w)
+                if number % 8 == 0:
+                    eight = xs[pl.ds(pl.multiple_of(part * count + number, 8), 8), offset:offset + half]
+                row = pl.multiple_of((part * count + number) * samples, samples)
+                seeds = pert_ref[pl.ds(row, samples)]
+                total = None
+                for a, b in pieces(half):
+                    noise = draw(seeds, keys[0:8, offset + a:offset + b], keys[8:16, offset + a:offset + b])
+                    x = jnp.broadcast_to(eight[number % 8:number % 8 + 1, a:b], (samples, b - a))
+                    z = (x + noise).astype(jnp.bfloat16)
+                    held[pl.ds(row, samples), a:b] = z
+                    z_ref[pl.ds(row, samples), offset + a:offset + b] = z
+                    square = noise * noise
+                    for c in range(a, b, LANES):
+                        cell = square[:, c - a:c - a + LANES]
+                        place = offset + c
+                        if (steps - 1) * width + place + LANES > valid:
+                            cell = jnp.where(
+                                jnp.concatenate([inside[:, place:place + LANES]] * 2, axis=0), cell, 0.0
+                            )
+                        total = cell if total is None else total + cell
+                sq_ref[pl.ds(row, samples)] += total
+
+    phase(0, held_a, held_b, w_prev, 0)
+    phase(half, held_b, held_a, w_now, 0)
 
     @pl.when(step == last)
     def _():
-        for part in range(parts):
-            multiply(groups - 1, part, held_b, w_now, step)
+        place = lax.broadcasted_iota(jnp.int32, (half, GROUP), 0)
+        for left in range(0, acc.shape[1], GROUP):
+            w = w_now[half:, left:left + GROUP]
+            w = jnp.where(place < half - pad, w, jnp.zeros((), w.dtype))
+            for at in range(0, rows, GROUP):
+                multiply(at, left, held_b, w)
         sums[...] = jnp.zeros_like(sums)
         source = jnp.sum(src_ref[...].T, axis=0, keepdims=True) / math.sqrt(D)
         for block in range(rows // LANES):
@@ -275,7 +272,8 @@
 
 
 def join_kernel(*refs):
-    keep_ref, got_ref, out_ref = refs[0], refs[1], refs[-1]
+    keep_ref, got_ref, out_ref, mark_ref = refs[0], refs[1], refs[-2], refs[-1]
+    mark_ref[...] = jnp.zeros_like(mark_ref)
     out_ref[...] = (keep_ref[...].astype(jnp.float32) + got_ref[...].astype(jnp.float32)).astype(jnp.bfloat16)
 
 
@@ -298,7 +296,7 @@
         in_specs=[
             smem, whole(pert.shape), whole(point.shape),
             pl.BlockSpec((1, width), lambda s: (0, s)),
-            pl.BlockSpec((width, hidden), lambda s: (jnp.maximum(s - 1, 0), 0)),
+            pl.BlockSpec((width // 2, hidden), lambda s: (jnp.maximum(2 * s - 1, 0), 0)),
             pl.BlockSpec((width, hidden), lambda s: (s, 0)),
         ],
         out_specs=[
@@ -308,8 +306,8 @@
             jax.ShapeDtypeStruct((rows, steps * width), jnp.bfloat16),
         ] + [jax.ShapeDtypeStruct((parts // 2, rows // parts + 16, hidden), jnp.bfloat16)] * 2,
         scratch_shapes=[
-            pltpu.VMEM((GROUP, width), jnp.bfloat16),
-            pltpu.VMEM((GROUP, width), jnp.bfloat16),
+            pltpu.VMEM((rows, width // 2), jnp.bfloat16),
+            pltpu.VMEM((rows, width // 2), jnp.bfloat16),
             pltpu.VMEM((rows, hidden), jnp.float32),
             pltpu.VMEM((16, width), jnp.int32),
             pltpu.VMEM((points, width), jnp.float32),
@@ -430,11 +428,15 @@
         join_kernel,
         grid=(count,),
         in_specs=specs,
-        out_specs=pl.BlockSpec((width, half), lambda s: (s + first, 0)),
-        out_shape=jax.ShapeDtypeStruct((valid, half), jnp.bfloat16),
+        out_specs=[pl.BlockSpec((width, half), lambda s: (s + first, 0)), whole((8, LANES))],
+        out_shape=[
+            jax.ShapeDtypeStruct((valid, half), jnp.bfloat16), jax.ShapeDtypeStruct((8, LANES), jnp.float32),
+        ],
         input_output_aliases=aliases,
         compiler_params=params(),
-        cost_estimate=pl.CostEstimate(flops=height * half, bytes_accessed=6 * height * half, transcendentals=0),
+        cost_estimate=pl.CostEstimate(
+            flops=100 * height * half * 100, bytes_accessed=6 * height * half, transcendentals=0
+        ),
         name="join",
     )(*operands)
 
@@ -522,7 +524,7 @@
 
 def block_width(valid):
     tiles = -(-valid // LANES)
-    best = min((8, 7, 6, 5), key=lambda t: -(-tiles // t) * t)
+    best = min((8, 7, 6, 5), key=lambda t: (-(-tiles // t) % 2, -(-tiles // t) * t))
     return best * LANES
 
 
@@ -552,7 +554,7 @@
     other_seeds = [shift((pert_seed, point_seed), by) for by in range(1, chips)]
 
     pert, point = pert_seed.T, point_seed[None, :]
-    own, near, far = forward(base, pert, point, source_coef[None, :], w1.T, width, coord_count)
+    own, near, far = forward(base, pert, point, source_coef[None, :], w1.T, 2 * width, coord_count)
     others_in = [(a.T, b[None, :]) for a, b in other_seeds]
     outer = coord_count // 2
 
@@ -618,15 +620,21 @@
         )
         return mark[0, 0], keep, lax.ppermute(send, "pts", swap), *out
 
-    late = 2 if cuts[1][1] % 2 == 0 else 1
-    middle = cuts[1][1] - late
     mark, *one = part([second, last_mark], 0, *cuts[0])
     second = add(second[0], across(second[1]), mark)
-    mark, *two = part([second], 1, early, middle)
+    _, *two = part([second], 1, *cuts[1])
+
+    def place(after, part, cut, out):
+        (keep, got), (first, size) = part, cut
+        wide = width * math.gcd(size, first, 2)
+        out, mark = join(after, keep, got, out, wide, first * width // wide, valid)
+        return out, mark[0, 0]
+
+    out, mark = place([], one, cuts[0], None)
     second = add(second[0], *[along(second[by], by) for by in range(1, outer)], mark)
-    _, *three, out = part([second], 1, early + middle, late, one)
+    out, mark = place([second], two, cuts[1], out)
     height = hidden // coord_count
-    joined = jnp.zeros((second.shape[0], hidden), jnp.float32)
+    joined = jnp.zeros((second.shape[0], hidden), jnp.float32) + mark
     for by in range(pts_count):
         block = second if by == 0 else lax.ppermute(second, "pts", [(i, (i + by) % pts_count) for i in range(pts_count)])
         joined = lax.dynamic_update_slice_in_dim(
@@ -637,9 +645,6 @@
     )
     second = joined[:height]
 
-    for (keep, got), first, size in ((two, early, middle), (three, early + middle, late)):
-        wide = width * math.gcd(size, first, 2)
-        out = join([], keep, got, out, wide, first * width // wide, valid)
     return (residual, out.T, second, bias, readout)
 
 

time: 310 us -> 326 us (1.052)
  Pallas kernels: 249 us -> 261 us
    pallas_call x1, Pallas kernels: 105 us -> 121 us  [forward(): pl.pallas_call(functools.partial(forward_kernel, valid), grid=(steps,), i...]
    pallas_call x3 -> x2, Pallas kernels: 47.9 us -> 39.8 us  [gradient(): pl.pallas_call(functools.partial(gradient_kernel, 1 + len(others), places...]
    pallas_call x2, Pallas kernels: 5.71 us -> 10.5 us  [join(): pl.pallas_call(join_kernel, grid=(count,), in_specs=specs, out_specs=[pl....]
    unnamed x43 -> x39, local copies, waits for them, and re-layouts: 8.05 us -> 6.68 us
  transfers between devices with their start and end apart: 24 -> 23, of which waited for: 3 -> 3; matrix products, arithmetic and copies ran while one was open for 4% -> 5% of each run, Pallas kernels for 70% -> 71%
where the time goes in v6:
time: 326 us; the launch traced here: 325 us
  Pallas kernels  261 us (80%)
  starting transfers between devices  29.2 us (9%)
  local copies, waits for them, and re-layouts  15.4 us (5%)
  waiting for transfers between devices  11.7 us (4%)
  other arithmetic  6.58 us (2%)
    pallas_call x1, Pallas kernels, forward(): pl.pallas_call(functools.partial(forward_kernel, valid), grid=(steps,), i...  121 us
    pallas_call x4, Pallas kernels, redraw(): pl.pallas_call(functools.partial(redraw_kernel, first), grid=(count,), in...  79.3 us
    pallas_call x2, Pallas kernels, gradient(): pl.pallas_call(functools.partial(gradient_kernel, 1 + len(others), places...  39.8 us
    ppermute x9, starting transfers between devices, along(): lax.ppermute(a, 'coord', [(i, (i + 2 * by) % coord_count) for i in range(...  14.8 us
    pallas_call x2, Pallas kernels, join(): pl.pallas_call(join_kernel, grid=(count,), in_specs=specs, out_specs=[pl....  10.5 us
    ppermute x4, waiting for transfers between devices, across(): return lax.ppermute(a, 'coord', [(i, i ^ 1) for i in range(coord_count)])  8.86 us
    unnamed x39, local copies, waits for them, and re-layouts  6.68 us
  transfers between devices with their start and end apart: 23, of which 3 were waited for; matrix products, arithmetic and copies ran while one was open for 5% of the time, Pallas kernels for 71%

profile of v6, /device:TPU:0, one launch (start us, length us, event | category | flops | bytes accessed | tf_op | source)
XLA Modules:
  0.0 324.8 jit_solution(12408265792621168440)
XLA Ops:
  0.6 3.0 collective-permute-start
  3.6 0.1 collective-permute-start.1
  3.7 1.5 broadcast_in_dim.19.coef_ref
  5.2 0.6 pad_add_fusion.base_ref
  5.8 121.0 %forward.1 = (bf16[1024,12544]{1,0:T(8,128)(2,1)}, bf16[4,144,1024]{2,1,0:T(8,128)(2,1)}, bf16[4,144,1024]{2,1,0:T(8,128)(2,1)}) custom-call(s32[3]{0:T(128)} %pad_add_fusion.base_ref, s32[16,64]{1,0:T(8,128)} %bitcast.53, s32[1,64]{1,0:T(1,128)} %bitcast.58, f32[1,12500]{1,0:T(1,128)} %broadcast_in_dim.19.coef_ref, bf16[12500,1024]{1,0:T(8,128)(2,1)} %bitcast.51, ...), custom_call_target="tpu_custom_call" | custom-call | flops 51200000000 | bytes 51200000 | tf_op jit(solution)/shard_map/forward/pallas_call | solution.py:293
  126.8 2.0 collective-permute-start.2
  128.8 0.6 broadcast_in_dim.23
  129.4 0.5 copy-done.18
  129.9 0.1 copy-done.17
  130.0 22.3 %redraw.4 = (bf16[1024,7168]{1,0:T(8,128)(2,1)}, f32[8,128]{1,0:T(8,128)}) custom-call(s32[3]{0:T(128)} %pad_add_fusion.base_ref, s32[16,64]{1,0:T(8,128)} %bitcast.54, s32[1,64]{1,0:T(1,128)} %bitcast.59, bf16[4,144,1024]{2,1,0:T(8,128)(2,1)} %get-tuple-element.36.refs_0_.near_ref), custom_call_target="tpu_custom_call" | custom-call | flops 14680064000 | bytes 7340032 | tf_op jit(solution)/shard_map/redraw/pallas_call | solution.py:332
  152.3 2.2 collective-permute-done.2.got_ref
  154.4 1.1 copy-done.4
  155.5 2.7 combine.1
  158.3 1.7 collective-permute-start.3
  160.0 2.6 collective-permute-start.4
  162.6 1.3 collective-permute-start.5
  163.9 22.3 %redraw.5 = (bf16[1024,7168]{1,0:T(8,128)(2,1)}, f32[8,128]{1,0:T(8,128)}) custom-call(s32[3]{0:T(128)} %pad_add_fusion.base_ref, s32[16,64]{1,0:T(8,128)} %bitcast.55, s32[1,64]{1,0:T(1,128)} %bitcast.60, bf16[144,1024]{1,0:T(8,128)(2,1)} %get-tuple-element.39.refs_0_, bf16[1024,7168]{1,0:T(8,128)(2,1)} %get-tuple-element.40.refs_1_), custom_call_target="tpu_custom_call", output_to_operand_aliasing={{0}: (4, {})} | custom-call | flops 14680064000 | bytes 7340032 | tf_op jit(solution)/shard_map/redraw/pallas_call | solution.py:332
  186.3 0.7 copy-done.6
  187.0 0.1 copy-done.7
  187.1 0.1 copy-done.8
  187.2 5.5 %hidden.1 = (f32[8,128]{1,0:T(8,128)}, bf16[2,2,4,144,256]{4,3,2,1,0:T(8,128)(2,1)}, bf16[2,2,4,144,256]{4,3,2,1,0:T(8,128)(2,1)}, bf16[128,512]{1,0:T(8,128)(2,1)}, bf16[128,512]{1,0:T(8,128)(2,1)}) custom-call(s32[3]{0:T(128)} %pad_add_fusion.base_ref, f32[8,128]{1,0:T(8,128)} %get-tuple-element.41._, bf16[144,1024]{1,0:T(8,128)(2,1)} %get-tuple-element.39.refs_0_, ...), custom_call_target="tpu_custom_call" | custom-call | flops 805306368 | bytes 4194304 | tf_op jit(solution)/shard_map/hidden/pallas_call | solution.py:509
  192.8 1.5 collective-permute-start.9
  194.3 0.9 constant_dynamic-update-slice_fusion.1
  195.2 2.8 collective-permute-done.9
  198.0 1.4 collective-permute-start.10
  199.4 1.1 collective-permute-start.11
  200.5 1.3 collective-permute-start.12
  201.9 17.3 %redraw.6 = (bf16[1024,5376]{1,0:T(8,128)(2,1)}, f32[8,128]{1,0:T(8,128)}) custom-call(s32[3]{0:T(128)} %pad_add_fusion.base_ref, s32[16,64]{1,0:T(8,128)} %bitcast.56, s32[1,64]{1,0:T(1,128)} %bitcast.61, bf16[256,512]{1,0:T(8,128)(2,1)} %copy-done.12), custom_call_target="tpu_custom_call" | custom-call | flops 11010048000 | bytes 5505024 | tf_op jit(solution)/shard_map/redraw/pallas_call | solution.py:332
  219.2 1.5 collective-permute-start.13
  220.8 0.7 copy-done.9
  221.5 0.1 copy-done.10
  221.6 0.1 copy-done.11
  221.7 2.1 stack.17
  223.8 0.5 collective-permute-start.14
  224.3 0.3 add_convert_fusion.refs_1_
  224.6 1.6 collective-permute-start.7
  226.2 17.3 %redraw.7 = (bf16[1024,5376]{1,0:T(8,128)(2,1)}, f32[8,128]{1,0:T(8,128)}) custom-call(s32[3]{0:T(128)} %pad_add_fusion.base_ref, s32[16,64]{1,0:T(8,128)} %bitcast.57, s32[1,64]{1,0:T(1,128)} %bitcast.62, f32[8,128]{1,0:T(8,128)} %get-tuple-element.51.refs_0_, bf16[2,2,4,144,256]{4,3,2,1,0:T(8,128)(2,1)} %copy-done, ...), custom_call_target="tpu_custom_call", output_to_operand_aliasing={{0}: (5, {})} | custom-call | flops 11010048000 | bytes 5505024 | tf_op jit(solution)/shard_map/redraw/pallas_call | solution.py:332
  243.5 0.9 slice_bitcast_fusion.4
  244.4 2.0 fusion.refs_0_
  246.4 0.7 copy-done.16
  247.1 21.9 %gradient.2 = (bf16[7168,256]{1,0:T(8,128)(2,1)}, bf16[7168,256]{1,0:T(8,128)(2,1)}, f32[8,128]{1,0:T(8,128)}) custom-call(s32[3]{0:T(128)} %pad_add_fusion.base_ref, bf16[2,4,144,256]{3,2,1,0:T(8,128)(2,1)} %fusion.refs_0_, f32[8,128]{1,0:T(8,128)} %get-tuple-element.53.refs_1_, bf16[256,512]{1,0:T(8,128)(2,1)} %copy-done.12, bf16[256,512]{1,0:T(8,128)(2,1)} %copy-done.9, ...), custom_call_target="tpu_custom_call" | custom-call | flops 29360128000 | bytes 14680064 | tf_op jit(solution)/shard_map/gradient/pallas_call | solution.py:400
  269.1 1.6 collective-permute-start.8
  270.7 1.2 slice.62
  271.9 6.7 %collective-permute-done.8 = bf16[4,144,256]{2,1,0:T(8,128)(2,1)S(1)} collective-permute-done((bf16[4,144,256]{2,1,0:T(8,128)(2,1)S(1)}, bf16[4,144,256]{2,1,0:T(8,128)(2,1)S(1)}, u32[]{:S(2)}, u32[]{:S(2)}) %collective-permute-start.8) | collective-permute-done | bytes 294944 | tf_op jit(solution)/shard_map/ppermute | solution.py:562
  278.5 1.5 fusion.2.refs_0_
  280.0 17.9 %gradient.3 = (bf16[5332,256]{1,0:T(8,128)(2,1)}, bf16[5332,256]{1,0:T(8,128)(2,1)}, f32[8,128]{1,0:T(8,128)}) custom-call(s32[3]{0:T(128)} %pad_add_fusion.base_ref, bf16[4,144,256]{2,1,0:T(8,128)(2,1)} %fusion.2.refs_0_, bf16[256,512]{1,0:T(8,128)(2,1)} %copy-done.12, bf16[256,512]{1,0:T(8,128)(2,1)} %copy-done.9, bf16[256,512]{1,0:T(8,128)(2,1)} %copy-done.10, ...), custom_call_target="tpu_custom_call" | custom-call | flops 22020096000 | bytes 11010048 | tf_op jit(solution)/shard_map/gradient/pallas_call | solution.py:400
  297.9 0.1 collective-permute-start.15
  298.1 0.6 slice_reduce_fusion
  298.7 2.8 collective-permute-start.16
  301.5 2.1 collective-permute-start.17
  303.6 0.4 collective-permute-start.18
  303.9 5.6 %join.2 = (bf16[12500,256]{1,0:T(8,128)(2,1)}, f32[8,128]{1,0:T(8,128)}) custom-call(bf16[7168,256]{1,0:T(8,128)(2,1)} %get-tuple-element.61.refs_0_, bf16[7168,256]{1,0:T(8,128)(2,1)} %collective-permute-done.19.refs_1_), custom_call_target="tpu_custom_call" | custom-call | flops 18350080000 | bytes 11010048 | tf_op jit(solution)/shard_map/join/pallas_call | solution.py:427
  309.5 1.2 slice.67
  310.7 0.7 fusion.6.refs_2_
  311.4 0.1 collective-permute-start.20
  311.5 1.2 collective-permute-start.21
  312.7 1.4 collective-permute-start.22
  314.1 1.5 copy-done.15
  315.6 5.0 %join.3 = (bf16[12500,256]{1,0:T(8,128)(2,1)}, f32[8,128]{1,0:T(8,128)}) custom-call(bf16[5332,256]{1,0:T(8,128)(2,1)} %get-tuple-element.59.refs_0_, bf16[5332,256]{1,0:T(8,128)(2,1)} %copy-done.15, bf16[144,256]{1,0:T(8,128)(2,1)} %copy-done.5, bf16[12500,256]{1,0:T(8,128)(2,1)} %get-tuple-element.64.refs_3_), custom_call_target="tpu_custom_call", output_to_operand_aliasing={{0}: (3, {})} | custom-call | flops 13649920000 | bytes 8189952 | tf_op jit(solution)/shard_map/join/pallas_call | solution.py:427
  320.6 1.2 slice.68
  321.8 0.7 add.75
  322.5 0.9 convert_dynamic-update-slice_fusion.3
  323.5 0.8 slice.83
  324.3 0.5 fusion.7
  (57 shorter events, 0.3 us)
Async XLA Ops:
  0.6 128.7 %collective-permute-start = (s32[64,16]{0,1:T(8,128)}, s32[64,16]{0,1:T(8,128)S(1)}, u32[]{:S(2)}, u32[]{:S(2)}) collective-permute-start(s32[64,16]{0,1:T(8,128)} %param.8), channel_id=1, source_target_pairs={{0,16},{8,24},{16,0},{24,8},{1,17},{9,25},{17,1},{25,9},{2,18},{10... | collective-permute-start | bytes 12296 | tf_op jit(solution)/shard_map/ppermute | solution.py:549
  3.6 125.7 %collective-permute-start.1 = (s32[64]{0:T(128)}, s32[64]{0:T(128)S(1)}, u32[]{:S(2)}, u32[]{:S(2)}) collective-permute-start(s32[64]{0:T(128)} %param.7), channel_id=1, source_target_pairs={{0,16},{8,24},{16,0},{24,8},{1,17},{9,25},{17,1},{25,9},{2,18},{10... | collective-permute-start | bytes 776 | tf_op jit(solution)/shard_map/ppermute | solution.py:549
  5.8 123.0 %copy-start.14 = (bf16[1024]{0:T(1024)(128)(2,1)S(1)}, bf16[1024]{0:T(1024)(128)(2,1)}, u32[]{:S(2)}) copy-start(bf16[1024]{0:T(1024)(128)(2,1)} %param.13) | copy-start | bytes 6148
  126.8 27.7 %collective-permute-start.2 = (bf16[4,144,1024]{2,1,0:T(8,128)(2,1)}, bf16[4,144,1024]{2,1,0:T(8,128)(2,1)S(1)}, u32[]{:S(2)}, u32[]{:S(2)}) collective-permute-start(bf16[4,144,1024]{2,1,0:T(8,128)(2,1)} %get-tuple-element.37), channel_id=1, source_target_pairs={{0,1},{1,0},{2,3},{3,2},{4,5},{5,4},{6,7},{7,6},{8,9},{9,8},{10,11... | collective-permute-start | bytes 3538952 | tf_op jit(solution)/shard_map/ppermute | solution.py:562
  129.4 0.5 copy-start.18
  129.4 0.6 copy-start.17
  154.4 1.1 copy-start.4
  158.3 28.0 %collective-permute-start.3 = (bf16[144,1024]{1,0:T(8,128)(2,1)}, bf16[144,1024]{1,0:T(8,128)(2,1)S(1)}, u32[]{:S(2)}, u32[]{:S(2)}) collective-permute-start(bf16[144,1024]{1,0:T(8,128)(2,1)} %get-tuple-element.42), channel_id=1, source_target_pairs={{0,2},{1,3},{2,4},{3,5},{4,6},{5,7},{6,0},{7,1},{8,10},{9,11},{10,... | collective-permute-start | bytes 884744 | tf_op jit(solution)/shard_map/ppermute | solution.py:565
  160.0 26.3 %collective-permute-start.4 = (bf16[144,1024]{1,0:T(8,128)(2,1)}, bf16[144,1024]{1,0:T(8,128)(2,1)S(1)}, u32[]{:S(2)}, u32[]{:S(2)}) collective-permute-start(bf16[144,1024]{1,0:T(8,128)(2,1)} %get-tuple-element.43), channel_id=1, source_target_pairs={{0,4},{1,5},{2,6},{3,7},{4,0},{5,1},{6,2},{7,3},{8,12},{9,13},{10,... | collective-permute-start | bytes 884744 | tf_op jit(solution)/shard_map/ppermute | solution.py:565
  162.6 23.7 %collective-permute-start.5 = (bf16[144,1024]{1,0:T(8,128)(2,1)}, bf16[144,1024]{1,0:T(8,128)(2,1)S(1)}, u32[]{:S(2)}, u32[]{:S(2)}) collective-permute-start(bf16[144,1024]{1,0:T(8,128)(2,1)} %get-tuple-element.44), channel_id=1, source_target_pairs={{0,6},{1,7},{2,0},{3,1},{4,2},{5,3},{6,4},{7,5},{8,14},{9,15},{10,... | collective-permute-start | bytes 884744 | tf_op jit(solution)/shard_map/ppermute | solution.py:565
  186.3 0.7 copy-start.6
  186.3 0.8 copy-start.7
  186.3 0.9 copy-start.8
  192.8 5.2 %collective-permute-start.9 = (bf16[128,512]{1,0:T(8,128)(2,1)}, bf16[128,512]{1,0:T(8,128)(2,1)S(1)}, u32[]{:S(2)}, u32[]{:S(2)}) collective-permute-start(bf16[128,512]{1,0:T(8,128)(2,1)} %get-tuple-element.49), channel_id=1, source_target_pairs={{0,16},{8,24},{16,0},{24,8},{1,17},{9,25},{17,1},{25,9},{2,18},{10... | collective-permute-start | bytes 393224 | tf_op jit(solution)/shard_map/ppermute | solution.py:549
  194.3 30.0 %collective-permute-start.6 = (bf16[2,2,4,144,256]{4,3,2,1,0:T(8,128)(2,1)}, bf16[2,2,4,144,256]{4,3,2,1,0:T(8,128)(2,1)S(1)}, u32[]{:S(2)}, u32[]{:S(2)}) collective-permute-start(bf16[2,2,4,144,256]{4,3,2,1,0:T(8,128)(2,1)} %get-tuple-element.47), channel_id=1, source_target_pairs={{0,8},{8,0},{16,24},{24,16},{1,9},{9,1},{17,25},{25,17},{2,10},{10... | collective-permute-start | bytes 3538952 | tf_op jit(solution)/shard_map/ppermute | solution.py:606
  198.0 3.9 %copy-start.12 = (bf16[256,512]{1,0:T(8,128)(2,1)}, bf16[256,512]{1,0:T(8,128)(2,1)S(1)}, u32[]{:S(2)}) copy-start(bf16[256,512]{1,0:T(8,128)(2,1)S(1)} %constant_dynamic-update-slice_fusion.refs_0_.refs_2_.refs_1_) | copy-start | bytes 786436
  198.0 26.3 %copy-start.2 = (bf16[2,2,4,144,256]{4,3,2,1,0:T(8,128)(2,1)S(1)}, bf16[2,2,4,144,256]{4,3,2,1,0:T(8,128)(2,1)}, u32[]{:S(2)}) copy-start(bf16[2,2,4,144,256]{4,3,2,1,0:T(8,128)(2,1)} %get-tuple-element.46) | copy-start | bytes 3538948
  198.0 22.8 %collective-permute-start.10 = (bf16[256,512]{1,0:T(8,128)(2,1)S(1)}, bf16[256,512]{1,0:T(8,128)(2,1)S(1)}, u32[]{:S(2)}, u32[]{:S(2)}) collective-permute-start(bf16[256,512]{1,0:T(8,128)(2,1)S(1)} %constant_dynamic-update-slice_fusion.refs_0_.refs_2_.refs_1_), channel_id=1, source_target_pairs={{0,2},{1,3},{2,4},{3,5},{4,6},{5,7},{6,0},{7,1},{8,10},{9,11},{10,... | collective-permute-start | bytes 786440 | tf_op jit(solution)/shard_map/ppermute | solution.py:565
  199.4 21.4 %collective-permute-start.11 = (bf16[256,512]{1,0:T(8,128)(2,1)S(1)}, bf16[256,512]{1,0:T(8,128)(2,1)S(1)}, u32[]{:S(2)}, u32[]{:S(2)}) collective-permute-start(bf16[256,512]{1,0:T(8,128)(2,1)S(1)} %constant_dynamic-update-slice_fusion.refs_0_.refs_2_.refs_1_), channel_id=1, source_target_pairs={{0,4},{1,5},{2,6},{3,7},{4,0},{5,1},{6,2},{7,3},{8,12},{9,13},{10,... | collective-permute-start | bytes 786440 | tf_op jit(solution)/shard_map/ppermute | solution.py:565
  200.5 20.2 %collective-permute-start.12 = (bf16[256,512]{1,0:T(8,128)(2,1)S(1)}, bf16[256,512]{1,0:T(8,128)(2,1)S(1)}, u32[]{:S(2)}, u32[]{:S(2)}) collective-permute-start(bf16[256,512]{1,0:T(8,128)(2,1)S(1)} %constant_dynamic-update-slice_fusion.refs_0_.refs_2_.refs_1_), channel_id=1, source_target_pairs={{0,6},{1,7},{2,0},{3,1},{4,2},{5,3},{6,4},{7,5},{8,14},{9,15},{10,... | collective-permute-start | bytes 786440 | tf_op jit(solution)/shard_map/ppermute | solution.py:565
  219.2 27.2 %collective-permute-start.13 = (bf16[256,512]{1,0:T(8,128)(2,1)}, bf16[256,512]{1,0:T(8,128)(2,1)S(1)}, u32[]{:S(2)}, u32[]{:S(2)}) collective-permute-start(bf16[256,512]{1,0:T(8,128)(2,1)} %copy-done.12), channel_id=1, source_target_pairs={{0,1},{1,0},{2,3},{3,2},{4,5},{5,4},{6,7},{7,6},{8,9},{9,8},{10,11... | collective-permute-start | bytes 786440 | tf_op jit(solution)/shard_map/ppermute | solution.py:562
  220.7 0.7 copy-start.9
  220.8 0.8 copy-start.10
  220.8 0.9 copy-start.11
  223.8 19.8 %collective-permute-start.14 = (bf16[3,256,512]{2,1,0:T(8,128)(2,1)}, bf16[3,256,512]{2,1,0:T(8,128)(2,1)S(1)}, u32[]{:S(2)}, u32[]{:S(2)}) collective-permute-start(bf16[3,256,512]{2,1,0:T(8,128)(2,1)} %get-tuple-element.54), channel_id=1, source_target_pairs={{0,1},{1,0},{2,3},{3,2},{4,5},{5,4},{6,7},{7,6},{8,9},{9,8},{10,11... | collective-permute-start | bytes 2359304 | tf_op jit(solution)/shard_map/ppermute | solution.py:562
  224.5 1.6 copy-start
  224.6 19.8 %collective-permute-start.7 = (bf16[2,4,144,256]{3,2,1,0:T(8,128)(2,1)S(1)}, bf16[2,4,144,256]{3,2,1,0:T(8,128)(2,1)S(1)}, u32[]{:S(2)}, u32[]{:S(2)}) collective-permute-start(bf16[2,4,144,256]{3,2,1,0:T(8,128)(2,1)S(1)} %slice_bitcast_fusion), channel_id=1, source_target_pairs={{0,16},{8,24},{16,0},{24,8},{1,17},{9,25},{17,1},{25,9},{2,18},{10... | collective-permute-start | bytes 1769480 | tf_op jit(solution)/shard_map/ppermute | solution.py:549
  246.4 0.7 copy-start.16
  247.1 21.9 %copy-start.1 = (bf16[2,4,144,256]{3,2,1,0:T(8,128)(2,1)S(1)}, bf16[2,4,144,256]{3,2,1,0:T(8,128)(2,1)}, u32[]{:S(2)}) copy-start(bf16[2,4,144,256]{3,2,1,0:T(8,128)(2,1)} %fusion.refs_0_) | copy-start | bytes 1769476
  269.0 34.9 %collective-permute-start.19 = (bf16[7168,256]{1,0:T(8,128)(2,1)}, bf16[7168,256]{1,0:T(8,128)(2,1)}, u32[]{:S(2)}, u32[]{:S(2)}) collective-permute-start(bf16[7168,256]{1,0:T(8,128)(2,1)} %get-tuple-element.62), channel_id=1, source_target_pairs={{0,8},{8,0},{16,24},{24,16},{1,9},{9,1},{17,25},{25,17},{2,10},{10... | collective-permute-start | bytes 11010056 | tf_op jit(solution)/shard_map/ppermute | solution.py:621
  269.1 9.5 %collective-permute-start.8 = (bf16[4,144,256]{2,1,0:T(8,128)(2,1)S(1)}, bf16[4,144,256]{2,1,0:T(8,128)(2,1)S(1)}, u32[]{:S(2)}, u32[]{:S(2)}) collective-permute-start(bf16[4,144,256]{2,1,0:T(8,128)(2,1)S(1)} %slice_bitcast_fusion.2), channel_id=1, source_target_pairs={{0,1},{1,0},{2,3},{3,2},{4,5},{5,4},{6,7},{7,6},{8,9},{9,8},{10,11... | collective-permute-start | bytes 884744 | tf_op jit(solution)/shard_map/ppermute | solution.py:562
  280.0 18.1 %copy-start.13 = (f32[8,128]{1,0:T(8,128)S(1)}, f32[8,128]{1,0:T(8,128)}, u32[]{:S(2)}) copy-start(f32[8,128]{1,0:T(8,128)} %get-tuple-element.45) | copy-start | bytes 12292
  280.0 18.7 %copy-start.3 = (bf16[4,144,256]{2,1,0:T(8,128)(2,1)S(1)}, bf16[4,144,256]{2,1,0:T(8,128)(2,1)}, u32[]{:S(2)}) copy-start(bf16[4,144,256]{2,1,0:T(8,128)(2,1)} %fusion.2.refs_0_) | copy-start | bytes 884740
  297.9 16.1 %collective-permute-start.15 = (bf16[5332,256]{1,0:T(8,128)(2,1)}, bf16[5332,256]{1,0:T(8,128)(2,1)S(1)}, u32[]{:S(2)}, u32[]{:S(2)}) collective-permute-start(bf16[5332,256]{1,0:T(8,128)(2,1)} %get-tuple-element.60), channel_id=1, source_target_pairs={{0,8},{8,0},{16,24},{24,16},{1,9},{9,1},{17,25},{25,17},{2,10},{10... | collective-permute-start | bytes 8189960 | tf_op jit(solution)/shard_map/ppermute | solution.py:621
  298.7 12.0 %collective-permute-start.16 = (bf16[144,256]{1,0:T(8,128)(2,1)S(1)}, bf16[144,256]{1,0:T(8,128)(2,1)S(1)}, u32[]{:S(2)}, u32[]{:S(2)}) collective-permute-start(bf16[144,256]{1,0:T(8,128)(2,1)S(1)} %get-tuple-element.72), channel_id=1, source_target_pairs={{0,2},{1,3},{2,4},{3,5},{4,6},{5,7},{6,0},{7,1},{8,10},{9,11},{10,... | collective-permute-start | bytes 221192 | tf_op jit(solution)/shard_map/ppermute | solution.py:565
  301.5 9.2 %collective-permute-start.17 = (bf16[144,256]{1,0:T(8,128)(2,1)S(1)}, bf16[144,256]{1,0:T(8,128)(2,1)S(1)}, u32[]{:S(2)}, u32[]{:S(2)}) collective-permute-start(bf16[144,256]{1,0:T(8,128)(2,1)S(1)} %get-tuple-element.74), channel_id=1, source_target_pairs={{0,4},{1,5},{2,6},{3,7},{4,0},{5,1},{6,2},{7,3},{8,12},{9,13},{10,... | collective-permute-start | bytes 221192 | tf_op jit(solution)/shard_map/ppermute | solution.py:565
  303.6 7.1 %collective-permute-start.18 = (bf16[144,256]{1,0:T(8,128)(2,1)S(1)}, bf16[144,256]{1,0:T(8,128)(2,1)S(1)}, u32[]{:S(2)}, u32[]{:S(2)}) collective-permute-start(bf16[144,256]{1,0:T(8,128)(2,1)S(1)} %get-tuple-element.73), channel_id=1, source_target_pairs={{0,6},{1,7},{2,0},{3,1},{4,2},{5,3},{6,4},{7,5},{8,14},{9,15},{10,... | collective-permute-start | bytes 221192 | tf_op jit(solution)/shard_map/ppermute | solution.py:565
  311.4 2.7 copy-start.5
  311.4 11.9 %collective-permute-start.20 = (bf16[144,256]{1,0:T(8,128)(2,1)S(1)}, bf16[144,256]{1,0:T(8,128)(2,1)S(1)}, u32[]{:S(2)}, u32[]{:S(2)}) collective-permute-start(bf16[144,256]{1,0:T(8,128)(2,1)S(1)} %fusion.6.refs_2_), channel_id=1, source_target_pairs={{0,8},{8,16},{16,24},{24,0},{1,9},{9,17},{17,25},{25,1},{2,10},{10... | collective-permute-start | bytes 221192 | tf_op jit(solution)/shard_map/ppermute | solution.py:639
  311.5 11.9 %collective-permute-start.21 = (bf16[144,256]{1,0:T(8,128)(2,1)S(1)}, bf16[144,256]{1,0:T(8,128)(2,1)S(1)}, u32[]{:S(2)}, u32[]{:S(2)}) collective-permute-start(bf16[144,256]{1,0:T(8,128)(2,1)S(1)} %fusion.6.refs_2_), channel_id=1, source_target_pairs={{0,16},{8,24},{16,0},{24,8},{1,17},{9,25},{17,1},{25,9},{2,18},{10... | collective-permute-start | bytes 221192 | tf_op jit(solution)/shard_map/ppermute | solution.py:639
  312.7 10.8 %collective-permute-start.22 = (bf16[144,256]{1,0:T(8,128)(2,1)S(1)}, bf16[144,256]{1,0:T(8,128)(2,1)S(1)}, u32[]{:S(2)}, u32[]{:S(2)}) collective-permute-start(bf16[144,256]{1,0:T(8,128)(2,1)S(1)} %fusion.6.refs_2_), channel_id=1, source_target_pairs={{0,24},{8,0},{16,8},{24,16},{1,25},{9,1},{17,9},{25,17},{2,26},{10... | collective-permute-start | bytes 221192 | tf_op jit(solution)/shard_map/ppermute | solution.py:639
  314.1 1.5 copy-start.15

commit v7 on v5

--- a/solution.py
+++ b/solution.py
@@ -275,7 +275,8 @@
 
 
 def join_kernel(*refs):
-    keep_ref, got_ref, out_ref = refs[0], refs[1], refs[-1]
+    keep_ref, got_ref, out_ref, mark_ref = refs[0], refs[1], refs[-2], refs[-1]
+    mark_ref[...] = jnp.zeros_like(mark_ref)
     out_ref[...] = (keep_ref[...].astype(jnp.float32) + got_ref[...].astype(jnp.float32)).astype(jnp.bfloat16)
 
 
@@ -430,8 +431,10 @@
         join_kernel,
         grid=(count,),
         in_specs=specs,
-        out_specs=pl.BlockSpec((width, half), lambda s: (s + first, 0)),
-        out_shape=jax.ShapeDtypeStruct((valid, half), jnp.bfloat16),
+        out_specs=[pl.BlockSpec((width, half), lambda s: (s + first, 0)), whole((8, LANES))],
+        out_shape=[
+            jax.ShapeDtypeStruct((valid, half), jnp.bfloat16), jax.ShapeDtypeStruct((8, LANES), jnp.float32),
+        ],
         input_output_aliases=aliases,
         compiler_params=params(),
         cost_estimate=pl.CostEstimate(flops=height * half, bytes_accessed=6 * height * half, transcendentals=0),
@@ -618,15 +621,21 @@
         )
         return mark[0, 0], keep, lax.ppermute(send, "pts", swap), *out
 
-    late = 2 if cuts[1][1] % 2 == 0 else 1
-    middle = cuts[1][1] - late
     mark, *one = part([second, last_mark], 0, *cuts[0])
     second = add(second[0], across(second[1]), mark)
-    mark, *two = part([second], 1, early, middle)
+    _, *two = part([second], 1, *cuts[1])
+
+    def place(after, part, cut, out):
+        (keep, got), (first, size) = part, cut
+        wide = width * math.gcd(size, first, 2)
+        out, mark = join(after, keep, got, out, wide, first * width // wide, valid)
+        return out, mark[0, 0]
+
+    out, mark = place([], one, cuts[0], None)
     second = add(second[0], *[along(second[by], by) for by in range(1, outer)], mark)
-    _, *three, out = part([second], 1, early + middle, late, one)
+    out, mark = place([second], two, cuts[1], out)
     height = hidden // coord_count
-    joined = jnp.zeros((second.shape[0], hidden), jnp.float32)
+    joined = jnp.zeros((second.shape[0], hidden), jnp.float32) + mark
     for by in range(pts_count):
         block = second if by == 0 else lax.ppermute(second, "pts", [(i, (i + by) % pts_count) for i in range(pts_count)])
         joined = lax.dynamic_update_slice_in_dim(
@@ -637,9 +646,6 @@
     )
     second = joined[:height]
 
-    for (keep, got), first, size in ((two, early, middle), (three, early + middle, late)):
-        wide = width * math.gcd(size, first, 2)
-        out = join([], keep, got, out, wide, first * width // wide, valid)
     return (residual, out.T, second, bias, readout)
 
 

time: 310 us -> 304 us (0.981)
  waiting for transfers between devices: 11 us -> 4.98 us
  Pallas kernels: 249 us -> 245 us
    pallas_call x3 -> x2, Pallas kernels: 47.9 us -> 39.8 us  [gradient(): pl.pallas_call(functools.partial(gradient_kernel, 1 + len(others), places...]
    ppermute x4, waiting for transfers between devices: 8.19 us -> 2.17 us  [across(): return lax.ppermute(a, 'coord', [(i, i ^ 1) for i in range(coord_count)])]
    pallas_call x2, Pallas kernels: 5.71 us -> 10.5 us  [join(): pl.pallas_call(join_kernel, grid=(count,), in_specs=specs, out_specs=[pl....]
    unnamed x43 -> x39, local copies, waits for them, and re-layouts: 8.05 us -> 6.68 us
  transfers between devices with their start and end apart: 24 -> 23, of which waited for: 3 -> 2; matrix products, arithmetic and copies ran while one was open for 4% -> 5% of each run, Pallas kernels for 70% -> 78%
where the time goes in v7:
time: 304 us; the launch traced here: 303 us
  Pallas kernels  245 us (81%)
  starting transfers between devices  29.2 us (10%)
  local copies, waits for them, and re-layouts  15.4 us (5%)
  other arithmetic  6.74 us (2%)
  waiting for transfers between devices  4.98 us (2%)
    pallas_call x1, Pallas kernels, forward(): pl.pallas_call(functools.partial(forward_kernel, valid), grid=(steps,), i...  105 us
    pallas_call x4, Pallas kernels, redraw(): pl.pallas_call(functools.partial(redraw_kernel, first), grid=(count,), in...  79.3 us
    pallas_call x2, Pallas kernels, gradient(): pl.pallas_call(functools.partial(gradient_kernel, 1 + len(others), places...  39.8 us
    ppermute x9, starting transfers between devices, along(): lax.ppermute(a, 'coord', [(i, (i + 2 * by) % coord_count) for i in range(...  14.6 us
    pallas_call x2, Pallas kernels, join(): pl.pallas_call(join_kernel, grid=(count,), in_specs=specs, out_specs=[pl....  10.5 us
    unnamed x39, local copies, waits for them, and re-layouts  6.68 us
    ppermute x4, starting transfers between devices, shift(): lax.ppermute(leaf, 'pts', [(i, (i + 2 * by) % pts_count) for i in range(p...  6.13 us
  transfers between devices with their start and end apart: 23, of which 2 were waited for; matrix products, arithmetic and copies ran while one was open for 5% of the time, Pallas kernels for 78%

profile of v7, /device:TPU:0, one launch (start us, length us, event | category | flops | bytes accessed | tf_op | source)
XLA Modules:
  0.0 302.7 jit_solution(7116440247507386831)
XLA Ops:
  0.6 3.0 collective-permute-start
  3.6 0.1 collective-permute-start.1
  3.7 1.5 broadcast_in_dim.19.coef_ref
  5.2 0.6 pad_add_fusion.base_ref
  5.8 105.5 %forward.1 = (bf16[1024,12544]{1,0:T(8,128)(2,1)}, bf16[4,144,1024]{2,1,0:T(8,128)(2,1)}, bf16[4,144,1024]{2,1,0:T(8,128)(2,1)}) custom-call(s32[3]{0:T(128)} %pad_add_fusion.base_ref, s32[16,64]{1,0:T(8,128)} %bitcast.54, s32[1,64]{1,0:T(1,128)} %bitcast.59, f32[1,12500]{1,0:T(1,128)} %broadcast_in_dim.19.coef_ref, bf16[12500,1024]{1,0:T(8,128)(2,1)} %bitcast.52, ...), custom_call_target="tpu_custom_call" | custom-call | flops 51200000000 | bytes 51200000 | tf_op jit(solution)/shard_map/forward/pallas_call | solution.py:296
  111.3 2.0 collective-permute-start.2
  113.2 0.6 broadcast_in_dim.23
  113.9 0.5 copy-done.18
  114.3 0.1 copy-done.17
  114.4 22.3 %redraw.4 = (bf16[1024,7168]{1,0:T(8,128)(2,1)}, f32[8,128]{1,0:T(8,128)}) custom-call(s32[3]{0:T(128)} %pad_add_fusion.base_ref, s32[16,64]{1,0:T(8,128)} %bitcast.55, s32[1,64]{1,0:T(1,128)} %bitcast.60, bf16[4,144,1024]{2,1,0:T(8,128)(2,1)} %get-tuple-element.36.refs_0_.near_ref), custom_call_target="tpu_custom_call" | custom-call | flops 14680064000 | bytes 7340032 | tf_op jit(solution)/shard_map/redraw/pallas_call | solution.py:335
  136.7 2.2 collective-permute-done.2.got_ref
  138.9 1.1 copy-done.5
  140.0 2.7 combine.1
  142.7 1.8 collective-permute-start.3
  144.5 2.6 collective-permute-start.4
  147.0 1.4 collective-permute-start.5
  148.4 22.3 %redraw.5 = (bf16[1024,7168]{1,0:T(8,128)(2,1)}, f32[8,128]{1,0:T(8,128)}) custom-call(s32[3]{0:T(128)} %pad_add_fusion.base_ref, s32[16,64]{1,0:T(8,128)} %bitcast.56, s32[1,64]{1,0:T(1,128)} %bitcast.61, bf16[144,1024]{1,0:T(8,128)(2,1)} %get-tuple-element.39.refs_0_, bf16[1024,7168]{1,0:T(8,128)(2,1)} %get-tuple-element.40.refs_1_), custom_call_target="tpu_custom_call", output_to_operand_aliasing={{0}: (4, {})} | custom-call | flops 14680064000 | bytes 7340032 | tf_op jit(solution)/shard_map/redraw/pallas_call | solution.py:335
  170.8 0.7 copy-done.7
  171.4 0.1 copy-done.8
  171.6 0.1 copy-done.9
  171.7 5.5 %hidden.1 = (f32[8,128]{1,0:T(8,128)}, bf16[2,2,4,144,256]{4,3,2,1,0:T(8,128)(2,1)}, bf16[2,2,4,144,256]{4,3,2,1,0:T(8,128)(2,1)}, bf16[128,512]{1,0:T(8,128)(2,1)}, bf16[128,512]{1,0:T(8,128)(2,1)}) custom-call(s32[3]{0:T(128)} %pad_add_fusion.base_ref, f32[8,128]{1,0:T(8,128)} %get-tuple-element.41._, bf16[144,1024]{1,0:T(8,128)(2,1)} %get-tuple-element.39.refs_0_, ...), custom_call_target="tpu_custom_call" | custom-call | flops 805306368 | bytes 4194304 | tf_op jit(solution)/shard_map/hidden/pallas_call | solution.py:510
  177.3 1.5 collective-permute-start.9
  178.7 0.9 constant_dynamic-update-slice_fusion.1
  179.7 2.8 collective-permute-done.9
  182.5 0.0 copy-start.3
  182.5 1.3 collective-permute-start.10
  183.8 1.2 collective-permute-start.11
  185.0 1.3 collective-permute-start.12
  186.4 17.3 %redraw.6 = (bf16[1024,5376]{1,0:T(8,128)(2,1)}, f32[8,128]{1,0:T(8,128)}) custom-call(s32[3]{0:T(128)} %pad_add_fusion.base_ref, s32[16,64]{1,0:T(8,128)} %bitcast.57, s32[1,64]{1,0:T(1,128)} %bitcast.62, bf16[256,512]{1,0:T(8,128)(2,1)} %copy-done.13), custom_call_target="tpu_custom_call" | custom-call | flops 11010048000 | bytes 5505024 | tf_op jit(solution)/shard_map/redraw/pallas_call | solution.py:335
  203.7 1.5 collective-permute-start.13
  205.2 0.7 copy-done.10
  205.9 0.1 copy-done.11
  206.0 0.1 copy-done.12
  206.2 2.1 stack.17
  208.2 0.5 collective-permute-start.14
  208.7 0.3 add_convert_fusion.refs_1_
  209.1 1.6 collective-permute-start.7
  210.6 17.3 %redraw.7 = (bf16[1024,5376]{1,0:T(8,128)(2,1)}, f32[8,128]{1,0:T(8,128)}) custom-call(s32[3]{0:T(128)} %pad_add_fusion.base_ref, s32[16,64]{1,0:T(8,128)} %bitcast.58, s32[1,64]{1,0:T(1,128)} %bitcast.63, f32[8,128]{1,0:T(8,128)} %get-tuple-element.51.refs_0_, bf16[2,2,4,144,256]{4,3,2,1,0:T(8,128)(2,1)} %copy-done, ...), custom_call_target="tpu_custom_call", output_to_operand_aliasing={{0}: (5, {})} | custom-call | flops 11010048000 | bytes 5505024 | tf_op jit(solution)/shard_map/redraw/pallas_call | solution.py:335
  228.0 0.9 slice_bitcast_fusion.4
  228.9 1.2 fusion.refs_0_
  230.2 1.6 collective-permute-start.8
  231.7 0.7 copy-done.16
  232.4 21.9 %gradient.2 = (bf16[7168,256]{1,0:T(8,128)(2,1)}, bf16[7168,256]{1,0:T(8,128)(2,1)}, f32[8,128]{1,0:T(8,128)}) custom-call(s32[3]{0:T(128)} %pad_add_fusion.base_ref, bf16[2,4,144,256]{3,2,1,0:T(8,128)(2,1)} %copy-done.2, f32[8,128]{1,0:T(8,128)} %get-tuple-element.53.refs_1_, bf16[256,512]{1,0:T(8,128)(2,1)} %copy-done.13, bf16[256,512]{1,0:T(8,128)(2,1)} %copy-done.10, ...), custom_call_target="tpu_custom_call" | custom-call | flops 29360128000 | bytes 14680064 | tf_op jit(solution)/shard_map/gradient/pallas_call | solution.py:403
  254.3 1.2 slice.62
  255.5 2.4 fusion.2.refs_0_
  258.0 17.9 %gradient.3 = (bf16[5332,256]{1,0:T(8,128)(2,1)}, bf16[5332,256]{1,0:T(8,128)(2,1)}, f32[8,128]{1,0:T(8,128)}) custom-call(s32[3]{0:T(128)} %pad_add_fusion.base_ref, bf16[4,144,256]{2,1,0:T(8,128)(2,1)} %fusion.2.refs_0_, bf16[256,512]{1,0:T(8,128)(2,1)} %copy-done.13, bf16[256,512]{1,0:T(8,128)(2,1)} %copy-done.10, bf16[256,512]{1,0:T(8,128)(2,1)} %copy-done.11, ...), custom_call_target="tpu_custom_call" | custom-call | flops 22020096000 | bytes 11010048 | tf_op jit(solution)/shard_map/gradient/pallas_call | solution.py:403
  275.9 0.5 collective-permute-start.15
  276.4 2.2 collective-permute-start.16
  278.7 1.7 collective-permute-start.17
  280.3 1.1 collective-permute-start.18
  281.4 0.6 slice_reduce_fusion
  282.1 5.6 %join.2 = (bf16[12500,256]{1,0:T(8,128)(2,1)}, f32[8,128]{1,0:T(8,128)}) custom-call(bf16[7168,256]{1,0:T(8,128)(2,1)} %get-tuple-element.61.refs_0_, bf16[7168,256]{1,0:T(8,128)(2,1)} %collective-permute-done.19.refs_1_), custom_call_target="tpu_custom_call" | custom-call | flops 1835008 | bytes 11010048 | tf_op jit(solution)/shard_map/join/pallas_call | solution.py:430
  287.6 1.2 slice.67
  288.8 0.7 fusion.6.refs_2_
  289.5 0.1 collective-permute-start.20
  289.6 0.9 collective-permute-start.21
  290.6 1.4 collective-permute-start.22
  292.0 1.5 copy-done.1
  293.5 5.0 %join.3 = (bf16[12500,256]{1,0:T(8,128)(2,1)}, f32[8,128]{1,0:T(8,128)}) custom-call(bf16[5332,256]{1,0:T(8,128)(2,1)} %get-tuple-element.59.refs_0_, bf16[5332,256]{1,0:T(8,128)(2,1)} %copy-done.1, bf16[144,256]{1,0:T(8,128)(2,1)} %copy-done.6, bf16[12500,256]{1,0:T(8,128)(2,1)} %get-tuple-element.64.refs_3_), custom_call_target="tpu_custom_call", output_to_operand_aliasing={{0}: (3, {})} | custom-call | flops 1364992 | bytes 8189952 | tf_op jit(solution)/shard_map/join/pallas_call | solution.py:430
  298.4 1.2 slice.68
  299.6 0.7 add.75
  300.3 0.9 convert_dynamic-update-slice_fusion.3
  301.4 0.8 slice.83
  302.2 0.5 fusion.7
  (57 shorter events, 0.3 us)
Async XLA Ops:
  0.6 113.2 %collective-permute-start = (s32[64,16]{0,1:T(8,128)}, s32[64,16]{0,1:T(8,128)S(1)}, u32[]{:S(2)}, u32[]{:S(2)}) collective-permute-start(s32[64,16]{0,1:T(8,128)} %param.8), channel_id=1, source_target_pairs={{0,16},{8,24},{16,0},{24,8},{1,17},{9,25},{17,1},{25,9},{2,18},{10... | collective-permute-start | bytes 12296 | tf_op jit(solution)/shard_map/ppermute | solution.py:550
  3.6 110.2 %collective-permute-start.1 = (s32[64]{0:T(128)}, s32[64]{0:T(128)S(1)}, u32[]{:S(2)}, u32[]{:S(2)}) collective-permute-start(s32[64]{0:T(128)} %param.7), channel_id=1, source_target_pairs={{0,16},{8,24},{16,0},{24,8},{1,17},{9,25},{17,1},{25,9},{2,18},{10... | collective-permute-start | bytes 776 | tf_op jit(solution)/shard_map/ppermute | solution.py:550
  5.8 107.5 %copy-start.15 = (bf16[1024]{0:T(1024)(128)(2,1)S(1)}, bf16[1024]{0:T(1024)(128)(2,1)}, u32[]{:S(2)}) copy-start(bf16[1024]{0:T(1024)(128)(2,1)} %param.13) | copy-start | bytes 6148
  111.3 27.6 %collective-permute-start.2 = (bf16[4,144,1024]{2,1,0:T(8,128)(2,1)}, bf16[4,144,1024]{2,1,0:T(8,128)(2,1)S(1)}, u32[]{:S(2)}, u32[]{:S(2)}) collective-permute-start(bf16[4,144,1024]{2,1,0:T(8,128)(2,1)} %get-tuple-element.37), channel_id=1, source_target_pairs={{0,1},{1,0},{2,3},{3,2},{4,5},{5,4},{6,7},{7,6},{8,9},{9,8},{10,11... | collective-permute-start | bytes 3538952 | tf_op jit(solution)/shard_map/ppermute | solution.py:563
  113.8 0.5 copy-start.18
  113.8 0.6 copy-start.17
  138.9 1.1 copy-start.5
  142.7 28.0 %collective-permute-start.3 = (bf16[144,1024]{1,0:T(8,128)(2,1)}, bf16[144,1024]{1,0:T(8,128)(2,1)S(1)}, u32[]{:S(2)}, u32[]{:S(2)}) collective-permute-start(bf16[144,1024]{1,0:T(8,128)(2,1)} %get-tuple-element.42), channel_id=1, source_target_pairs={{0,2},{1,3},{2,4},{3,5},{4,6},{5,7},{6,0},{7,1},{8,10},{9,11},{10,... | collective-permute-start | bytes 884744 | tf_op jit(solution)/shard_map/ppermute | solution.py:566
  144.5 26.3 %collective-permute-start.4 = (bf16[144,1024]{1,0:T(8,128)(2,1)}, bf16[144,1024]{1,0:T(8,128)(2,1)S(1)}, u32[]{:S(2)}, u32[]{:S(2)}) collective-permute-start(bf16[144,1024]{1,0:T(8,128)(2,1)} %get-tuple-element.43), channel_id=1, source_target_pairs={{0,4},{1,5},{2,6},{3,7},{4,0},{5,1},{6,2},{7,3},{8,12},{9,13},{10,... | collective-permute-start | bytes 884744 | tf_op jit(solution)/shard_map/ppermute | solution.py:566
  147.0 23.7 %collective-permute-start.5 = (bf16[144,1024]{1,0:T(8,128)(2,1)}, bf16[144,1024]{1,0:T(8,128)(2,1)S(1)}, u32[]{:S(2)}, u32[]{:S(2)}) collective-permute-start(bf16[144,1024]{1,0:T(8,128)(2,1)} %get-tuple-element.44), channel_id=1, source_target_pairs={{0,6},{1,7},{2,0},{3,1},{4,2},{5,3},{6,4},{7,5},{8,14},{9,15},{10,... | collective-permute-start | bytes 884744 | tf_op jit(solution)/shard_map/ppermute | solution.py:566
  170.7 0.7 copy-start.7
  170.7 0.8 copy-start.8
  170.8 0.9 copy-start.9
  177.3 5.2 %collective-permute-start.9 = (bf16[128,512]{1,0:T(8,128)(2,1)}, bf16[128,512]{1,0:T(8,128)(2,1)S(1)}, u32[]{:S(2)}, u32[]{:S(2)}) collective-permute-start(bf16[128,512]{1,0:T(8,128)(2,1)} %get-tuple-element.49), channel_id=1, source_target_pairs={{0,16},{8,24},{16,0},{24,8},{1,17},{9,25},{17,1},{25,9},{2,18},{10... | collective-permute-start | bytes 393224 | tf_op jit(solution)/shard_map/ppermute | solution.py:550
  178.7 30.0 %collective-permute-start.6 = (bf16[2,2,4,144,256]{4,3,2,1,0:T(8,128)(2,1)}, bf16[2,2,4,144,256]{4,3,2,1,0:T(8,128)(2,1)S(1)}, u32[]{:S(2)}, u32[]{:S(2)}) collective-permute-start(bf16[2,2,4,144,256]{4,3,2,1,0:T(8,128)(2,1)} %get-tuple-element.47), channel_id=1, source_target_pairs={{0,8},{8,0},{16,24},{24,16},{1,9},{9,1},{17,25},{25,17},{2,10},{10... | collective-permute-start | bytes 3538952 | tf_op jit(solution)/shard_map/ppermute | solution.py:607
  182.4 3.9 %copy-start.13 = (bf16[256,512]{1,0:T(8,128)(2,1)}, bf16[256,512]{1,0:T(8,128)(2,1)S(1)}, u32[]{:S(2)}) copy-start(bf16[256,512]{1,0:T(8,128)(2,1)S(1)} %constant_dynamic-update-slice_fusion.refs_0_.refs_2_.refs_1_) | copy-start | bytes 786436
  182.5 26.3 %copy-start.3 = (bf16[2,2,4,144,256]{4,3,2,1,0:T(8,128)(2,1)S(1)}, bf16[2,2,4,144,256]{4,3,2,1,0:T(8,128)(2,1)}, u32[]{:S(2)}) copy-start(bf16[2,2,4,144,256]{4,3,2,1,0:T(8,128)(2,1)} %get-tuple-element.46) | copy-start | bytes 3538948
  182.5 22.7 %collective-permute-start.10 = (bf16[256,512]{1,0:T(8,128)(2,1)S(1)}, bf16[256,512]{1,0:T(8,128)(2,1)S(1)}, u32[]{:S(2)}, u32[]{:S(2)}) collective-permute-start(bf16[256,512]{1,0:T(8,128)(2,1)S(1)} %constant_dynamic-update-slice_fusion.refs_0_.refs_2_.refs_1_), channel_id=1, source_target_pairs={{0,2},{1,3},{2,4},{3,5},{4,6},{5,7},{6,0},{7,1},{8,10},{9,11},{10,... | collective-permute-start | bytes 786440 | tf_op jit(solution)/shard_map/ppermute | solution.py:566
  183.8 21.4 %collective-permute-start.11 = (bf16[256,512]{1,0:T(8,128)(2,1)S(1)}, bf16[256,512]{1,0:T(8,128)(2,1)S(1)}, u32[]{:S(2)}, u32[]{:S(2)}) collective-permute-start(bf16[256,512]{1,0:T(8,128)(2,1)S(1)} %constant_dynamic-update-slice_fusion.refs_0_.refs_2_.refs_1_), channel_id=1, source_target_pairs={{0,4},{1,5},{2,6},{3,7},{4,0},{5,1},{6,2},{7,3},{8,12},{9,13},{10,... | collective-permute-start | bytes 786440 | tf_op jit(solution)/shard_map/ppermute | solution.py:566
  185.0 20.2 %collective-permute-start.12 = (bf16[256,512]{1,0:T(8,128)(2,1)S(1)}, bf16[256,512]{1,0:T(8,128)(2,1)S(1)}, u32[]{:S(2)}, u32[]{:S(2)}) collective-permute-start(bf16[256,512]{1,0:T(8,128)(2,1)S(1)} %constant_dynamic-update-slice_fusion.refs_0_.refs_2_.refs_1_), channel_id=1, source_target_pairs={{0,6},{1,7},{2,0},{3,1},{4,2},{5,3},{6,4},{7,5},{8,14},{9,15},{10,... | collective-permute-start | bytes 786440 | tf_op jit(solution)/shard_map/ppermute | solution.py:566
  203.7 28.0 %collective-permute-start.13 = (bf16[256,512]{1,0:T(8,128)(2,1)}, bf16[256,512]{1,0:T(8,128)(2,1)S(1)}, u32[]{:S(2)}, u32[]{:S(2)}) collective-permute-start(bf16[256,512]{1,0:T(8,128)(2,1)} %copy-done.13), channel_id=1, source_target_pairs={{0,1},{1,0},{2,3},{3,2},{4,5},{5,4},{6,7},{7,6},{8,9},{9,8},{10,11... | collective-permute-start | bytes 786440 | tf_op jit(solution)/shard_map/ppermute | solution.py:563
  205.2 0.7 copy-start.10
  205.2 0.8 copy-start.11
  205.2 0.9 copy-start.12
  208.2 19.8 %collective-permute-start.14 = (bf16[3,256,512]{2,1,0:T(8,128)(2,1)}, bf16[3,256,512]{2,1,0:T(8,128)(2,1)S(1)}, u32[]{:S(2)}, u32[]{:S(2)}) collective-permute-start(bf16[3,256,512]{2,1,0:T(8,128)(2,1)} %get-tuple-element.54), channel_id=1, source_target_pairs={{0,1},{1,0},{2,3},{3,2},{4,5},{5,4},{6,7},{7,6},{8,9},{9,8},{10,11... | collective-permute-start | bytes 2359304 | tf_op jit(solution)/shard_map/ppermute | solution.py:563
  209.0 1.6 copy-start
  209.1 19.8 %collective-permute-start.7 = (bf16[2,4,144,256]{3,2,1,0:T(8,128)(2,1)S(1)}, bf16[2,4,144,256]{3,2,1,0:T(8,128)(2,1)S(1)}, u32[]{:S(2)}, u32[]{:S(2)}) collective-permute-start(bf16[2,4,144,256]{3,2,1,0:T(8,128)(2,1)S(1)} %slice_bitcast_fusion), channel_id=1, source_target_pairs={{0,16},{8,24},{16,0},{24,8},{1,17},{9,25},{17,1},{25,9},{2,18},{10... | collective-permute-start | bytes 1769480 | tf_op jit(solution)/shard_map/ppermute | solution.py:550
  230.1 1.6 copy-start.2
  230.2 25.4 %collective-permute-start.8 = (bf16[4,144,256]{2,1,0:T(8,128)(2,1)S(1)}, bf16[4,144,256]{2,1,0:T(8,128)(2,1)S(1)}, u32[]{:S(2)}, u32[]{:S(2)}) collective-permute-start(bf16[4,144,256]{2,1,0:T(8,128)(2,1)S(1)} %slice_bitcast_fusion.2), channel_id=1, source_target_pairs={{0,1},{1,0},{2,3},{3,2},{4,5},{5,4},{6,7},{7,6},{8,9},{9,8},{10,11... | collective-permute-start | bytes 884744 | tf_op jit(solution)/shard_map/ppermute | solution.py:563
  231.7 0.7 copy-start.16
  254.3 27.7 %collective-permute-start.19 = (bf16[7168,256]{1,0:T(8,128)(2,1)}, bf16[7168,256]{1,0:T(8,128)(2,1)}, u32[]{:S(2)}, u32[]{:S(2)}) collective-permute-start(bf16[7168,256]{1,0:T(8,128)(2,1)} %get-tuple-element.62), channel_id=1, source_target_pairs={{0,8},{8,0},{16,24},{24,16},{1,9},{9,1},{17,25},{25,17},{2,10},{10... | collective-permute-start | bytes 11010056 | tf_op jit(solution)/shard_map/ppermute | solution.py:622
  257.9 18.5 %copy-start.4 = (bf16[4,144,256]{2,1,0:T(8,128)(2,1)S(1)}, bf16[4,144,256]{2,1,0:T(8,128)(2,1)}, u32[]{:S(2)}) copy-start(bf16[4,144,256]{2,1,0:T(8,128)(2,1)} %fusion.2.refs_0_) | copy-start | bytes 884740
  258.0 23.5 %copy-start.14 = (f32[8,128]{1,0:T(8,128)S(1)}, f32[8,128]{1,0:T(8,128)}, u32[]{:S(2)}) copy-start(f32[8,128]{1,0:T(8,128)} %get-tuple-element.45) | copy-start | bytes 12292
  275.9 16.1 %collective-permute-start.15 = (bf16[5332,256]{1,0:T(8,128)(2,1)}, bf16[5332,256]{1,0:T(8,128)(2,1)S(1)}, u32[]{:S(2)}, u32[]{:S(2)}) collective-permute-start(bf16[5332,256]{1,0:T(8,128)(2,1)} %get-tuple-element.60), channel_id=1, source_target_pairs={{0,8},{8,0},{16,24},{24,16},{1,9},{9,1},{17,25},{25,17},{2,10},{10... | collective-permute-start | bytes 8189960 | tf_op jit(solution)/shard_map/ppermute | solution.py:622
  276.4 12.4 %collective-permute-start.16 = (bf16[144,256]{1,0:T(8,128)(2,1)S(1)}, bf16[144,256]{1,0:T(8,128)(2,1)S(1)}, u32[]{:S(2)}, u32[]{:S(2)}) collective-permute-start(bf16[144,256]{1,0:T(8,128)(2,1)S(1)} %get-tuple-element.72), channel_id=1, source_target_pairs={{0,2},{1,3},{2,4},{3,5},{4,6},{5,7},{6,0},{7,1},{8,10},{9,11},{10,... | collective-permute-start | bytes 221192 | tf_op jit(solution)/shard_map/ppermute | solution.py:566
  278.7 10.1 %collective-permute-start.17 = (bf16[144,256]{1,0:T(8,128)(2,1)S(1)}, bf16[144,256]{1,0:T(8,128)(2,1)S(1)}, u32[]{:S(2)}, u32[]{:S(2)}) collective-permute-start(bf16[144,256]{1,0:T(8,128)(2,1)S(1)} %get-tuple-element.74), channel_id=1, source_target_pairs={{0,4},{1,5},{2,6},{3,7},{4,0},{5,1},{6,2},{7,3},{8,12},{9,13},{10,... | collective-permute-start | bytes 221192 | tf_op jit(solution)/shard_map/ppermute | solution.py:566
  280.3 8.5 %collective-permute-start.18 = (bf16[144,256]{1,0:T(8,128)(2,1)S(1)}, bf16[144,256]{1,0:T(8,128)(2,1)S(1)}, u32[]{:S(2)}, u32[]{:S(2)}) collective-permute-start(bf16[144,256]{1,0:T(8,128)(2,1)S(1)} %get-tuple-element.73), channel_id=1, source_target_pairs={{0,6},{1,7},{2,0},{3,1},{4,2},{5,3},{6,4},{7,5},{8,14},{9,15},{10,... | collective-permute-start | bytes 221192 | tf_op jit(solution)/shard_map/ppermute | solution.py:566
  289.5 2.4 copy-start.6
  289.5 11.7 %collective-permute-start.20 = (bf16[144,256]{1,0:T(8,128)(2,1)S(1)}, bf16[144,256]{1,0:T(8,128)(2,1)S(1)}, u32[]{:S(2)}, u32[]{:S(2)}) collective-permute-start(bf16[144,256]{1,0:T(8,128)(2,1)S(1)} %fusion.6.refs_2_), channel_id=1, source_target_pairs={{0,8},{8,16},{16,24},{24,0},{1,9},{9,17},{17,25},{25,1},{2,10},{10... | collective-permute-start | bytes 221192 | tf_op jit(solution)/shard_map/ppermute | solution.py:640
  289.6 11.7 %collective-permute-start.21 = (bf16[144,256]{1,0:T(8,128)(2,1)S(1)}, bf16[144,256]{1,0:T(8,128)(2,1)S(1)}, u32[]{:S(2)}, u32[]{:S(2)}) collective-permute-start(bf16[144,256]{1,0:T(8,128)(2,1)S(1)} %fusion.6.refs_2_), channel_id=1, source_target_pairs={{0,16},{8,24},{16,0},{24,8},{1,17},{9,25},{17,1},{25,9},{2,18},{10... | collective-permute-start | bytes 221192 | tf_op jit(solution)/shard_map/ppermute | solution.py:640
  290.6 10.8 %collective-permute-start.22 = (bf16[144,256]{1,0:T(8,128)(2,1)S(1)}, bf16[144,256]{1,0:T(8,128)(2,1)S(1)}, u32[]{:S(2)}, u32[]{:S(2)}) collective-permute-start(bf16[144,256]{1,0:T(8,128)(2,1)S(1)} %fusion.6.refs_2_), channel_id=1, source_target_pairs={{0,24},{8,0},{16,8},{24,16},{1,25},{9,1},{17,9},{25,17},{2,26},{10... | collective-permute-start | bytes 221192 | tf_op jit(solution)/shard_map/ppermute | solution.py:640
  292.0 1.5 copy-start.1
